TPU v7x, 512 devices: a whole 4x8x8 slice. The times are simulated.
512 devices in a mesh: member: 4 (over x_lo, core), region: 128 (over z, y, x_hi).
Axes of the slice: x: 4 (x_hi: 2, x_lo: 2; x = x_hi * 2 + x_lo), y: 8, z: 8, core: 2. Of those that a mesh axis runs over, the one named last changes fastest.
Arguments:
- prior_tracer_ensemble: float32 [80, 1024, 2048], P('member', 'region'), may hold values from -6 to 6
- diffusion_numbers: float32 [1024, 2048], P('region'), may hold values from 0.02 to 0.24
- measured_site_index: int32 [4, 2048], P(None, 'region'), may hold values from 0 to 16383
- measured_readings: float32 [4, 2048], P(None, 'region'), may hold values from -6 to 6
- measurement_error_spread: float32 [4, 2048], P(None, 'region'), may hold values from 0.1 to 1
- measured_slot_tally: int32 [4, 128], replicated, may hold values from 1 to 16, 1024 in all within a row
Outputs:
- analysis: float32 [80, 1024, 2048], P(None, 'region', 'member')
Inputs may be any that keep to these rules, and one draw needn't show every extreme that they name: `measured_slot_tally`: the live slots of a region are its first ones; the counts of each batch sum to 8 times the number of regions and reach 16 in some region.
All inputs are finite; a program needn't handle non-finite values.
Results may differ from a plain program's by a relative error of at most 0.0003.
Values sent between devices are 32-bit elements; how exact they have to be, the bound alone decides.
No kernel may reach another device: no remote copies, remote signals or barrier semaphores. Data moves between devices by JAX's collectives and lax.ppermute only.
A program may use at most 64 MiB of HBM per device.

v0:
```python
import jax
import jax.numpy as jnp
from jax import lax
from jax.sharding import PartitionSpec as P

REACH = 2
RADIUS = 16


epsilon = 1e-05
highest = lax.Precision.HIGHEST


def padded(cells, sides, width):
    for axis, dim in sides:
        count = lax.axis_size(axis)
        ends = count - 1
        head = lax.slice_in_dim(cells, 0, width, axis=dim)
        tail = lax.slice_in_dim(cells, cells.shape[dim] - width, cells.shape[dim], axis=dim)
        cells = jnp.concatenate(
            [
                lax.ppermute(tail, axis, [(i, (i + 1) % count) for i in range(ends)]),
                cells,
                lax.ppermute(head, axis, [((i + 1) % count, i) for i in range(ends)]),
            ],
            axis=dim,
        )
    return cells


def from_behind(value, axis, steps):
    count = lax.axis_size(axis)
    initial, last = (max(0, -steps), min(count, count - steps))
    return lax.ppermute(value, axis, [(source, source + steps) for source in range(initial, last)])


def increments(obs_prior, measured_readings, measurement_error_spread, live_slots):
    members = obs_prior.shape[1]
    average = jnp.mean(obs_prior, axis=1, keepdims=True)
    anomaly = obs_prior - average
    spread = jnp.sum(anomaly * anomaly, axis=1, keepdims=True) / (members - 1) + epsilon
    obs_noise = jnp.where(live_slots > 0.5, measurement_error_spread, 1.0)[:, None]
    posterior = 1.0 / (1.0 / spread + 1.0 / obs_noise)
    post_mean = posterior * (average / spread + measured_readings[:, None] / obs_noise)
    increment = post_mean - average + (jnp.sqrt(posterior / spread) - 1.0) * anomaly
    return (anomaly, spread[:, 0], increment)


def taper_weights(cell_rows, cell_cols, obs_rows, obs_cols, vertical_sums, radius):
    row_gap = cell_rows[:, None] - obs_rows[None, :]
    col_gap = jnp.abs(cell_cols[:, None] - obs_cols[None, :])
    col_gap = jnp.minimum(col_gap, vertical_sums - col_gap)
    scaled_gap = (row_gap * row_gap + col_gap * col_gap) / float(radius * radius)
    remain = jnp.maximum(1.0 - scaled_gap, 0.0)
    return remain * remain


def regress(region_block, anomaly, spread, increment, weights):
    members = region_block.shape[0]
    average = jnp.mean(region_block, axis=0, keepdims=True)
    state_anomaly = region_block - average
    covariance = jnp.einsum("ec,je->cj", state_anomaly, anomaly, precision=highest) / (members - 1)
    regression = weights * covariance / spread[None, :]
    return region_block + jnp.einsum("cj,je->ec", regression, increment, precision=highest)


def local(
    prior_tracer_ensemble,
    diffusion_numbers,
    measured_site_index,
    measured_readings,
    measurement_error_spread,
    measured_slot_tally,
):
    haloed_tracer = padded(prior_tracer_ensemble, (("region", 1),), 1)
    lower_boundary_lines = haloed_tracer[:, :-2, :]
    upper_boundary_lines = haloed_tracer[:, 2:, :]
    eastern_strips = jnp.roll(prior_tracer_ensemble, -1, axis=2)
    western_strips = jnp.roll(prior_tracer_ensemble, 1, axis=2)
    diffused_tracer = prior_tracer_ensemble + diffusion_numbers[None] * (
        upper_boundary_lines
        + lower_boundary_lines
        + eastern_strips
        + western_strips
        - 4.0 * prior_tracer_ensemble
    )
    ensemble_tracers = lax.all_to_all(
        diffused_tracer, "member", split_axis=2, concat_axis=0, tiled=True
    )
    members, row_count, quarter = ensemble_tracers.shape
    vertical_sums = prior_tracer_ensemble.shape[2]
    capacity = measured_site_index.shape[1]
    blocks = 2 * REACH + 1
    region_id = lax.axis_index("region")
    quarter_id = lax.axis_index("member")
    state_flat = ensemble_tracers.reshape(members, row_count * quarter)
    cell_index = jnp.arange(row_count * quarter, dtype=jnp.int32)
    cell_rows = (region_id * row_count + cell_index // quarter).astype(jnp.float32)
    cell_cols = (quarter_id * quarter + cell_index % quarter).astype(jnp.float32)
    slot_index = jnp.arange(capacity, dtype=jnp.int32)
    window_regions = region_id - REACH + jnp.arange(blocks, dtype=jnp.int32)
    edge_zeros = jnp.zeros((REACH,), jnp.int32)
    for batch_index in range(measured_site_index.shape[0]):
        obs_cells = measured_site_index[batch_index]
        local_rows = obs_cells // vertical_sums
        obs_cols = obs_cells % vertical_sums
        owned_slots = obs_cols // quarter == quarter_id
        position = jnp.where(owned_slots, local_rows * quarter + obs_cols - quarter_id * quarter, 0)
        owned_prior = jnp.where(owned_slots[None, :], jnp.take(state_flat, position, axis=1), 0.0)
        obs_prior = lax.psum(owned_prior.T, "member")
        obs_facts = jnp.stack(
            [
                measured_readings[batch_index],
                measurement_error_spread[batch_index],
                obs_cells.astype(jnp.float32),
            ]
        )
        arrivals = {0: (obs_prior, obs_facts)}
        for offset in range(-REACH, REACH + 1):
            if offset != 0:
                arrivals[offset] = from_behind((obs_prior, obs_facts), "region", -offset)
        near_priors = jnp.concatenate(
            [arrivals[offset][0] for offset in range(-REACH, REACH + 1)], axis=0
        )
        near_facts = jnp.concatenate(
            [arrivals[offset][1] for offset in range(-REACH, REACH + 1)], axis=1
        )
        padded_counts = jnp.concatenate([edge_zeros, measured_slot_tally[batch_index], edge_zeros])
        near_counts = lax.dynamic_slice_in_dim(padded_counts, region_id, blocks, 0)
        live_slots = (slot_index[None, :] < near_counts[:, None]).reshape(-1).astype(jnp.float32)
        near_cells = near_facts[2].astype(jnp.int32)
        near_rows = (
            (
                window_regions[:, None] * row_count
                + (near_cells // vertical_sums).reshape(blocks, capacity)
            )
            .reshape(-1)
            .astype(jnp.float32)
        )
        near_cols = (near_cells % vertical_sums).astype(jnp.float32)
        anomaly, spread, increment = increments(
            near_priors, near_facts[0], near_facts[1], live_slots
        )
        weights = (
            taper_weights(cell_rows, cell_cols, near_rows, near_cols, vertical_sums, RADIUS)
            * live_slots[None, :]
        )
        state_flat = regress(state_flat, anomaly, spread, increment, weights)
    return state_flat.reshape(members, row_count, quarter)


def solution(mesh):
    placed = (
        P("member", "region", None),
        P("region", None),
        P(None, "region"),
        P(None, "region"),
        P(None, "region"),
        P(),
    )
    return jax.shard_map(
        local, mesh=mesh, in_specs=placed, out_specs=P(None, "region", "member"), check_vma=False
    )
```

profile of v0, /device:TPU:248, one launch (start us, length us, event | category | flops | bytes accessed | tf_op | source)
XLA Modules:
  0.0 296.1 jit_solution(5072061764705304081)
XLA Ops:
  2.3 4.7 %collective-permute-start.6 = (f32[3,16]{1,0:T(4,128)S(1)}, f32[3,16]{1,0:T(4,128)}, u32[]{:S(2)}, u32[]{:S(2)}) collective-permute-start(f32[3,16]{1,0:T(4,128)S(1)} %pad_maximum_fusion.2), channel_id=1, source_target_pairs={{0,2},{1,3},{2,4},{3,5},{4,6},{5,7},{6,8},{7,9},{8,10},{9,11},{10,... | collective-permute-start | bytes 584 | tf_op jit(solution)/shard_map/ppermute | solution.py:34
  7.0 4.9 %collective-permute-start.7 = (f32[3,16]{1,0:T(4,128)S(1)}, f32[3,16]{1,0:T(4,128)}, u32[]{:S(2)}, u32[]{:S(2)}) collective-permute-start(f32[3,16]{1,0:T(4,128)S(1)} %pad_maximum_fusion.2), channel_id=1, source_target_pairs={{0,1},{1,2},{2,3},{3,4},{4,5},{5,6},{6,7},{7,8},{8,9},{9,10},{10,1... | collective-permute-start | bytes 584 | tf_op jit(solution)/shard_map/ppermute | solution.py:34
  17.3 4.0 %collective-permute-start.1 = (f32[20,1,2048]{2,0,1:T(8,128)S(1)}, f32[20,1,2048]{2,0,1:T(8,128)S(1)}, u32[]{:S(2)}, u32[]{:S(2)}) collective-permute-start(f32[20,1,2048]{2,0,1:T(8,128)S(1)} %copy.77), channel_id=1, source_target_pairs={{0,1},{1,2},{2,3},{3,4},{4,5},{5,6},{6,7},{7,8},{8,9},{9,10},{10,1... | collective-permute-start | bytes 491528 | tf_op jit(solution)/shard_map/ppermute | solution.py:22
  21.4 4.2 %collective-permute-start = (f32[20,1,2048]{2,0,1:T(8,128)S(1)}, f32[20,1,2048]{2,0,1:T(8,128)}, u32[]{:S(2)}, u32[]{:S(2)}) collective-permute-start(f32[20,1,2048]{2,0,1:T(8,128)S(1)} %copy.76), channel_id=1, source_target_pairs={{1,0},{2,1},{3,2},{4,3},{5,4},{6,5},{7,6},{8,7},{9,8},{10,9},{11,1... | collective-permute-start | bytes 491528 | tf_op jit(solution)/shard_map/ppermute | solution.py:24
  33.9 10.1 %collective-permute-start.30 = (f32[3,16]{1,0:T(4,128)S(1)}, f32[3,16]{1,0:T(4,128)S(1)}, u32[]{:S(2)}, u32[]{:S(2)}) collective-permute-start(f32[3,16]{1,0:T(4,128)S(1)} %pad_maximum_fusion.5), channel_id=1, source_target_pairs={{0,2},{1,3},{2,4},{3,5},{4,6},{5,7},{6,8},{7,9},{8,10},{9,11},{10,... | collective-permute-start | bytes 584 | tf_op jit(solution)/shard_map/ppermute | solution.py:34
  46.5 5.8 %collective-permute-start.32 = (f32[3,16]{1,0:T(4,128)S(1)}, f32[3,16]{1,0:T(4,128)}, u32[]{:S(2)}, u32[]{:S(2)}) collective-permute-start(f32[3,16]{1,0:T(4,128)S(1)} %pad_maximum_fusion.5), channel_id=1, source_target_pairs={{1,0},{2,1},{3,2},{4,3},{5,4},{6,5},{7,6},{8,7},{9,8},{10,9},{11,1... | collective-permute-start | bytes 584 | tf_op jit(solution)/shard_map/ppermute | solution.py:34
  55.0 7.2 %collective-permute-start.22 = (f32[3,16]{1,0:T(4,128)S(1)}, f32[3,16]{1,0:T(4,128)S(1)}, u32[]{:S(2)}, u32[]{:S(2)}) collective-permute-start(f32[3,16]{1,0:T(4,128)S(1)} %pad_maximum_fusion.4), channel_id=1, source_target_pairs={{0,2},{1,3},{2,4},{3,5},{4,6},{5,7},{6,8},{7,9},{8,10},{9,11},{10,... | collective-permute-start | bytes 584 | tf_op jit(solution)/shard_map/ppermute | solution.py:34
  65.3 5.8 %collective-permute-start.24 = (f32[3,16]{1,0:T(4,128)S(1)}, f32[3,16]{1,0:T(4,128)}, u32[]{:S(2)}, u32[]{:S(2)}) collective-permute-start(f32[3,16]{1,0:T(4,128)S(1)} %pad_maximum_fusion.4), channel_id=1, source_target_pairs={{1,0},{2,1},{3,2},{4,3},{5,4},{6,5},{7,6},{8,7},{9,8},{10,9},{11,1... | collective-permute-start | bytes 584 | tf_op jit(solution)/shard_map/ppermute | solution.py:34
  73.8 7.2 %collective-permute-start.14 = (f32[3,16]{1,0:T(4,128)S(1)}, f32[3,16]{1,0:T(4,128)S(1)}, u32[]{:S(2)}, u32[]{:S(2)}) collective-permute-start(f32[3,16]{1,0:T(4,128)S(1)} %pad_maximum_fusion.3), channel_id=1, source_target_pairs={{0,2},{1,3},{2,4},{3,5},{4,6},{5,7},{6,8},{7,9},{8,10},{9,11},{10,... | collective-permute-start | bytes 584 | tf_op jit(solution)/shard_map/ppermute | solution.py:34
  83.5 5.8 %collective-permute-start.16 = (f32[3,16]{1,0:T(4,128)S(1)}, f32[3,16]{1,0:T(4,128)}, u32[]{:S(2)}, u32[]{:S(2)}) collective-permute-start(f32[3,16]{1,0:T(4,128)S(1)} %pad_maximum_fusion.3), channel_id=1, source_target_pairs={{1,0},{2,1},{3,2},{4,3},{5,4},{6,5},{7,6},{8,7},{9,8},{10,9},{11,1... | collective-permute-start | bytes 584 | tf_op jit(solution)/shard_map/ppermute | solution.py:34
  92.0 6.2 %collective-permute-done.17 = f32[3,16]{1,0:T(4,128)} collective-permute-done((f32[3,16]{1,0:T(4,128)S(1)}, f32[3,16]{1,0:T(4,128)}, u32[]{:S(2)}, u32[]{:S(2)}) %collective-permute-start.17) | collective-permute-done | bytes 224 | tf_op jit(solution)/shard_map/ppermute | solution.py:34
  103.6 6.2 %copy.70 = f32[20,8,2048]{0,1,2:T(8,128)} copy(f32[20,8,2048]{2,1,0:T(8,128)} %fusion.41) | data formatting | bytes 2621440 | tf_op jit(solution)/shard_map/add | solution.py:80
  109.8 11.2 %reshape.509 = f32[4,1,81920]{2,1,0:T(1,128)} reshape(f32[2048,8,20]{2,1,0:T(8,128)} %bitcast.181) | data formatting | bytes 2621440
  127.2 14.7 %all-to-all-done = f32[4,1,81920]{2,1,0:T(1,128)S(1)} async-done(((f32[4,1,81920]{2,1,0:T(1,128)}), f32[4,1,81920]{2,1,0:T(1,128)S(1)}, u32[]{:S(2)}, u32[]{:S(2)}) %all-to-all-start) | async-done | bytes 1310752 | tf_op jit(solution)/shard_map/all_to_all | solution.py:87
  142.4 4.4 %reduce.1 = f32[4,81920]{1,0:T(4,128)S(1)} reduce(f32[4,1,81920]{2,1,0:T(1,128)S(1)} %all-to-all-done, f32[]{:T(128)} %broadcast.1061), dimensions={1}, to_apply=%all_to_all.11.reduce_sub_computation | reduce | bytes 2621444 | tf_op jit(solution)/shard_map/all_to_all | solution.py:87
  146.8 13.0 %reshape.510 = f32[2048,8,20]{2,1,0:T(8,128)} reshape(f32[4,81920]{1,0:T(4,128)S(1)} %reduce.1) | data formatting | bytes 2621440
  159.9 5.6 %copy.71 = f32[20,8,4,512]{3,1,0,2:T(8,128)S(1)} copy(f32[20,8,4,512]{0,1,3,2:T(8,128)} %bitcast.182) | data formatting | bytes 2621440 | tf_op jit(solution)/shard_map/all_to_all | solution.py:87
  170.3 5.8 %psum.28 = f32[16,80]{1,0:T(8,128)S(1)} all-reduce(f32[16,80]{1,0:T(8,128)S(1)} %fusion.96), channel_id=1, replica_groups=mesh['member'=4,'region'=128] {'member'}, use_global_device_ids=true, to_apply=%region_0.2 | all-reduce | flops 1280 | bytes 10240 | tf_op jit(solution)/shard_map/psum | solution.py:110
  176.1 3.9 %collective-permute-start.2 = (f32[16,80]{1,0:T(8,128)S(1)}, f32[16,80]{1,0:T(8,128)S(1)}, u32[]{:S(2)}, u32[]{:S(2)}) collective-permute-start(f32[16,80]{1,0:T(8,128)S(1)} %psum.28), channel_id=1, source_target_pairs={{0,2},{1,3},{2,4},{3,5},{4,6},{5,7},{6,8},{7,9},{8,10},{9,11},{10,... | collective-permute-start | bytes 15368 | tf_op jit(solution)/shard_map/ppermute | solution.py:34
  182.0 6.3 %collective-permute-start.4 = (f32[16,80]{1,0:T(8,128)S(1)}, f32[16,80]{1,0:T(8,128)S(1)}, u32[]{:S(2)}, u32[]{:S(2)}) collective-permute-start(f32[16,80]{1,0:T(8,128)S(1)} %psum.28), channel_id=1, source_target_pairs={{1,0},{2,1},{3,2},{4,3},{5,4},{6,5},{7,6},{8,7},{9,8},{10,9},{11,1... | collective-permute-start | bytes 15368 | tf_op jit(solution)/shard_map/ppermute | solution.py:34
  190.7 6.5 %collective-permute-done.5 = f32[16,80]{1,0:T(8,128)S(1)} collective-permute-done((f32[16,80]{1,0:T(8,128)S(1)}, f32[16,80]{1,0:T(8,128)S(1)}, u32[]{:S(2)}, u32[]{:S(2)}) %collective-permute-start.5) | collective-permute-done | bytes 5152 | tf_op jit(solution)/shard_map/ppermute | solution.py:34
  202.4 5.7 %psum.29 = f32[16,80]{1,0:T(8,128)S(1)} all-reduce(f32[16,80]{1,0:T(8,128)S(1)} %fusion.95), channel_id=1, replica_groups=mesh['member'=4,'region'=128] {'member'}, use_global_device_ids=true, to_apply=%region_4.6 | all-reduce | flops 1280 | bytes 10240 | tf_op jit(solution)/shard_map/psum | solution.py:110
  212.0 6.3 %collective-permute-start.12 = (f32[16,80]{1,0:T(8,128)S(1)}, f32[16,80]{1,0:T(8,128)S(1)}, u32[]{:S(2)}, u32[]{:S(2)}) collective-permute-start(f32[16,80]{1,0:T(8,128)S(1)} %psum.29), channel_id=1, source_target_pairs={{1,0},{2,1},{3,2},{4,3},{5,4},{6,5},{7,6},{8,7},{9,8},{10,9},{11,1... | collective-permute-start | bytes 15368 | tf_op jit(solution)/shard_map/ppermute | solution.py:34
  218.3 3.9 %collective-permute-start.13 = (f32[16,80]{1,0:T(8,128)S(1)}, f32[16,80]{1,0:T(8,128)S(1)}, u32[]{:S(2)}, u32[]{:S(2)}) collective-permute-start(f32[16,80]{1,0:T(8,128)S(1)} %psum.29), channel_id=1, source_target_pairs={{2,0},{3,1},{4,2},{5,3},{6,4},{7,5},{8,6},{9,7},{10,8},{11,9},{12,... | collective-permute-start | bytes 15368 | tf_op jit(solution)/shard_map/ppermute | solution.py:34
  222.3 4.8 %collective-permute-done.13 = f32[16,80]{1,0:T(8,128)S(1)} collective-permute-done((f32[16,80]{1,0:T(8,128)S(1)}, f32[16,80]{1,0:T(8,128)S(1)}, u32[]{:S(2)}, u32[]{:S(2)}) %collective-permute-start.13) | collective-permute-done | bytes 5152 | tf_op jit(solution)/shard_map/ppermute | solution.py:34
  235.6 5.7 %psum.30 = f32[16,80]{1,0:T(8,128)S(1)} all-reduce(f32[16,80]{1,0:T(8,128)S(1)} %fusion.94), channel_id=1, replica_groups=mesh['member'=4,'region'=128] {'member'}, use_global_device_ids=true, to_apply=%region_8.10 | all-reduce | flops 1280 | bytes 10240 | tf_op jit(solution)/shard_map/psum | solution.py:110
  245.2 6.3 %collective-permute-start.20 = (f32[16,80]{1,0:T(8,128)S(1)}, f32[16,80]{1,0:T(8,128)S(1)}, u32[]{:S(2)}, u32[]{:S(2)}) collective-permute-start(f32[16,80]{1,0:T(8,128)S(1)} %psum.30), channel_id=1, source_target_pairs={{1,0},{2,1},{3,2},{4,3},{5,4},{6,5},{7,6},{8,7},{9,8},{10,9},{11,1... | collective-permute-start | bytes 15368 | tf_op jit(solution)/shard_map/ppermute | solution.py:34
  255.5 4.8 %collective-permute-done.21 = f32[16,80]{1,0:T(8,128)S(1)} collective-permute-done((f32[16,80]{1,0:T(8,128)S(1)}, f32[16,80]{1,0:T(8,128)S(1)}, u32[]{:S(2)}, u32[]{:S(2)}) %collective-permute-start.21) | collective-permute-done | bytes 5152 | tf_op jit(solution)/shard_map/ppermute | solution.py:34
  265.5 6.0 %psum.31 = f32[16,80]{1,0:T(8,128)S(1)} all-reduce(f32[16,80]{1,0:T(8,128)S(1)} %fusion.93), channel_id=1, replica_groups=mesh['member'=4,'region'=128] {'member'}, use_global_device_ids=true, to_apply=%region_12.14 | all-reduce | flops 1280 | bytes 10240 | tf_op jit(solution)/shard_map/psum | solution.py:110
  275.4 6.3 %collective-permute-start.28 = (f32[16,80]{1,0:T(8,128)S(1)}, f32[16,80]{1,0:T(8,128)S(1)}, u32[]{:S(2)}, u32[]{:S(2)}) collective-permute-start(f32[16,80]{1,0:T(8,128)S(1)} %psum.31), channel_id=1, source_target_pairs={{1,0},{2,1},{3,2},{4,3},{5,4},{6,5},{7,6},{8,7},{9,8},{10,9},{11,1... | collective-permute-start | bytes 15368 | tf_op jit(solution)/shard_map/ppermute | solution.py:34
  281.7 3.9 %collective-permute-start.29 = (f32[16,80]{1,0:T(8,128)S(1)}, f32[16,80]{1,0:T(8,128)S(1)}, u32[]{:S(2)}, u32[]{:S(2)}) collective-permute-start(f32[16,80]{1,0:T(8,128)S(1)} %psum.31), channel_id=1, source_target_pairs={{2,0},{3,1},{4,2},{5,3},{6,4},{7,5},{8,6},{9,7},{10,8},{11,9},{12,... | collective-permute-start | bytes 15368 | tf_op jit(solution)/shard_map/ppermute | solution.py:34
  285.7 4.8 %collective-permute-done.29 = f32[16,80]{1,0:T(8,128)S(1)} collective-permute-done((f32[16,80]{1,0:T(8,128)S(1)}, f32[16,80]{1,0:T(8,128)S(1)}, u32[]{:S(2)}, u32[]{:S(2)}) %collective-permute-start.29) | collective-permute-done | bytes 5152 | tf_op jit(solution)/shard_map/ppermute | solution.py:34
  (198 shorter events, 92.3 us)
Async XLA Ops:
  2.3 29.7 %collective-permute-start.6 = (f32[3,16]{1,0:T(4,128)S(1)}, f32[3,16]{1,0:T(4,128)}, u32[]{:S(2)}, u32[]{:S(2)}) collective-permute-start(f32[3,16]{1,0:T(4,128)S(1)} %pad_maximum_fusion.2), channel_id=1, source_target_pairs={{0,2},{1,3},{2,4},{3,5},{4,6},{5,7},{6,8},{7,9},{8,10},{9,11},{10,... | collective-permute-start | bytes 584 | tf_op jit(solution)/shard_map/ppermute | solution.py:34
  7.0 26.9 %collective-permute-start.7 = (f32[3,16]{1,0:T(4,128)S(1)}, f32[3,16]{1,0:T(4,128)}, u32[]{:S(2)}, u32[]{:S(2)}) collective-permute-start(f32[3,16]{1,0:T(4,128)S(1)} %pad_maximum_fusion.2), channel_id=1, source_target_pairs={{0,1},{1,2},{2,3},{3,4},{4,5},{5,6},{6,7},{7,8},{8,9},{9,10},{10,1... | collective-permute-start | bytes 584 | tf_op jit(solution)/shard_map/ppermute | solution.py:34
  11.9 32.1 %collective-permute-start.8 = (f32[3,16]{1,0:T(4,128)S(1)}, f32[3,16]{1,0:T(4,128)}, u32[]{:S(2)}, u32[]{:S(2)}) collective-permute-start(f32[3,16]{1,0:T(4,128)S(1)} %pad_maximum_fusion.2), channel_id=1, source_target_pairs={{1,0},{2,1},{3,2},{4,3},{5,4},{6,5},{7,6},{8,7},{9,8},{10,9},{11,1... | collective-permute-start | bytes 584 | tf_op jit(solution)/shard_map/ppermute | solution.py:34
  17.3 81.8 %collective-permute-start.1 = (f32[20,1,2048]{2,0,1:T(8,128)S(1)}, f32[20,1,2048]{2,0,1:T(8,128)S(1)}, u32[]{:S(2)}, u32[]{:S(2)}) collective-permute-start(f32[20,1,2048]{2,0,1:T(8,128)S(1)} %copy.77), channel_id=1, source_target_pairs={{0,1},{1,2},{2,3},{3,4},{4,5},{5,6},{6,7},{7,8},{8,9},{9,10},{10,1... | collective-permute-start | bytes 491528 | tf_op jit(solution)/shard_map/ppermute | solution.py:22
  21.4 77.8 %collective-permute-start = (f32[20,1,2048]{2,0,1:T(8,128)S(1)}, f32[20,1,2048]{2,0,1:T(8,128)}, u32[]{:S(2)}, u32[]{:S(2)}) collective-permute-start(f32[20,1,2048]{2,0,1:T(8,128)S(1)} %copy.76), channel_id=1, source_target_pairs={{1,0},{2,1},{3,2},{4,3},{5,4},{6,5},{7,6},{8,7},{9,8},{10,9},{11,1... | collective-permute-start | bytes 491528 | tf_op jit(solution)/shard_map/ppermute | solution.py:24
  31.9 14.6 %collective-permute-start.9 = (f32[3,16]{1,0:T(4,128)S(1)}, f32[3,16]{1,0:T(4,128)S(1)}, u32[]{:S(2)}, u32[]{:S(2)}) collective-permute-start(f32[3,16]{1,0:T(4,128)S(1)} %pad_maximum_fusion.2), channel_id=1, source_target_pairs={{2,0},{3,1},{4,2},{5,3},{6,4},{7,5},{8,6},{9,7},{10,8},{11,9},{12,... | collective-permute-start | bytes 584 | tf_op jit(solution)/shard_map/ppermute | solution.py:34
  33.9 19.2 %collective-permute-start.30 = (f32[3,16]{1,0:T(4,128)S(1)}, f32[3,16]{1,0:T(4,128)S(1)}, u32[]{:S(2)}, u32[]{:S(2)}) collective-permute-start(f32[3,16]{1,0:T(4,128)S(1)} %pad_maximum_fusion.5), channel_id=1, source_target_pairs={{0,2},{1,3},{2,4},{3,5},{4,6},{5,7},{6,8},{7,9},{8,10},{9,11},{10,... | collective-permute-start | bytes 584 | tf_op jit(solution)/shard_map/ppermute | solution.py:34
  44.0 11.0 %collective-permute-start.31 = (f32[3,16]{1,0:T(4,128)S(1)}, f32[3,16]{1,0:T(4,128)}, u32[]{:S(2)}, u32[]{:S(2)}) collective-permute-start(f32[3,16]{1,0:T(4,128)S(1)} %pad_maximum_fusion.5), channel_id=1, source_target_pairs={{0,1},{1,2},{2,3},{3,4},{4,5},{5,6},{6,7},{7,8},{8,9},{9,10},{10,1... | collective-permute-start | bytes 584 | tf_op jit(solution)/shard_map/ppermute | solution.py:34
  46.5 15.7 %collective-permute-start.32 = (f32[3,16]{1,0:T(4,128)S(1)}, f32[3,16]{1,0:T(4,128)}, u32[]{:S(2)}, u32[]{:S(2)}) collective-permute-start(f32[3,16]{1,0:T(4,128)S(1)} %pad_maximum_fusion.5), channel_id=1, source_target_pairs={{1,0},{2,1},{3,2},{4,3},{5,4},{6,5},{7,6},{8,7},{9,8},{10,9},{11,1... | collective-permute-start | bytes 584 | tf_op jit(solution)/shard_map/ppermute | solution.py:34
  53.0 11.7 %collective-permute-start.33 = (f32[3,16]{1,0:T(4,128)S(1)}, f32[3,16]{1,0:T(4,128)S(1)}, u32[]{:S(2)}, u32[]{:S(2)}) collective-permute-start(f32[3,16]{1,0:T(4,128)S(1)} %pad_maximum_fusion.5), channel_id=1, source_target_pairs={{2,0},{3,1},{4,2},{5,3},{6,4},{7,5},{8,6},{9,7},{10,8},{11,9},{12,... | collective-permute-start | bytes 584 | tf_op jit(solution)/shard_map/ppermute | solution.py:34
  55.0 16.9 %collective-permute-start.22 = (f32[3,16]{1,0:T(4,128)S(1)}, f32[3,16]{1,0:T(4,128)S(1)}, u32[]{:S(2)}, u32[]{:S(2)}) collective-permute-start(f32[3,16]{1,0:T(4,128)S(1)} %pad_maximum_fusion.4), channel_id=1, source_target_pairs={{0,2},{1,3},{2,4},{3,5},{4,6},{5,7},{6,8},{7,9},{8,10},{9,11},{10,... | collective-permute-start | bytes 584 | tf_op jit(solution)/shard_map/ppermute | solution.py:34
  62.2 11.5 %collective-permute-start.23 = (f32[3,16]{1,0:T(4,128)S(1)}, f32[3,16]{1,0:T(4,128)S(1)}, u32[]{:S(2)}, u32[]{:S(2)}) collective-permute-start(f32[3,16]{1,0:T(4,128)S(1)} %pad_maximum_fusion.4), channel_id=1, source_target_pairs={{0,1},{1,2},{2,3},{3,4},{4,5},{5,6},{6,7},{7,8},{8,9},{9,10},{10,1... | collective-permute-start | bytes 584 | tf_op jit(solution)/shard_map/ppermute | solution.py:34
  65.3 15.7 %collective-permute-start.24 = (f32[3,16]{1,0:T(4,128)S(1)}, f32[3,16]{1,0:T(4,128)}, u32[]{:S(2)}, u32[]{:S(2)}) collective-permute-start(f32[3,16]{1,0:T(4,128)S(1)} %pad_maximum_fusion.4), channel_id=1, source_target_pairs={{1,0},{2,1},{3,2},{4,3},{5,4},{6,5},{7,6},{8,7},{9,8},{10,9},{11,1... | collective-permute-start | bytes 584 | tf_op jit(solution)/shard_map/ppermute | solution.py:34
  71.8 11.7 %collective-permute-start.25 = (f32[3,16]{1,0:T(4,128)S(1)}, f32[3,16]{1,0:T(4,128)S(1)}, u32[]{:S(2)}, u32[]{:S(2)}) collective-permute-start(f32[3,16]{1,0:T(4,128)S(1)} %pad_maximum_fusion.4), channel_id=1, source_target_pairs={{2,0},{3,1},{4,2},{5,3},{6,4},{7,5},{8,6},{9,7},{10,8},{11,9},{12,... | collective-permute-start | bytes 584 | tf_op jit(solution)/shard_map/ppermute | solution.py:34
  73.8 15.5 %collective-permute-start.14 = (f32[3,16]{1,0:T(4,128)S(1)}, f32[3,16]{1,0:T(4,128)S(1)}, u32[]{:S(2)}, u32[]{:S(2)}) collective-permute-start(f32[3,16]{1,0:T(4,128)S(1)} %pad_maximum_fusion.3), channel_id=1, source_target_pairs={{0,2},{1,3},{2,4},{3,5},{4,6},{5,7},{6,8},{7,9},{8,10},{9,11},{10,... | collective-permute-start | bytes 584 | tf_op jit(solution)/shard_map/ppermute | solution.py:34
  81.0 11.0 %collective-permute-start.15 = (f32[3,16]{1,0:T(4,128)S(1)}, f32[3,16]{1,0:T(4,128)}, u32[]{:S(2)}, u32[]{:S(2)}) collective-permute-start(f32[3,16]{1,0:T(4,128)S(1)} %pad_maximum_fusion.3), channel_id=1, source_target_pairs={{0,1},{1,2},{2,3},{3,4},{4,5},{5,6},{6,7},{7,8},{8,9},{9,10},{10,1... | collective-permute-start | bytes 584 | tf_op jit(solution)/shard_map/ppermute | solution.py:34
  89.3 8.9 %collective-permute-start.17 = (f32[3,16]{1,0:T(4,128)S(1)}, f32[3,16]{1,0:T(4,128)}, u32[]{:S(2)}, u32[]{:S(2)}) collective-permute-start(f32[3,16]{1,0:T(4,128)S(1)} %pad_maximum_fusion.3), channel_id=1, source_target_pairs={{2,0},{3,1},{4,2},{5,3},{6,4},{7,5},{8,6},{9,7},{10,8},{11,9},{12,... | collective-permute-start | bytes 584 | tf_op jit(solution)/shard_map/ppermute | solution.py:34
  121.0 20.9 %all-to-all-start = ((f32[4,1,81920]{2,1,0:T(1,128)}), f32[4,1,81920]{2,1,0:T(1,128)S(1)}, u32[]{:S(2)}, u32[]{:S(2)}) async-start(f32[4,1,81920]{2,1,0:T(1,128)} %reshape.509), calls=%async_computation | async-start | bytes 2621440 | tf_op jit(solution)/shard_map/all_to_all | solution.py:87
  176.1 14.5 %collective-permute-start.2 = (f32[16,80]{1,0:T(8,128)S(1)}, f32[16,80]{1,0:T(8,128)S(1)}, u32[]{:S(2)}, u32[]{:S(2)}) collective-permute-start(f32[16,80]{1,0:T(8,128)S(1)} %psum.28), channel_id=1, source_target_pairs={{0,2},{1,3},{2,4},{3,5},{4,6},{5,7},{6,8},{7,9},{8,10},{9,11},{10,... | collective-permute-start | bytes 15368 | tf_op jit(solution)/shard_map/ppermute | solution.py:34
  180.1 10.6 %collective-permute-start.3 = (f32[16,80]{1,0:T(8,128)S(1)}, f32[16,80]{1,0:T(8,128)S(1)}, u32[]{:S(2)}, u32[]{:S(2)}) collective-permute-start(f32[16,80]{1,0:T(8,128)S(1)} %psum.28), channel_id=1, source_target_pairs={{0,1},{1,2},{2,3},{3,4},{4,5},{5,6},{6,7},{7,8},{8,9},{9,10},{10,1... | collective-permute-start | bytes 15368 | tf_op jit(solution)/shard_map/ppermute | solution.py:34
  188.3 8.9 %collective-permute-start.5 = (f32[16,80]{1,0:T(8,128)S(1)}, f32[16,80]{1,0:T(8,128)S(1)}, u32[]{:S(2)}, u32[]{:S(2)}) collective-permute-start(f32[16,80]{1,0:T(8,128)S(1)} %psum.28), channel_id=1, source_target_pairs={{2,0},{3,1},{4,2},{5,3},{6,4},{7,5},{8,6},{9,7},{10,8},{11,9},{12,... | collective-permute-start | bytes 15368 | tf_op jit(solution)/shard_map/ppermute | solution.py:34
  208.1 14.1 %collective-permute-start.10 = (f32[16,80]{1,0:T(8,128)S(1)}, f32[16,80]{1,0:T(8,128)S(1)}, u32[]{:S(2)}, u32[]{:S(2)}) collective-permute-start(f32[16,80]{1,0:T(8,128)S(1)} %psum.29), channel_id=1, source_target_pairs={{0,2},{1,3},{2,4},{3,5},{4,6},{5,7},{6,8},{7,9},{8,10},{9,11},{10,... | collective-permute-start | bytes 15368 | tf_op jit(solution)/shard_map/ppermute | solution.py:34
  210.0 12.2 %collective-permute-start.11 = (f32[16,80]{1,0:T(8,128)S(1)}, f32[16,80]{1,0:T(8,128)S(1)}, u32[]{:S(2)}, u32[]{:S(2)}) collective-permute-start(f32[16,80]{1,0:T(8,128)S(1)} %psum.29), channel_id=1, source_target_pairs={{0,1},{1,2},{2,3},{3,4},{4,5},{5,6},{6,7},{7,8},{8,9},{9,10},{10,1... | collective-permute-start | bytes 15368 | tf_op jit(solution)/shard_map/ppermute | solution.py:34
  212.0 10.3 %collective-permute-start.12 = (f32[16,80]{1,0:T(8,128)S(1)}, f32[16,80]{1,0:T(8,128)S(1)}, u32[]{:S(2)}, u32[]{:S(2)}) collective-permute-start(f32[16,80]{1,0:T(8,128)S(1)} %psum.29), channel_id=1, source_target_pairs={{1,0},{2,1},{3,2},{4,3},{5,4},{6,5},{7,6},{8,7},{9,8},{10,9},{11,1... | collective-permute-start | bytes 15368 | tf_op jit(solution)/shard_map/ppermute | solution.py:34
  241.3 14.1 %collective-permute-start.18 = (f32[16,80]{1,0:T(8,128)S(1)}, f32[16,80]{1,0:T(8,128)S(1)}, u32[]{:S(2)}, u32[]{:S(2)}) collective-permute-start(f32[16,80]{1,0:T(8,128)S(1)} %psum.30), channel_id=1, source_target_pairs={{0,2},{1,3},{2,4},{3,5},{4,6},{5,7},{6,8},{7,9},{8,10},{9,11},{10,... | collective-permute-start | bytes 15368 | tf_op jit(solution)/shard_map/ppermute | solution.py:34
  243.2 12.2 %collective-permute-start.19 = (f32[16,80]{1,0:T(8,128)S(1)}, f32[16,80]{1,0:T(8,128)S(1)}, u32[]{:S(2)}, u32[]{:S(2)}) collective-permute-start(f32[16,80]{1,0:T(8,128)S(1)} %psum.30), channel_id=1, source_target_pairs={{0,1},{1,2},{2,3},{3,4},{4,5},{5,6},{6,7},{7,8},{8,9},{9,10},{10,1... | collective-permute-start | bytes 15368 | tf_op jit(solution)/shard_map/ppermute | solution.py:34
  245.2 10.3 %collective-permute-start.20 = (f32[16,80]{1,0:T(8,128)S(1)}, f32[16,80]{1,0:T(8,128)S(1)}, u32[]{:S(2)}, u32[]{:S(2)}) collective-permute-start(f32[16,80]{1,0:T(8,128)S(1)} %psum.30), channel_id=1, source_target_pairs={{1,0},{2,1},{3,2},{4,3},{5,4},{6,5},{7,6},{8,7},{9,8},{10,9},{11,1... | collective-permute-start | bytes 15368 | tf_op jit(solution)/shard_map/ppermute | solution.py:34
  251.5 8.9 %collective-permute-start.21 = (f32[16,80]{1,0:T(8,128)S(1)}, f32[16,80]{1,0:T(8,128)S(1)}, u32[]{:S(2)}, u32[]{:S(2)}) collective-permute-start(f32[16,80]{1,0:T(8,128)S(1)} %psum.30), channel_id=1, source_target_pairs={{2,0},{3,1},{4,2},{5,3},{6,4},{7,5},{8,6},{9,7},{10,8},{11,9},{12,... | collective-permute-start | bytes 15368 | tf_op jit(solution)/shard_map/ppermute | solution.py:34
  271.5 14.1 %collective-permute-start.26 = (f32[16,80]{1,0:T(8,128)S(1)}, f32[16,80]{1,0:T(8,128)S(1)}, u32[]{:S(2)}, u32[]{:S(2)}) collective-permute-start(f32[16,80]{1,0:T(8,128)S(1)} %psum.31), channel_id=1, source_target_pairs={{0,2},{1,3},{2,4},{3,5},{4,6},{5,7},{6,8},{7,9},{8,10},{9,11},{10,... | collective-permute-start | bytes 15368 | tf_op jit(solution)/shard_map/ppermute | solution.py:34
  273.4 12.2 %collective-permute-start.27 = (f32[16,80]{1,0:T(8,128)S(1)}, f32[16,80]{1,0:T(8,128)S(1)}, u32[]{:S(2)}, u32[]{:S(2)}) collective-permute-start(f32[16,80]{1,0:T(8,128)S(1)} %psum.31), channel_id=1, source_target_pairs={{0,1},{1,2},{2,3},{3,4},{4,5},{5,6},{6,7},{7,8},{8,9},{9,10},{10,1... | collective-permute-start | bytes 15368 | tf_op jit(solution)/shard_map/ppermute | solution.py:34
  275.4 10.3 %collective-permute-start.28 = (f32[16,80]{1,0:T(8,128)S(1)}, f32[16,80]{1,0:T(8,128)S(1)}, u32[]{:S(2)}, u32[]{:S(2)}) collective-permute-start(f32[16,80]{1,0:T(8,128)S(1)} %psum.31), channel_id=1, source_target_pairs={{1,0},{2,1},{3,2},{4,3},{5,4},{6,5},{7,6},{8,7},{9,8},{10,9},{11,1... | collective-permute-start | bytes 15368 | tf_op jit(solution)/shard_map/ppermute | solution.py:34
  281.7 8.9 %collective-permute-start.29 = (f32[16,80]{1,0:T(8,128)S(1)}, f32[16,80]{1,0:T(8,128)S(1)}, u32[]{:S(2)}, u32[]{:S(2)}) collective-permute-start(f32[16,80]{1,0:T(8,128)S(1)} %psum.31), channel_id=1, source_target_pairs={{2,0},{3,1},{4,2},{5,3},{6,4},{7,5},{8,6},{9,7},{10,8},{11,9},{12,... | collective-permute-start | bytes 15368 | tf_op jit(solution)/shard_map/ppermute | solution.py:34
  (20 other events, 344.5 us)
where the time goes:
time: 298 us; the launch traced here: 296 us
  starting transfers between devices  139 us (47%)
  local copies, waits for them, and re-layouts  62.4 us (21%)
  waiting for transfers between devices  42 us (14%)
  blocking collectives  23.3 us (8%)
  other arithmetic  14.7 us (5%)
  matrix products  13.8 us (5%)
    ppermute x32, starting transfers between devices, from_behind(): lax.ppermute(value, axis, [(source, source + steps) for source in range(i...  127 us
    unnamed x57, local copies, waits for them, and re-layouts  27.7 us
    ppermute x32, waiting for transfers between devices, from_behind(): lax.ppermute(value, axis, [(source, source + steps) for source in range(i...  27.3 us
    psum x4, blocking collectives, local(): obs_prior = lax.psum(owned_prior.T, 'member')  23.3 us
    all_to_all x1, waiting for transfers between devices, local(): lax.all_to_all(diffused_tracer, 'member', split_axis=2, concat_axis=0, ti...  14.7 us
    dot_general x4, matrix products, regress(): jnp.einsum('ec,je->cj', state_anomaly, anomaly, precision=highest)  8.35 us
    add x1, local copies, waits for them, and re-layouts, local(): prior_tracer_ensemble + diffusion_numbers[None] * (upper_boundary_lines +...  6.23 us
    all_to_all x2, local copies, waits for them, and re-layouts, local(): lax.all_to_all(diffused_tracer, 'member', split_axis=2, concat_axis=0, ti...  6.07 us
  transfers between devices with their start and end apart: 35, of which 6 were waited for; matrix products, arithmetic and copies ran while one was open for 5% of the time, Pallas kernels for 0%

commit v1 on v0

v1 whole, which is shorter than its diff:
```python
import functools

import jax
import jax.numpy as jnp
from jax import lax
from jax.experimental import pallas as pl
from jax.experimental.pallas import tpu as pltpu
from jax.sharding import PartitionSpec as P

REACH = 2
RADIUS = 16
epsilon = 1e-05
LANES = 128
f32 = jnp.float32
bf16 = jnp.bfloat16

FACTS = 5
READING, VARIANCE, ROW, COLUMN, LIVE = range(FACTS)


def lane_of(shape):
    return lax.broadcasted_iota(jnp.int32, shape, len(shape) - 1)


def row_of(shape):
    return lax.broadcasted_iota(jnp.int32, shape, len(shape) - 2)


def halves(x):
    hi = x.astype(bf16).astype(f32)
    return hi, x - hi


def product(a, b, dims):
    a_hi, a_lo = [v.astype(bf16) for v in halves(a)]
    b_hi, b_lo = [v.astype(bf16) for v in halves(b)]
    dot = functools.partial(lax.dot_general, dimension_numbers=(dims, ((), ())), preferred_element_type=f32)
    return dot(a_hi, b_hi) + (dot(a_hi, b_lo) + dot(a_lo, b_hi))


def step_kernel(
    region_ref, site_ref, tally_ref, tracer_ref, above_ref, below_ref, diffusion_ref,
    site_vec_ref, reading_ref, variance_ref, stepped_ref, parcel_ref, board,
):
    own, rows, width = tracer_ref.shape
    batches, slots = site_ref.shape
    copies = parcel_ref.shape[0]
    quarters = 4
    tiles = width // LANES // quarters
    region = region_ref[0]
    diffusion = diffusion_ref[...]
    row = row_of((rows, width))
    for e in range(own):
        x = tracer_ref[e]
        lower = jnp.where(row == 0, above_ref[e : e + 1, :], pltpu.roll(x, 1, 0))
        upper = jnp.where(row == rows - 1, below_ref[e : e + 1, :], pltpu.roll(x, rows - 1, 0))
        east = pltpu.roll(x, width - 1, 1)
        west = pltpu.roll(x, 1, 1)
        y = x + diffusion * (upper + lower + east + west - 4.0 * x)
        for q in range(quarters):
            for t in range(tiles):
                at = ((q * own + e) * tiles + t) * rows
                col = (q * tiles + t) * LANES
                stepped_ref[at : at + rows, :] = y[:, col : col + LANES]
    board[...] = jnp.zeros_like(board)
    lane = lane_of((own, LANES))
    for b in range(batches):
        picked = jnp.zeros((own, LANES), f32)
        for k in range(slots):
            cell = site_ref[b, k]
            col = lax.rem(cell, width)
            tile = lax.div(col, LANES)
            start = lax.div(tile, tiles) * (own * tiles * rows) + lax.rem(tile, tiles) * rows + lax.div(cell, width)
            line = stepped_ref[pl.ds(start, own, stride=tiles * rows), :]
            shift = lax.rem(k - lax.rem(col, LANES) + LANES, LANES)
            picked = jnp.where(lane == k, pltpu.roll(line, shift, 1), picked)
        at = b * 32
        board[at : at + own, :] = picked
        cells = site_vec_ref[b : b + 1, :]
        count = tally_ref[b, region]
        facts = [
            reading_ref[b : b + 1, :],
            variance_ref[b : b + 1, :],
            (region * rows + lax.div(cells, width)).astype(f32),
            lax.rem(cells, width).astype(f32),
            jnp.where(lane_of((1, slots)) < count, 1.0, 0.0),
        ]
        for i, fact in enumerate(facts):
            board[at + own + i : at + own + i + 1, 0:slots] = fact
    parcel = board[...].T[:slots, :]
    for i in range(copies):
        parcel_ref[i] = parcel


def gather_kernel(parcels_ref, pair_ref):
    count, slots, _ = parcels_ref.shape
    members = count // 2
    own = 20
    lane = lane_of((slots, LANES))
    for b in range(4):
        for p in range(2):
            total = jnp.zeros((slots, LANES), f32)
            for m in range(members):
                moved = pltpu.roll(parcels_ref[p * members + m], (own * m - 32 * b) % LANES, 1)
                end = own * (m + 1) + (FACTS if m == members - 1 else 0)
                total = jnp.where((lane >= own * m) & (lane < end), moved, total)
            at = (b * 2 + p) * slots
            pair_ref[at : at + slots, :] = total


def beside(hi, lo):
    lane = lane_of(hi.shape)
    again = pltpu.roll(hi, 80, 1)
    last = pltpu.roll(lo, 32, 1)
    first = jnp.where(lane < 80, hi, again)
    second = jnp.where(lane < 32, again, last)
    return jnp.concatenate([first.astype(bf16), second.astype(bf16)], axis=1)


def below_each_other(x):
    hi, lo = halves(x)
    hi, lo = hi.astype(bf16), lo.astype(bf16)
    return jnp.concatenate([hi, lo, hi, jnp.zeros((16, x.shape[1]), bf16)], axis=0)


def update_kernel(
    place_ref, own_ref, minus_ref, plus_ref, down_ref, up_ref, state_ref,
    out_ref, obs, inc_ref, ano_ref, gain_lhs, inc_lhs, near_ref, board, updated, *, width,
):
    members = 80
    parity = place_ref[0]
    quarter = place_ref[1]
    region = place_ref[2]
    rows, quarter_width = out_ref.shape[1:]
    tiles = quarter_width // LANES
    scale = 1.0 / (RADIUS * RADIUS)
    pieces = [
        (down_ref, 160), (down_ref, 96), (down_ref, 0), (minus_ref, 0), (own_ref, 0), (plus_ref, 0), (up_ref, 0), (up_ref, 96), (up_ref, 160),
        (down_ref, 128), (down_ref, 32), (minus_ref, 32), (own_ref, 32), (plus_ref, 32), (up_ref, 32), (up_ref, 128),
        (down_ref, 64), (minus_ref, 64), (own_ref, 64), (plus_ref, 64), (up_ref, 64),
        (minus_ref, 96), (own_ref, 96), (plus_ref, 96),
    ]
    for i, (ref, at) in enumerate(pieces):
        obs[32 * i : 32 * i + 32, :] = ref[at : at + 32, :]
    starts = [0, 288, 512, 672, 768]
    centres = [96, 64, 32, 0]
    total = starts[-1]
    pick = jnp.where(lane_of((8, LANES)) == members + ROW + row_of((8, LANES)), 1.0, 0.0)
    across = lax.dot_general(
        pick, obs[...], (((1,), (1,)), ((), ())), precision=lax.Precision.HIGHEST, preferred_element_type=f32
    )
    for b in range(4):
        n = starts[b + 1] - starts[b]
        x = obs[starts[b] : starts[b + 1], :]
        member = lane_of((n, LANES)) < members
        fact = lambda i: x[:, members + i : members + i + 1]
        average = jnp.sum(jnp.where(member, x, 0.0), axis=1, keepdims=True) / members
        anomaly = jnp.where(member, x - average, 0.0)
        spread = jnp.sum(anomaly * anomaly, axis=1, keepdims=True) / (members - 1) + epsilon
        live = fact(LIVE)
        noise = jnp.where(live > 0.5, fact(VARIANCE), 1.0)
        posterior = 1.0 / (1.0 / spread + 1.0 / noise)
        post_mean = posterior * (average / spread + fact(READING) / noise)
        increment = post_mean - average + (jnp.sqrt(posterior / spread) - 1.0) * anomaly
        increment = jnp.where(member, increment, 0.0)
        scaled = anomaly * (live / ((members - 1) * spread))
        inc_ref[0:n, :] = increment
        ano_ref[0:n, :] = scaled
        at = centres[b] + 16 * parity
        gain_lhs[b] = beside(*halves(ano_ref[pl.ds(at, 80), :]))
        near_ref[b] = obs[pl.ds(starts[b] + at, 80), :]
        board[...] = jnp.zeros_like(board)
        board[0:80, :] = inc_ref[pl.ds(at, 80), :]
        inc_lhs[b] = beside(*halves(board[...].T[0:80, :]))
        if b < 3:
            y = obs[starts[b + 1] : total, :]
            m = total - starts[b + 1]
            inside = lane_of((m, LANES)) < members
            mean = jnp.sum(jnp.where(inside, y, 0.0), axis=1, keepdims=True) / members
            off = jnp.where(inside, y - mean, 0.0)
            covariance = product(off, scaled, ((1,), (1,)))
            row_gap = y[:, members + ROW : members + ROW + 1] - across[0:1, starts[b] : starts[b + 1]]
            col_gap = jnp.abs(y[:, members + COLUMN : members + COLUMN + 1] - across[1:2, starts[b] : starts[b + 1]])
            col_gap = jnp.minimum(col_gap, width - col_gap)
            remain = jnp.maximum(1.0 - (row_gap * row_gap + col_gap * col_gap) * scale, 0.0)
            weights = remain * remain * covariance
            obs[starts[b + 1] : total, :] = y + product(weights, increment, ((1,), (0,)))
    cols = (lane_of((80, quarter_width)) + quarter * quarter_width).astype(f32)
    closeness = []
    for b in range(4):
        gap = jnp.abs(cols - near_ref[b, :, members + COLUMN : members + COLUMN + 1])
        gap = jnp.minimum(gap, width - gap)
        closeness.append(1.0 - gap * gap * scale)
    for r in range(rows):
        state = jnp.concatenate(
            [state_ref[pl.ds(t * rows + r, members, stride=tiles * rows), :] for t in range(tiles)], axis=1
        )
        for b in range(4):
            mean = jnp.mean(state, axis=0, keepdims=True)
            covariance = jnp.dot(gain_lhs[b], below_each_other(state - mean), preferred_element_type=f32)
            gap = (region * rows + r).astype(f32) - near_ref[b, :, members + ROW : members + ROW + 1]
            remain = jnp.maximum(closeness[b] - gap * gap * scale, 0.0)
            weights = remain * remain * covariance
            state = state + jnp.dot(inc_lhs[b], below_each_other(weights), preferred_element_type=f32)
        for t in range(tiles):
            updated[pl.ds(t * rows + r, members, stride=tiles * rows), :] = state[:, t * LANES : (t + 1) * LANES]
    for e in range(members):
        for t in range(tiles):
            at = (e * tiles + t) * rows
            out_ref[e, :, t * LANES : (t + 1) * LANES] = updated[at : at + rows, :]


def local(tracer, diffusion, sites, readings, variances, tally):
    own, rows, width = tracer.shape
    regions = lax.axis_size("region")
    quarters = lax.axis_size("member")
    batches, slots = sites.shape
    quarter_width = width // quarters
    members = own * quarters
    region = lax.axis_index("region")
    quarter = lax.axis_index("member")
    upward = [(i, i + 1) for i in range(regions - 1)]
    downward = [(i + 1, i) for i in range(regions - 1)]
    above = lax.ppermute(tracer[:, rows - 1, :], "region", upward)
    below = lax.ppermute(tracer[:, 0, :], "region", downward)
    vmem = pl.BlockSpec(memory_space=pltpu.VMEM)
    smem = pl.BlockSpec(memory_space=pltpu.SMEM)
    limit = pltpu.CompilerParams(vmem_limit_bytes=32 * 1024 * 1024)
    stepped, parcel = pl.pallas_call(
        step_kernel,
        out_shape=(
            jax.ShapeDtypeStruct((own * rows * width // LANES, LANES), f32),
            jax.ShapeDtypeStruct((2 * quarters, slots, LANES), f32),
        ),
        in_specs=[smem] * 3 + [vmem] * 7,
        out_specs=(vmem, vmem),
        scratch_shapes=[pltpu.VMEM((LANES, LANES), f32)],
        compiler_params=limit,
        name="step",
    )(region[None].astype(jnp.int32), sites, tally, tracer, above, below, diffusion, sites, readings, variances)
    lines = [[2 * quarters * g + i for i in range(2 * quarters)] for g in range(regions // 2)]
    parcels = lax.all_to_all(parcel, ("region", "member"), 0, 0, axis_index_groups=lines)
    state = lax.all_to_all(
        stepped.reshape(quarters, own * rows * quarter_width // LANES, LANES), "member", 0, 0
    ).reshape(members * rows * quarter_width // LANES, LANES)
    pair = pl.pallas_call(
        gather_kernel,
        out_shape=jax.ShapeDtypeStruct((batches * 2 * slots, LANES), f32),
        in_specs=[vmem],
        out_specs=vmem,
        name="gather",
    )(parcels)

    def shifted(value, steps):
        return lax.ppermute(value, "region", [(i, (i + steps) % regions) for i in range(regions)])

    block = 2 * slots
    minus, plus = shifted(pair, 2), shifted(pair, -2)
    down = shifted(jnp.concatenate([plus[: 3 * block], pair[: 2 * block], minus[:block]]), 6)
    up = shifted(jnp.concatenate([minus[: 3 * block], pair[: 2 * block], plus[:block]]), -6)
    place = jnp.stack([region % 2, quarter, region]).astype(jnp.int32)
    total = 24 * block
    return pl.pallas_call(
        functools.partial(update_kernel, width=width),
        out_shape=jax.ShapeDtypeStruct((members, rows, quarter_width), f32),
        in_specs=[smem] + [vmem] * 6,
        out_specs=vmem,
        scratch_shapes=[
            pltpu.VMEM((total, LANES), f32),
            pltpu.VMEM((9 * block, LANES), f32),
            pltpu.VMEM((9 * block, LANES), f32),
            pltpu.VMEM((4, 80, 256), bf16),
            pltpu.VMEM((4, 80, 256), bf16),
            pltpu.VMEM((4, 80, LANES), f32),
            pltpu.VMEM((LANES, LANES), f32),
            pltpu.VMEM(state.shape, f32),
        ],
        compiler_params=limit,
        name="update",
    )(place, pair, minus, plus, down, up, state)


def solution(mesh):
    placed = (
        P("member", "region", None),
        P("region", None),
        P(None, "region"),
        P(None, "region"),
        P(None, "region"),
        P(),
    )
    return jax.shard_map(
        local, mesh=mesh, in_specs=placed, out_specs=P(None, "region", "member"), check_vma=False
    )
```

time: 298 us -> 92.9 us (0.31)
  the two profiles are of different devices: /device:TPU:248 before, /device:TPU:1 now
where the time goes in v1:
time: 92.9 us; the launch traced here: 92.4 us
  starting transfers between devices  32.8 us (35%)
  waiting for transfers between devices  23.3 us (25%)
  Pallas kernels  20.1 us (22%)
  blocking collectives  12.1 us (13%)
  local copies, waits for them, and re-layouts  3.87 us (4%)
    ppermute x4, starting transfers between devices, shifted(): lax.ppermute(value, 'region', [(i, (i + steps) % regions) for i in range(...  21.7 us
    ppermute x4, waiting for transfers between devices, shifted(): lax.ppermute(value, 'region', [(i, (i + steps) % regions) for i in range(...  16.7 us
    pallas_call x1, Pallas kernels, local(): pl.pallas_call(functools.partial(update_kernel, width=width), out_shape=j...  15.4 us
    all_to_all x1, blocking collectives, local(): lax.all_to_all(parcel, ('region', 'member'), 0, 0, axis_index_groups=lines)  12.1 us
    ppermute x1, starting transfers between devices, local(): above = lax.ppermute(tracer[:, rows - 1, :], 'region', upward)  5.49 us
    ppermute x1, waiting for transfers between devices, local(): below = lax.ppermute(tracer[:, 0, :], 'region', downward)  5.39 us
    all_to_all x1, starting transfers between devices, local(): lax.all_to_all(stepped.reshape(quarters, own * rows * quarter_width // LA...  4.28 us
    pallas_call x1, Pallas kernels, local(): pl.pallas_call(step_kernel, out_shape=(jax.ShapeDtypeStruct((own * rows *...  3.15 us
  transfers between devices with their start and end apart: 7, of which 5 were waited for; matrix products, arithmetic and copies ran while one was open for 1% of the time, Pallas kernels for 2%

profile of v1, /device:TPU:1, one launch (start us, length us, event | category | flops | bytes accessed | tf_op | source)
XLA Modules:
  0.0 92.4 jit_solution(9263757080691561992)
XLA Ops:
  0.0 0.0 copy-start.5
  0.0 0.0 copy-start.3
  0.0 0.0 copy-start.2
  0.0 2.1 %fusion.2 = (f32[20,1,2048]{2,1,0:T(1,128)S(1)}, f32[20,1,2048]{2,1,0:T(1,128)S(1)}) fusion(f32[20,8,2048]{2,1,0:T(8,128)} %tracer_ref.1), kind=kLoop, calls=%fused_computation.7 | loop fusion | bytes 655360 | tf_op jit(solution)/shard_map/slice | solution.py:225
  2.1 0.1 copy.14
  2.2 5.5 %collective-permute-start = (f32[20,2048]{1,0:T(8,128)S(1)}, f32[20,2048]{1,0:T(8,128)S(1)}, u32[]{:S(2)}, u32[]{:S(2)}) collective-permute-start(f32[20,2048]{1,0:T(8,128)S(1)} %bitcast.12), channel_id=1, source_target_pairs={{0,1},{1,2},{2,3},{3,4},{4,5},{5,6},{6,7},{7,8},{8,9},{9,10},{10,1... | collective-permute-start | bytes 491528 | tf_op jit(solution)/shard_map/ppermute | solution.py:224
  7.7 0.1 copy.13
  7.7 1.3 %collective-permute-start.1 = (f32[20,2048]{1,0:T(8,128)S(1)}, f32[20,2048]{1,0:T(8,128)S(1)}, u32[]{:S(2)}, u32[]{:S(2)}) collective-permute-start(f32[20,2048]{1,0:T(8,128)S(1)} %bitcast.13), channel_id=1, source_target_pairs={{1,0},{2,1},{3,2},{4,3},{5,4},{6,5},{7,6},{8,7},{9,8},{10,9},{11,1... | collective-permute-start | bytes 491528 | tf_op jit(solution)/shard_map/ppermute | solution.py:225
  9.1 1.2 %collective-permute-done.above_ref = f32[20,2048]{1,0:T(8,128)S(1)} collective-permute-done((f32[20,2048]{1,0:T(8,128)S(1)}, f32[20,2048]{1,0:T(8,128)S(1)}, u32[]{:S(2)}, u32[]{:S(2)}) %collective-permute-start) | collective-permute-done | bytes 163872 | tf_op jit(solution)/shard_map/ppermute | solution.py:224
  10.3 5.4 %collective-permute-done.1.below_ref = f32[20,2048]{1,0:T(8,128)S(1)} collective-permute-done((f32[20,2048]{1,0:T(8,128)S(1)}, f32[20,2048]{1,0:T(8,128)S(1)}, u32[]{:S(2)}, u32[]{:S(2)}) %collective-permute-start.1) | collective-permute-done | bytes 163872 | tf_op jit(solution)/shard_map/ppermute | solution.py:225
  15.7 0.0 copy-done
  15.7 0.0 copy-done.4
  15.7 0.0 copy-done.6
  15.7 0.0 copy-done.5
  15.7 0.0 copy-done.3
  15.7 3.1 %step.1 = (f32[2560,128]{1,0:T(8,128)}, f32[8,16,128]{2,1,0:T(8,128)S(1)}) custom-call(s32[1]{0:T(128)} %bitcast.2.region_ref, s32[4,16]{1,0:T(4,128)S(1)} %copy-done.3, s32[4,128]{1,0:T(4,128)S(1)} %copy-done.4, f32[20,8,2048]{2,1,0:T(8,128)S(1)} %copy-done, f32[20,2048]{1,0:T(8,128)S(1)} %collective-permute-done.above_ref, ...), custom_call_target="tpu_custom_call" | custom-call | tf_op jit(solution)/shard_map/step/pallas_call | solution.py:229
  18.9 12.1 %all_to_all.10.parcels_ref = f32[8,16,128]{2,1,0:T(8,128)} all-to-all(f32[8,16,128]{2,1,0:T(8,128)S(1)} %get-tuple-element.7), channel_id=1, replica_groups={{0,128,256,384,1,129,257,385},{2,130,258,386,3,131,259,387},{4,132,260,..., dimensions={0} | all-to-all | bytes 131072 | tf_op jit(solution)/shard_map/all_to_all | solution.py:242
  30.9 4.3 %all-to-all-start.1 = ((f32[4,640,128]{2,1,0:T(8,128)}), f32[4,640,128]{2,1,0:T(8,128)S(1)}, u32[]{:S(2)}, u32[]{:S(2)}) async-start(f32[4,640,128]{2,1,0:T(8,128)} %bitcast.5), calls=%async_computation.1 | async-start | bytes 2621440 | tf_op jit(solution)/shard_map/all_to_all | solution.py:243
  35.2 1.6 %gather.1.own_ref = f32[128,128]{1,0:T(8,128)} custom-call(f32[8,16,128]{2,1,0:T(8,128)} %all_to_all.10.parcels_ref), custom_call_target="tpu_custom_call" | custom-call | tf_op jit(solution)/shard_map/gather/pallas_call | solution.py:246
  36.8 12.5 %collective-permute-start.3 = (f32[128,128]{1,0:T(8,128)}, f32[128,128]{1,0:T(8,128)S(1)}, u32[]{:S(2)}, u32[]{:S(2)}) collective-permute-start(f32[128,128]{1,0:T(8,128)} %gather.1.own_ref), channel_id=1, source_target_pairs={{0,126},{1,127},{2,0},{3,1},{4,2},{5,3},{6,4},{7,5},{8,6},{9,7},{1... | collective-permute-start | bytes 196616 | tf_op jit(solution)/shard_map/ppermute | solution.py:255
  49.4 1.9 %collective-permute-start.2 = (f32[128,128]{1,0:T(8,128)}, f32[128,128]{1,0:T(8,128)S(1)}, u32[]{:S(2)}, u32[]{:S(2)}) collective-permute-start(f32[128,128]{1,0:T(8,128)} %gather.1.own_ref), channel_id=1, source_target_pairs={{0,2},{1,3},{2,4},{3,5},{4,6},{5,7},{6,8},{7,9},{8,10},{9,11},{10,... | collective-permute-start | bytes 196616 | tf_op jit(solution)/shard_map/ppermute | solution.py:255
  51.3 0.8 slice.30
  52.1 0.0 collective-permute-done.3.plus_ref
  52.1 5.8 %collective-permute-done.2.minus_ref = f32[128,128]{1,0:T(8,128)S(1)} collective-permute-done((f32[128,128]{1,0:T(8,128)}, f32[128,128]{1,0:T(8,128)S(1)}, u32[]{:S(2)}, u32[]{:S(2)}) %collective-permute-start.2) | collective-permute-done | bytes 65568 | tf_op jit(solution)/shard_map/ppermute | solution.py:255
  57.9 3.7 %collective-permute-start.5 = (f32[192,128]{1,0:T(8,128)S(1)}, f32[192,128]{1,0:T(8,128)S(1)}, u32[]{:S(2)}, u32[]{:S(2)}) collective-permute-start(f32[192,128]{1,0:T(8,128)S(1)} %get-tuple-element.11), channel_id=1, source_target_pairs={{0,122},{1,123},{2,124},{3,125},{4,126},{5,127},{6,0},{7,1},{8,2},... | collective-permute-start | bytes 294920 | tf_op jit(solution)/shard_map/ppermute | solution.py:255
  61.7 3.5 %collective-permute-start.4 = (f32[192,128]{1,0:T(8,128)S(1)}, f32[192,128]{1,0:T(8,128)S(1)}, u32[]{:S(2)}, u32[]{:S(2)}) collective-permute-start(f32[192,128]{1,0:T(8,128)S(1)} %get-tuple-element.12), channel_id=1, source_target_pairs={{0,6},{1,7},{2,8},{3,9},{4,10},{5,11},{6,12},{7,13},{8,14},{9,15},... | collective-permute-start | bytes 294920 | tf_op jit(solution)/shard_map/ppermute | solution.py:255
  65.2 0.1 pad_add_fusion.place_ref
  65.3 0.3 collective-permute-done.5.up_ref
  65.6 10.5 %collective-permute-done.4.down_ref = f32[192,128]{1,0:T(8,128)S(1)} collective-permute-done((f32[192,128]{1,0:T(8,128)S(1)}, f32[192,128]{1,0:T(8,128)S(1)}, u32[]{:S(2)}, u32[]{:S(2)}) %collective-permute-start.4) | collective-permute-done | bytes 98336 | tf_op jit(solution)/shard_map/ppermute | solution.py:255
  76.2 0.0 all-to-all-done.1
  76.2 0.8 copy-done.1
  77.0 15.4 %update.1 = f32[80,8,512]{2,1,0:T(8,128)} custom-call(s32[3]{0:T(128)S(1)} %pad_add_fusion.place_ref, f32[128,128]{1,0:T(8,128)S(1)} %copy-done.1, f32[128,128]{1,0:T(8,128)S(1)} %collective-permute-done.2.minus_ref, f32[128,128]{1,0:T(8,128)S(1)} %collective-permute-done.3.plus_ref, f32[192,128]{1,0:T(8,128)S(1)} %collective-permute-done.4.down_ref, ...), custom_call_target="tpu_custom_call" | custom-call | tf_op jit(solution)/shard_map/update/pallas_call | solution.py:263
  (10 shorter events, 0.0 us)
Async XLA Ops:
  0.0 15.7 %copy-start = (f32[20,8,2048]{2,1,0:T(8,128)S(1)}, f32[20,8,2048]{2,1,0:T(8,128)}, u32[]{:S(2)}) copy-start(f32[20,8,2048]{2,1,0:T(8,128)} %tracer_ref.1) | copy-start | bytes 3932164
  0.0 15.7 %copy-start.4 = (s32[4,128]{1,0:T(4,128)S(1)}, s32[4,128]{1,0:T(4,128)}, u32[]{:S(2)}) copy-start(s32[4,128]{1,0:T(4,128)} %tally_ref.1) | copy-start | bytes 6148
  0.0 15.7 %copy-start.6 = (f32[4,16]{1,0:T(4,128)S(1)}, f32[4,16]{1,0:T(4,128)}, u32[]{:S(2)}) copy-start(f32[4,16]{1,0:T(4,128)} %variance_ref.1) | copy-start | bytes 772
  0.0 15.7 %copy-start.5 = (f32[4,16]{1,0:T(4,128)S(1)}, f32[4,16]{1,0:T(4,128)}, u32[]{:S(2)}) copy-start(f32[4,16]{1,0:T(4,128)} %reading_ref.1) | copy-start | bytes 772
  0.0 15.7 %copy-start.3 = (s32[4,16]{1,0:T(4,128)S(1)}, s32[4,16]{1,0:T(4,128)}, u32[]{:S(2)}) copy-start(s32[4,16]{1,0:T(4,128)} %site_vec_ref.1) | copy-start | bytes 772
  0.0 15.7 %copy-start.2 = (f32[8,2048]{1,0:T(8,128)S(1)}, f32[8,2048]{1,0:T(8,128)}, u32[]{:S(2)}) copy-start(f32[8,2048]{1,0:T(8,128)} %diffusion_ref.1) | copy-start | bytes 196612
  2.2 8.1 %collective-permute-start = (f32[20,2048]{1,0:T(8,128)S(1)}, f32[20,2048]{1,0:T(8,128)S(1)}, u32[]{:S(2)}, u32[]{:S(2)}) collective-permute-start(f32[20,2048]{1,0:T(8,128)S(1)} %bitcast.12), channel_id=1, source_target_pairs={{0,1},{1,2},{2,3},{3,4},{4,5},{5,6},{6,7},{7,8},{8,9},{9,10},{10,1... | collective-permute-start | bytes 491528 | tf_op jit(solution)/shard_map/ppermute | solution.py:224
  7.7 7.9 %collective-permute-start.1 = (f32[20,2048]{1,0:T(8,128)S(1)}, f32[20,2048]{1,0:T(8,128)S(1)}, u32[]{:S(2)}, u32[]{:S(2)}) collective-permute-start(f32[20,2048]{1,0:T(8,128)S(1)} %bitcast.13), channel_id=1, source_target_pairs={{1,0},{2,1},{3,2},{4,3},{5,4},{6,5},{7,6},{8,7},{9,8},{10,9},{11,1... | collective-permute-start | bytes 491528 | tf_op jit(solution)/shard_map/ppermute | solution.py:225
  30.9 45.2 %all-to-all-start.1 = ((f32[4,640,128]{2,1,0:T(8,128)}), f32[4,640,128]{2,1,0:T(8,128)S(1)}, u32[]{:S(2)}, u32[]{:S(2)}) async-start(f32[4,640,128]{2,1,0:T(8,128)} %bitcast.5), calls=%async_computation.1 | async-start | bytes 2621440 | tf_op jit(solution)/shard_map/all_to_all | solution.py:243
  36.8 15.3 %collective-permute-start.3 = (f32[128,128]{1,0:T(8,128)}, f32[128,128]{1,0:T(8,128)S(1)}, u32[]{:S(2)}, u32[]{:S(2)}) collective-permute-start(f32[128,128]{1,0:T(8,128)} %gather.1.own_ref), channel_id=1, source_target_pairs={{0,126},{1,127},{2,0},{3,1},{4,2},{5,3},{6,4},{7,5},{8,6},{9,7},{1... | collective-permute-start | bytes 196616 | tf_op jit(solution)/shard_map/ppermute | solution.py:255
  49.4 8.5 %collective-permute-start.2 = (f32[128,128]{1,0:T(8,128)}, f32[128,128]{1,0:T(8,128)S(1)}, u32[]{:S(2)}, u32[]{:S(2)}) collective-permute-start(f32[128,128]{1,0:T(8,128)} %gather.1.own_ref), channel_id=1, source_target_pairs={{0,2},{1,3},{2,4},{3,5},{4,6},{5,7},{6,8},{7,9},{8,10},{9,11},{10,... | collective-permute-start | bytes 196616 | tf_op jit(solution)/shard_map/ppermute | solution.py:255
  57.9 7.7 %collective-permute-start.5 = (f32[192,128]{1,0:T(8,128)S(1)}, f32[192,128]{1,0:T(8,128)S(1)}, u32[]{:S(2)}, u32[]{:S(2)}) collective-permute-start(f32[192,128]{1,0:T(8,128)S(1)} %get-tuple-element.11), channel_id=1, source_target_pairs={{0,122},{1,123},{2,124},{3,125},{4,126},{5,127},{6,0},{7,1},{8,2},... | collective-permute-start | bytes 294920 | tf_op jit(solution)/shard_map/ppermute | solution.py:255
  61.7 14.5 %collective-permute-start.4 = (f32[192,128]{1,0:T(8,128)S(1)}, f32[192,128]{1,0:T(8,128)S(1)}, u32[]{:S(2)}, u32[]{:S(2)}) collective-permute-start(f32[192,128]{1,0:T(8,128)S(1)} %get-tuple-element.12), channel_id=1, source_target_pairs={{0,6},{1,7},{2,8},{3,9},{4,10},{5,11},{6,12},{7,13},{8,14},{9,15},... | collective-permute-start | bytes 294920 | tf_op jit(solution)/shard_map/ppermute | solution.py:255
  76.2 0.8 copy-start.1

commit v2 on v1

v2 whole, which is shorter than its diff:
```python
import functools

import jax
import jax.numpy as jnp
from jax import lax
from jax.experimental import pallas as pl
from jax.experimental.pallas import tpu as pltpu
from jax.sharding import PartitionSpec as P

REACH = 2
RADIUS = 16
epsilon = 1e-05
LANES = 128
QUARTERS = 4
RING = 8
f32 = jnp.float32
bf16 = jnp.bfloat16

FACTS = 5
READING, VARIANCE, ROW, COLUMN, LIVE = range(FACTS)


def lane_of(shape):
    return lax.broadcasted_iota(jnp.int32, shape, len(shape) - 1)


def row_of(shape):
    return lax.broadcasted_iota(jnp.int32, shape, len(shape) - 2)


def halves(x):
    hi = x.astype(bf16).astype(f32)
    return hi, x - hi


def product(a, b, dims):
    a_hi, a_lo = [v.astype(bf16) for v in halves(a)]
    b_hi, b_lo = [v.astype(bf16) for v in halves(b)]
    dot = functools.partial(lax.dot_general, dimension_numbers=(dims, ((), ())), preferred_element_type=f32)
    return dot(a_hi, b_hi) + (dot(a_hi, b_lo) + dot(a_lo, b_hi))


def edges_kernel(tracer_ref, top_ref, bottom_ref):
    own, rows, _ = tracer_ref.shape
    for e in range(own):
        top_ref[e : e + 1, :] = tracer_ref[e, 0:1, :]
        bottom_ref[e : e + 1, :] = tracer_ref[e, rows - 1 : rows, :]


def step_kernel(
    region_ref, site_ref, tally_ref, tracer_ref, diffusion_ref, site_vec_ref, reading_ref, variance_ref,
    partial_ref, board_ref,
):
    own, rows, width = tracer_ref.shape
    batches, slots = site_ref.shape
    tiles = width // LANES // QUARTERS
    region = region_ref[0]
    diffusion = diffusion_ref[...]
    row = row_of((rows, width))
    for e in range(own):
        x = tracer_ref[e]
        lower = jnp.where(row == 0, 0.0, pltpu.roll(x, 1, 0))
        upper = jnp.where(row == rows - 1, 0.0, pltpu.roll(x, rows - 1, 0))
        east = pltpu.roll(x, width - 1, 1)
        west = pltpu.roll(x, 1, 1)
        y = x + diffusion * (upper + lower + east + west - 4.0 * x)
        for q in range(QUARTERS):
            for t in range(tiles):
                at = ((q * own + e) * tiles + t) * rows
                col = (q * tiles + t) * LANES
                partial_ref[at : at + rows, :] = y[:, col : col + LANES]
    board_ref[...] = jnp.zeros_like(board_ref)
    lane = lane_of((own, LANES))
    for b in range(batches):
        picked = jnp.zeros((own, LANES), f32)
        for k in range(slots):
            cell = site_ref[b, k]
            col = lax.rem(cell, width)
            tile = lax.div(col, LANES)
            start = lax.div(tile, tiles) * (own * tiles * rows) + lax.rem(tile, tiles) * rows + lax.div(cell, width)
            line = partial_ref[pl.ds(start, own, stride=tiles * rows), :]
            shift = lax.rem(k - lax.rem(col, LANES) + LANES, LANES)
            picked = jnp.where(lane == k, pltpu.roll(line, shift, 1), picked)
        at = b * 32
        board_ref[at : at + own, :] = picked
        cells = site_vec_ref[b : b + 1, :]
        count = tally_ref[b, region]
        facts = [
            reading_ref[b : b + 1, :],
            variance_ref[b : b + 1, :],
            (region * rows + lax.div(cells, width)).astype(f32),
            lax.rem(cells, width).astype(f32),
            jnp.where(lane_of((1, slots)) < count, 1.0, 0.0),
        ]
        for i, fact in enumerate(facts):
            board_ref[at + own + i : at + own + i + 1, 0:slots] = fact


def parcel_kernel(site_ref, board_ref, above_ref, below_ref, diffusion_ref, parcel_ref, halo, board):
    own, width = above_ref.shape
    batches, slots = site_ref.shape
    rows = diffusion_ref.shape[0]
    tiles = width // LANES
    for t in range(tiles):
        cols = slice(t * LANES, (t + 1) * LANES)
        halo[t * 24 : t * 24 + own, :] = above_ref[:, cols] * diffusion_ref[0:1, cols]
        halo[(tiles + t) * 24 : (tiles + t) * 24 + own, :] = below_ref[:, cols] * diffusion_ref[rows - 1 : rows, cols]
    halo[2 * tiles * 24 : 2 * tiles * 24 + 24, :] = jnp.zeros((24, LANES), f32)
    lane = lane_of((24, LANES))
    for b in range(batches):
        picked = jnp.zeros((24, LANES), f32)
        for k in range(slots):
            cell = site_ref[b, k]
            col = lax.rem(cell, width)
            row = lax.div(cell, width)
            tile = lax.div(col, LANES)
            block = jnp.where(row == 0, tile, jnp.where(row == rows - 1, tiles + tile, 2 * tiles))
            line = halo[pl.ds(pl.multiple_of(block * 24, 8), 24), :]
            shift = lax.rem(k - lax.rem(col, LANES) + LANES, LANES)
            picked = jnp.where(lane == k, pltpu.roll(line, shift, 1), picked)
        picked = jnp.where(row_of((24, LANES)) < own, picked, 0.0)
        board[b * 32 : b * 32 + 24, :] = board_ref[b * 32 : b * 32 + 24, :] + picked
        board[b * 32 + 24 : b * 32 + 32, :] = board_ref[b * 32 + 24 : b * 32 + 32, :]
    parcel = board[...].T[:slots, :]
    for i in range(parcel_ref.shape[0]):
        parcel_ref[i] = parcel


def finish_kernel(place_ref, partial_ref, above_ref, below_ref, diffusion_ref, stay_ref, near_ref, cross_ref):
    own = above_ref.shape[0]
    rows = diffusion_ref.shape[0]
    tiles = above_ref.shape[1] // LANES // QUARTERS
    size = own * tiles * rows
    row = row_of((rows, LANES))
    for i, (out_ref, base) in enumerate(((stay_ref, 0), (near_ref, 0), (cross_ref, 0), (cross_ref, size))):
        quarter = jnp.bitwise_xor(place_ref[1], i)
        for t in range(tiles):
            cols = pl.ds(pl.multiple_of((quarter * tiles + t) * LANES, LANES), LANES)
            diffusion = diffusion_ref[:, cols]
            first = jnp.where(row == 0, diffusion, 0.0)
            last = jnp.where(row == rows - 1, diffusion, 0.0)
            for e in range(own):
                at = (e * tiles + t) * rows
                part = partial_ref[pl.ds(pl.multiple_of(quarter * size + at, 8), rows), :]
                part = part + first * above_ref[e : e + 1, cols] + last * below_ref[e : e + 1, cols]
                out_ref[base + at : base + at + rows, :] = part


def pack_kernel(place_ref, plane_ref, other_ref, out_ref):
    count, slots, _ = plane_ref.shape
    y = place_ref[3]

    def parcel(o):
        at = y + o
        inside = (at >= 0) & (at < count)
        at = lax.rem(at + count, count)
        return jnp.where(inside, plane_ref[at], other_ref[at])

    lane = lane_of((slots, LANES))
    groups = [parcel(o) for o in (-1, 0, 1)]
    groups.append(jnp.where(lane < 96, parcel(-2), pltpu.roll(parcel(-4), 96, 1)))
    groups.append(jnp.where(lane < 96, parcel(2), pltpu.roll(parcel(4), 96, 1)))
    groups.append(jnp.where(lane < 64, parcel(-3), pltpu.roll(parcel(3), 64, 1)))
    for i in range(out_ref.shape[0]):
        for g, group in enumerate(groups):
            out_ref[i, g * slots : (g + 1) * slots, :] = group


def packed_at(offset, batch):
    if abs(offset) <= 1:
        return offset + 1, batch
    if abs(offset) == 3:
        return 5, batch + (2 if offset > 0 else 0)
    return (3 if offset < 0 else 4), (batch if abs(offset) == 2 else 3)


def beside(hi, lo):
    lane = lane_of(hi.shape)
    again = pltpu.roll(hi, 80, 1)
    last = pltpu.roll(lo, 32, 1)
    first = jnp.where(lane < 80, hi, again)
    second = jnp.where(lane < 32, again, last)
    return jnp.concatenate([first.astype(bf16), second.astype(bf16)], axis=1)


def below_each_other(x):
    hi, lo = halves(x)
    hi, lo = hi.astype(bf16), lo.astype(bf16)
    return jnp.concatenate([hi, lo, hi, jnp.zeros((16, x.shape[1]), bf16)], axis=0)


def update_kernel(
    place_ref, parcels_ref, state0_ref, state1_ref, state2_ref, state3_ref,
    out_ref, obs, inc_ref, ano_ref, gain_lhs, inc_lhs, near_ref, board, state_ref, updated, *, width,
):
    members = 80
    parity = place_ref[0]
    quarter = place_ref[1]
    region = place_ref[2]
    rows, quarter_width = out_ref.shape[1:]
    tiles = quarter_width // LANES
    scale = 1.0 / (RADIUS * RADIUS)
    own = members // QUARTERS
    slots = parcels_ref.shape[1] // 6
    lane = lane_of((slots, LANES))
    blocks = [(o, b) for b in range(4) for o in range(b - 4, 5 - b)]
    for i, (o, b) in enumerate(blocks):
        group, block = packed_at(o, b)
        for p in range(2):
            total = jnp.zeros((slots, LANES), f32)
            for m in range(QUARTERS):
                piece = parcels_ref[p * QUARTERS + m, group * slots : (group + 1) * slots, :]
                moved = pltpu.roll(piece, (own * m - 32 * block) % LANES, 1)
                end = own * (m + 1) + (FACTS if m == QUARTERS - 1 else 0)
                total = jnp.where((lane >= own * m) & (lane < end), moved, total)
            obs[(2 * i + p) * slots : (2 * i + p + 1) * slots, :] = total
    for i, ref in enumerate((state0_ref, state1_ref, state2_ref, state3_ref)):
        size = state0_ref.shape[0]
        at = pl.multiple_of(jnp.bitwise_xor(quarter, i) * size, 8)
        state_ref[pl.ds(at, size), :] = ref[0:size, :]
    starts = [0, 288, 512, 672, 768]
    centres = [96, 64, 32, 0]
    total = starts[-1]
    pick = jnp.where(lane_of((8, LANES)) == members + ROW + row_of((8, LANES)), 1.0, 0.0)
    across = lax.dot_general(
        pick, obs[...], (((1,), (1,)), ((), ())), precision=lax.Precision.HIGHEST, preferred_element_type=f32
    )
    for b in range(4):
        n = starts[b + 1] - starts[b]
        x = obs[starts[b] : starts[b + 1], :]
        member = lane_of((n, LANES)) < members
        fact = lambda i: x[:, members + i : members + i + 1]
        average = jnp.sum(jnp.where(member, x, 0.0), axis=1, keepdims=True) / members
        anomaly = jnp.where(member, x - average, 0.0)
        spread = jnp.sum(anomaly * anomaly, axis=1, keepdims=True) / (members - 1) + epsilon
        live = fact(LIVE)
        noise = jnp.where(live > 0.5, fact(VARIANCE), 1.0)
        posterior = 1.0 / (1.0 / spread + 1.0 / noise)
        post_mean = posterior * (average / spread + fact(READING) / noise)
        increment = post_mean - average + (jnp.sqrt(posterior / spread) - 1.0) * anomaly
        increment = jnp.where(member, increment, 0.0)
        scaled = anomaly * (live / ((members - 1) * spread))
        inc_ref[0:n, :] = increment
        ano_ref[0:n, :] = scaled
        at = centres[b] + 16 * parity
        gain_lhs[b] = beside(*halves(ano_ref[pl.ds(at, 80), :]))
        near_ref[b] = obs[pl.ds(starts[b] + at, 80), :]
        board[...] = jnp.zeros_like(board)
        board[0:80, :] = inc_ref[pl.ds(at, 80), :]
        inc_lhs[b] = beside(*halves(board[...].T[0:80, :]))
        if b < 3:
            y = obs[starts[b + 1] : total, :]
            m = total - starts[b + 1]
            inside = lane_of((m, LANES)) < members
            mean = jnp.sum(jnp.where(inside, y, 0.0), axis=1, keepdims=True) / members
            off = jnp.where(inside, y - mean, 0.0)
            covariance = product(off, scaled, ((1,), (1,)))
            row_gap = y[:, members + ROW : members + ROW + 1] - across[0:1, starts[b] : starts[b + 1]]
            col_gap = jnp.abs(y[:, members + COLUMN : members + COLUMN + 1] - across[1:2, starts[b] : starts[b + 1]])
            col_gap = jnp.minimum(col_gap, width - col_gap)
            remain = jnp.maximum(1.0 - (row_gap * row_gap + col_gap * col_gap) * scale, 0.0)
            weights = remain * remain * covariance
            obs[starts[b + 1] : total, :] = y + product(weights, increment, ((1,), (0,)))
    cols = (lane_of((80, quarter_width)) + quarter * quarter_width).astype(f32)
    closeness = []
    for b in range(4):
        gap = jnp.abs(cols - near_ref[b, :, members + COLUMN : members + COLUMN + 1])
        gap = jnp.minimum(gap, width - gap)
        closeness.append(1.0 - gap * gap * scale)
    together = 4

    def load(first):
        lines = [(r, t) for r in range(first, first + together) for t in range(tiles)]
        return jnp.concatenate([state_ref[pl.ds(t * rows + r, members, stride=tiles * rows), :] for r, t in lines], axis=1)

    def assimilate(state, b, first):
        mean = jnp.mean(state, axis=0, keepdims=True)
        covariance = jnp.dot(gain_lhs[b], below_each_other(state - mean), preferred_element_type=f32)
        tapers = []
        for r in range(first, first + together):
            gap = (region * rows + r).astype(f32) - near_ref[b, :, members + ROW : members + ROW + 1]
            remain = jnp.maximum(closeness[b] - gap * gap * scale, 0.0)
            tapers.append(remain * remain)
        weights = jnp.concatenate(tapers, axis=1) * covariance
        return state + jnp.dot(inc_lhs[b], below_each_other(weights), preferred_element_type=f32)

    for first in range(0, rows, together):
        state = load(first)
        for b in range(4):
            state = assimilate(state, b, first)
        for i in range(together * tiles):
            at = (i % tiles) * rows + first + i // tiles
            updated[pl.ds(at, members, stride=tiles * rows), :] = state[:, i * LANES : (i + 1) * LANES]
    for e in range(members):
        for t in range(tiles):
            at = (e * tiles + t) * rows
            out_ref[e, :, t * LANES : (t + 1) * LANES] = updated[at : at + rows, :]


def local(tracer, diffusion, sites, readings, variances, tally):
    own, rows, width = tracer.shape
    regions = lax.axis_size("region")
    batches, slots = sites.shape
    quarter_width = width // QUARTERS
    members = own * QUARTERS
    region = lax.axis_index("region")
    quarter = lax.axis_index("member")
    vmem = pl.BlockSpec(memory_space=pltpu.VMEM)
    smem = pl.BlockSpec(memory_space=pltpu.SMEM)
    limit = pltpu.CompilerParams(vmem_limit_bytes=32 * 1024 * 1024)
    line = jax.ShapeDtypeStruct((own, width), f32)
    place = jnp.stack([region % 2, quarter, region, region // 2 % RING]).astype(jnp.int32)
    top, bottom = pl.pallas_call(
        edges_kernel, out_shape=(line, line), in_specs=[vmem], out_specs=(vmem, vmem), compiler_params=limit, name="edges"
    )(tracer)
    above = lax.ppermute(bottom, "region", [(i, i + 1) for i in range(regions - 1)])
    below = lax.ppermute(top, "region", [(i + 1, i) for i in range(regions - 1)])
    partial, board = pl.pallas_call(
        step_kernel,
        out_shape=(
            jax.ShapeDtypeStruct((own * rows * width // LANES, LANES), f32),
            jax.ShapeDtypeStruct((LANES, LANES), f32),
        ),
        in_specs=[smem] * 3 + [vmem] * 5,
        out_specs=(vmem, vmem),
        compiler_params=limit,
        cost_estimate=pl.CostEstimate(flops=20_000_000, bytes_accessed=10_000_000, transcendentals=0),
        name="step",
    )(region[None].astype(jnp.int32), sites, tally, tracer, diffusion, sites, readings, variances)
    parcel = pl.pallas_call(
        parcel_kernel,
        out_shape=jax.ShapeDtypeStruct((RING, slots, LANES), f32),
        in_specs=[smem] + [vmem] * 4,
        out_specs=vmem,
        scratch_shapes=[pltpu.VMEM(((2 * width // LANES + 1) * 24, LANES), f32), pltpu.VMEM((LANES, LANES), f32)],
        compiler_params=limit,
        name="parcel",
    )(sites, board, above, below, diffusion)
    planes = regions // 2 // RING
    rings = [[(z * RING + y) * 2 + p for y in range(RING)] for z in range(planes) for p in range(2)]
    plane = lax.all_to_all(parcel, "region", 0, 0, axis_index_groups=rings)
    size = own * rows * quarter_width // LANES
    stay, near, cross = pl.pallas_call(
        finish_kernel,
        out_shape=[jax.ShapeDtypeStruct((n * size, LANES), f32) for n in (1, 1, 2)],
        in_specs=[smem] + [vmem] * 4,
        out_specs=[vmem] * 3,
        compiler_params=limit,
        cost_estimate=pl.CostEstimate(flops=2_000_000, bytes_accessed=4_000_000, transcendentals=0),
        name="finish",
    )(place, partial, above, below, diffusion)
    crossed = lax.ppermute(cross, "member", [(m, m ^ 2) for m in range(QUARTERS)])
    plane, _ = lax.optimization_barrier((plane, stay))
    to_core = [(m, m ^ 1) for m in range(QUARTERS)]
    states = [stay, lax.ppermute(near, "member", to_core), crossed, lax.ppermute(crossed[size:], "member", to_core)]
    swap = []
    for z in range(planes):
        for y in range(RING):
            to = z + (1 if y >= RING // 2 else -1)
            if 0 <= to < planes:
                swap += [((z * RING + y) * 2 + p, (to * RING + RING - 1 - y) * 2 + p) for p in range(2)]
    other = lax.ppermute(plane, "region", swap)
    packed = pl.pallas_call(
        pack_kernel,
        out_shape=jax.ShapeDtypeStruct((2 * QUARTERS, 6 * slots, LANES), f32),
        in_specs=[smem] + [vmem] * 2,
        out_specs=vmem,
        compiler_params=limit,
        name="pack",
    )(place, plane, other)
    packed, _ = lax.optimization_barrier((packed, crossed))
    lines = [[2 * QUARTERS * g + i for i in range(2 * QUARTERS)] for g in range(regions // 2)]
    parcels = lax.all_to_all(packed, ("region", "member"), 0, 0, axis_index_groups=lines)
    block = 2 * slots
    total = 24 * block
    return pl.pallas_call(
        functools.partial(update_kernel, width=width),
        out_shape=jax.ShapeDtypeStruct((members, rows, quarter_width), f32),
        in_specs=[smem] + [vmem] * 5,
        out_specs=vmem,
        scratch_shapes=[
            pltpu.VMEM((total, LANES), f32),
            pltpu.VMEM((9 * block, LANES), f32),
            pltpu.VMEM((9 * block, LANES), f32),
            pltpu.VMEM((4, 80, 256), bf16),
            pltpu.VMEM((4, 80, 256), bf16),
            pltpu.VMEM((4, 80, LANES), f32),
            pltpu.VMEM((LANES, LANES), f32),
            pltpu.VMEM((members * rows * quarter_width // LANES, LANES), f32),
            pltpu.VMEM((members * rows * quarter_width // LANES, LANES), f32),
        ],
        compiler_params=limit,
        name="update",
    )(place, parcels, *states)


def solution(mesh):
    placed = (
        P("member", "region", None),
        P("region", None),
        P(None, "region"),
        P(None, "region"),
        P(None, "region"),
        P(),
    )
    return jax.shard_map(
        local, mesh=mesh, in_specs=placed, out_specs=P(None, "region", "member"), check_vma=False
    )
```

time: 92.9 us -> 74 us (0.80)
  the two profiles are of different devices: /device:TPU:1 before, /device:TPU:200 now
where the time goes in v2:
time: 74 us; the launch traced here: 73.6 us
  starting transfers between devices  23.2 us (31%)
  waiting for transfers between devices  16.9 us (23%)
  Pallas kernels  16.4 us (22%)
  blocking collectives  15.5 us (21%)
  local copies, waits for them, and re-layouts  1.36 us (2%)
    all_to_all x1, blocking collectives, local(): plane = lax.all_to_all(parcel, 'region', 0, 0, axis_index_groups=rings)  15.5 us
    pallas_call x1, Pallas kernels, local(): pl.pallas_call(functools.partial(update_kernel, width=width), out_shape=j...  10.8 us
    ppermute x1, waiting for transfers between devices, local(): other = lax.ppermute(plane, 'region', swap)  7.74 us
    ppermute x1, starting transfers between devices, local(): lax.ppermute(bottom, 'region', [(i, i + 1) for i in range(regions - 1)])  5.06 us
    all_to_all x1, starting transfers between devices, local(): lax.all_to_all(packed, ('region', 'member'), 0, 0, axis_index_groups=lines)  4.81 us
    ppermute x1, waiting for transfers between devices, local(): lax.ppermute(top, 'region', [(i + 1, i) for i in range(regions - 1)])  4.17 us
    ppermute x1, starting transfers between devices, local(): lax.ppermute(cross, 'member', [(m, m ^ 2) for m in range(QUARTERS)])  3.4 us
    ppermute x1, starting transfers between devices, local(): lax.ppermute(top, 'region', [(i + 1, i) for i in range(regions - 1)])  3.31 us
  transfers between devices with their start and end apart: 7, of which 5 were waited for; matrix products, arithmetic and copies ran while one was open for 0% of the time, Pallas kernels for 6%

profile of v2, /device:TPU:200, one launch (start us, length us, event | category | flops | bytes accessed | tf_op | source)
XLA Modules:
  0.0 73.6 jit_solution(234076253216724576)
XLA Ops:
  0.0 0.0 copy-start
  0.0 1.3 %copy-done = f32[20,8,2048]{2,1,0:T(8,128)S(1)} copy-done((f32[20,8,2048]{2,1,0:T(8,128)S(1)}, f32[20,8,2048]{2,1,0:T(8,128)}, u32[]{:S(2)}) %copy-start) | copy-done | bytes 1310744
  1.3 0.0 copy-start.5
  1.3 0.0 copy-start.6
  1.3 0.1 edges.1
  1.4 5.1 %collective-permute-start = (f32[20,2048]{1,0:T(8,128)S(1)}, f32[20,2048]{1,0:T(8,128)S(1)}, u32[]{:S(2)}, u32[]{:S(2)}) collective-permute-start(f32[20,2048]{1,0:T(8,128)S(1)} %get-tuple-element.15), channel_id=1, source_target_pairs={{0,1},{1,2},{2,3},{3,4},{4,5},{5,6},{6,7},{7,8},{8,9},{9,10},{10,1... | collective-permute-start | bytes 491528 | tf_op jit(solution)/shard_map/ppermute | solution.py:316
  6.5 3.3 %collective-permute-start.1 = (f32[20,2048]{1,0:T(8,128)S(1)}, f32[20,2048]{1,0:T(8,128)S(1)}, u32[]{:S(2)}, u32[]{:S(2)}) collective-permute-start(f32[20,2048]{1,0:T(8,128)S(1)} %get-tuple-element.16), channel_id=1, source_target_pairs={{1,0},{2,1},{3,2},{4,3},{5,4},{6,5},{7,6},{8,7},{9,8},{10,9},{11,1... | collective-permute-start | bytes 491528 | tf_op jit(solution)/shard_map/ppermute | solution.py:317
  9.9 0.0 copy-done.1
  9.9 0.0 copy-done.2
  9.9 0.0 copy-done.3
  9.9 0.0 copy-done.4
  9.9 0.0 copy-done.5
  9.9 0.0 copy-done.6
  9.9 2.2 %step.1 = (f32[2560,128]{1,0:T(8,128)S(1)}, f32[128,128]{1,0:T(8,128)S(1)}) custom-call(s32[1]{0:T(128)} %bitcast.2.region_ref, s32[4,16]{1,0:T(4,128)S(1)} %copy-done.3, s32[4,128]{1,0:T(4,128)S(1)} %copy-done.4, f32[20,8,2048]{2,1,0:T(8,128)S(1)} %copy-done.1, f32[8,2048]{1,0:T(8,128)S(1)} %copy-done.2, s32[4,16]{1,0:T(4,128)S(1)} %copy-done.3, ...), custom_call_target="tpu_custom_call" | custom-call | flops 20000000 | bytes 10000000 | tf_op jit(solution)/shard_map/step/pallas_call | solution.py:318
  12.1 0.1 pad_add_fusion.place_ref
  12.2 0.4 collective-permute-done.above_ref
  12.6 4.2 %collective-permute-done.1.below_ref = f32[20,2048]{1,0:T(8,128)S(1)} collective-permute-done((f32[20,2048]{1,0:T(8,128)S(1)}, f32[20,2048]{1,0:T(8,128)S(1)}, u32[]{:S(2)}, u32[]{:S(2)}) %collective-permute-start.1) | collective-permute-done | bytes 163872 | tf_op jit(solution)/shard_map/ppermute | solution.py:317
  16.7 0.8 %finish.1 = (f32[640,128]{1,0:T(8,128)S(1)}, f32[640,128]{1,0:T(8,128)S(1)}, f32[1280,128]{1,0:T(8,128)S(1)}) custom-call(s32[4]{0:T(128)S(1)} %pad_add_fusion.place_ref, f32[2560,128]{1,0:T(8,128)S(1)} %get-tuple-element.17.partial_ref, f32[20,2048]{1,0:T(8,128)S(1)} %collective-permute-done.above_ref, f32[20,2048]{1,0:T(8,128)S(1)} %collective-permute-done.1.below_ref, ...), custom_call_target="tpu_custom_call" | custom-call | flops 2000000 | bytes 4000000 | tf_op jit(solution)/shard_map/finish/pallas_call | solution.py:343
  17.5 3.4 %collective-permute-start.3 = (f32[1280,128]{1,0:T(8,128)S(1)}, f32[1280,128]{1,0:T(8,128)S(1)}, u32[]{:S(2)}, u32[]{:S(2)}) collective-permute-start(f32[1280,128]{1,0:T(8,128)S(1)} %get-tuple-element.20), channel_id=1, source_target_pairs={{0,256},{128,384},{256,0},{384,128},{1,257},{129,385},{257,1},{385... | collective-permute-start | bytes 1966088 | tf_op jit(solution)/shard_map/ppermute | solution.py:352
  20.9 1.2 %parcel.1 = f32[8,16,128]{2,1,0:T(8,128)S(1)} custom-call(s32[4,16]{1,0:T(4,128)S(1)} %copy-done.3, f32[128,128]{1,0:T(8,128)S(1)} %get-tuple-element.14.board_ref, f32[20,2048]{1,0:T(8,128)S(1)} %collective-permute-done.above_ref, f32[20,2048]{1,0:T(8,128)S(1)} %collective-permute-done.1.below_ref, f32[8,2048]{1,0:T(8,128)S(1)} %copy-done.2), custom_call_target="tpu_custom_call" | custom-call | tf_op jit(solution)/shard_map/parcel/pallas_call | solution.py:330
  22.1 15.5 %all_to_all.10.plane_ref = f32[8,16,128]{2,1,0:T(8,128)S(1)} all-to-all(f32[8,16,128]{2,1,0:T(8,128)S(1)} %parcel.1), channel_id=1, replica_groups={{0,2,4,6,8,10,12,14},{1,3,5,7,9,11,13,15},{16,18,20,22,24,26,28,30},{17..., dimensions={0} | all-to-all | bytes 131072 | tf_op jit(solution)/shard_map/all_to_all | solution.py:341
  37.6 2.3 %collective-permute-start.2 = (f32[8,16,128]{2,1,0:T(8,128)S(1)}, f32[8,16,128]{2,1,0:T(8,128)S(1)}, u32[]{:S(2)}, u32[]{:S(2)}) collective-permute-start(f32[8,16,128]{2,1,0:T(8,128)S(1)} %all_to_all.10.plane_ref), channel_id=1, source_target_pairs={{8,22},{9,23},{10,20},{11,21},{12,18},{13,19},{14,16},{15,17},{16,... | collective-permute-start | bytes 196616 | tf_op jit(solution)/shard_map/ppermute | solution.py:362
  39.9 7.7 %collective-permute-done.2.other_ref = f32[8,16,128]{2,1,0:T(8,128)S(1)} collective-permute-done((f32[8,16,128]{2,1,0:T(8,128)S(1)}, f32[8,16,128]{2,1,0:T(8,128)S(1)}, u32[]{:S(2)}, u32[]{:S(2)}) %collective-permute-start.2) | collective-permute-done | bytes 65568 | tf_op jit(solution)/shard_map/ppermute | solution.py:362
  47.6 1.4 %pack.1 = f32[8,96,128]{2,1,0:T(8,128)} custom-call(s32[4]{0:T(128)S(1)} %pad_add_fusion.place_ref, f32[8,16,128]{2,1,0:T(8,128)S(1)} %all_to_all.10.plane_ref, f32[8,16,128]{2,1,0:T(8,128)S(1)} %collective-permute-done.2.other_ref), custom_call_target="tpu_custom_call" | custom-call | tf_op jit(solution)/shard_map/pack/pallas_call | solution.py:363
  49.0 0.0 collective-permute-done.3.state2_ref
  49.0 4.8 %all-to-all-start.1 = ((f32[8,96,128]{2,1,0:T(8,128)}), f32[8,96,128]{2,1,0:T(8,128)S(1)}, u32[]{:S(2)}, u32[]{:S(2)}) async-start(f32[8,96,128]{2,1,0:T(8,128)} %pack.1), calls=%async_computation.1 | async-start | bytes 786432 | tf_op jit(solution)/shard_map/all_to_all | solution.py:373
  53.8 2.4 %collective-permute-start.4 = (f32[640,128]{1,0:T(8,128)S(1)}, f32[640,128]{1,0:T(8,128)S(1)}, u32[]{:S(2)}, u32[]{:S(2)}) collective-permute-start(f32[640,128]{1,0:T(8,128)S(1)} %get-tuple-element.22), channel_id=1, source_target_pairs={{0,128},{128,0},{256,384},{384,256},{1,129},{129,1},{257,385},{385... | collective-permute-start | bytes 983048 | tf_op jit(solution)/shard_map/ppermute | solution.py:355
  56.3 1.9 %collective-permute-start.5 = (f32[640,128]{1,0:T(8,128)S(1)}, f32[640,128]{1,0:T(8,128)S(1)}, u32[]{:S(2)}, u32[]{:S(2)}) collective-permute-start(f32[640,128]{1,0:T(8,128)S(1)} %slice.4), channel_id=1, source_target_pairs={{0,128},{128,0},{256,384},{384,256},{1,129},{129,1},{257,385},{385... | collective-permute-start | bytes 983048 | tf_op jit(solution)/shard_map/ppermute | solution.py:355
  58.2 0.0 collective-permute-done.4.state1_ref
  58.2 1.6 %collective-permute-done.5.state3_ref = f32[640,128]{1,0:T(8,128)S(1)} collective-permute-done((f32[640,128]{1,0:T(8,128)S(1)}, f32[640,128]{1,0:T(8,128)S(1)}, u32[]{:S(2)}, u32[]{:S(2)}) %collective-permute-start.5) | collective-permute-done | bytes 327712 | tf_op jit(solution)/shard_map/ppermute | solution.py:355
  59.8 3.0 %all-to-all-done.1.parcels_ref = f32[8,96,128]{2,1,0:T(8,128)S(1)} async-done(((f32[8,96,128]{2,1,0:T(8,128)}), f32[8,96,128]{2,1,0:T(8,128)S(1)}, u32[]{:S(2)}, u32[]{:S(2)}) %all-to-all-start.1) | async-done | bytes 393248 | tf_op jit(solution)/shard_map/all_to_all | solution.py:373
  62.8 10.8 %update.1 = f32[80,8,512]{2,1,0:T(8,128)} custom-call(s32[4]{0:T(128)S(1)} %pad_add_fusion.place_ref, f32[8,96,128]{2,1,0:T(8,128)S(1)} %all-to-all-done.1.parcels_ref, f32[640,128]{1,0:T(8,128)S(1)} %get-tuple-element.18.state0_ref, f32[640,128]{1,0:T(8,128)S(1)} %collective-permute-done.4.state1_ref, f32[1280,128]{1,0:T(8,128)S(1)} %collective-permute-done.3.state2_ref, ...), custom_call_target="tpu_custom_call" | custom-call | tf_op jit(solution)/shard_map/update/pallas_call | solution.py:376
  (5 shorter events, 0.0 us)
Async XLA Ops:
  0.0 1.3 %copy-start = (f32[20,8,2048]{2,1,0:T(8,128)S(1)}, f32[20,8,2048]{2,1,0:T(8,128)}, u32[]{:S(2)}) copy-start(f32[20,8,2048]{2,1,0:T(8,128)} %tracer_ref.3) | copy-start | bytes 3932164
  1.3 8.6 %copy-start.1 = (f32[20,8,2048]{2,1,0:T(8,128)S(1)}, f32[20,8,2048]{2,1,0:T(8,128)}, u32[]{:S(2)}) copy-start(f32[20,8,2048]{2,1,0:T(8,128)} %tracer_ref.3) | copy-start | bytes 3932164
  1.3 8.6 %copy-start.2 = (f32[8,2048]{1,0:T(8,128)S(1)}, f32[8,2048]{1,0:T(8,128)}, u32[]{:S(2)}) copy-start(f32[8,2048]{1,0:T(8,128)} %diffusion_ref.5) | copy-start | bytes 196612
  1.3 8.6 %copy-start.3 = (s32[4,16]{1,0:T(4,128)S(1)}, s32[4,16]{1,0:T(4,128)}, u32[]{:S(2)}) copy-start(s32[4,16]{1,0:T(4,128)} %site_ref.3) | copy-start | bytes 772
  1.3 8.6 %copy-start.4 = (s32[4,128]{1,0:T(4,128)S(1)}, s32[4,128]{1,0:T(4,128)}, u32[]{:S(2)}) copy-start(s32[4,128]{1,0:T(4,128)} %tally_ref.1) | copy-start | bytes 6148
  1.3 8.6 %copy-start.5 = (f32[4,16]{1,0:T(4,128)S(1)}, f32[4,16]{1,0:T(4,128)}, u32[]{:S(2)}) copy-start(f32[4,16]{1,0:T(4,128)} %reading_ref.1) | copy-start | bytes 772
  1.3 8.6 %copy-start.6 = (f32[4,16]{1,0:T(4,128)S(1)}, f32[4,16]{1,0:T(4,128)}, u32[]{:S(2)}) copy-start(f32[4,16]{1,0:T(4,128)} %variance_ref.1) | copy-start | bytes 772
  1.4 11.1 %collective-permute-start = (f32[20,2048]{1,0:T(8,128)S(1)}, f32[20,2048]{1,0:T(8,128)S(1)}, u32[]{:S(2)}, u32[]{:S(2)}) collective-permute-start(f32[20,2048]{1,0:T(8,128)S(1)} %get-tuple-element.15), channel_id=1, source_target_pairs={{0,1},{1,2},{2,3},{3,4},{4,5},{5,6},{6,7},{7,8},{8,9},{9,10},{10,1... | collective-permute-start | bytes 491528 | tf_op jit(solution)/shard_map/ppermute | solution.py:316
  6.5 10.2 %collective-permute-start.1 = (f32[20,2048]{1,0:T(8,128)S(1)}, f32[20,2048]{1,0:T(8,128)S(1)}, u32[]{:S(2)}, u32[]{:S(2)}) collective-permute-start(f32[20,2048]{1,0:T(8,128)S(1)} %get-tuple-element.16), channel_id=1, source_target_pairs={{1,0},{2,1},{3,2},{4,3},{5,4},{6,5},{7,6},{8,7},{9,8},{10,9},{11,1... | collective-permute-start | bytes 491528 | tf_op jit(solution)/shard_map/ppermute | solution.py:317
  17.5 31.5 %collective-permute-start.3 = (f32[1280,128]{1,0:T(8,128)S(1)}, f32[1280,128]{1,0:T(8,128)S(1)}, u32[]{:S(2)}, u32[]{:S(2)}) collective-permute-start(f32[1280,128]{1,0:T(8,128)S(1)} %get-tuple-element.20), channel_id=1, source_target_pairs={{0,256},{128,384},{256,0},{384,128},{1,257},{129,385},{257,1},{385... | collective-permute-start | bytes 1966088 | tf_op jit(solution)/shard_map/ppermute | solution.py:352
  37.6 10.1 %collective-permute-start.2 = (f32[8,16,128]{2,1,0:T(8,128)S(1)}, f32[8,16,128]{2,1,0:T(8,128)S(1)}, u32[]{:S(2)}, u32[]{:S(2)}) collective-permute-start(f32[8,16,128]{2,1,0:T(8,128)S(1)} %all_to_all.10.plane_ref), channel_id=1, source_target_pairs={{8,22},{9,23},{10,20},{11,21},{12,18},{13,19},{14,16},{15,17},{16,... | collective-permute-start | bytes 196616 | tf_op jit(solution)/shard_map/ppermute | solution.py:362
  49.0 13.8 %all-to-all-start.1 = ((f32[8,96,128]{2,1,0:T(8,128)}), f32[8,96,128]{2,1,0:T(8,128)S(1)}, u32[]{:S(2)}, u32[]{:S(2)}) async-start(f32[8,96,128]{2,1,0:T(8,128)} %pack.1), calls=%async_computation.1 | async-start | bytes 786432 | tf_op jit(solution)/shard_map/all_to_all | solution.py:373
  53.8 4.4 %collective-permute-start.4 = (f32[640,128]{1,0:T(8,128)S(1)}, f32[640,128]{1,0:T(8,128)S(1)}, u32[]{:S(2)}, u32[]{:S(2)}) collective-permute-start(f32[640,128]{1,0:T(8,128)S(1)} %get-tuple-element.22), channel_id=1, source_target_pairs={{0,128},{128,0},{256,384},{384,256},{1,129},{129,1},{257,385},{385... | collective-permute-start | bytes 983048 | tf_op jit(solution)/shard_map/ppermute | solution.py:355
  56.3 3.5 %collective-permute-start.5 = (f32[640,128]{1,0:T(8,128)S(1)}, f32[640,128]{1,0:T(8,128)S(1)}, u32[]{:S(2)}, u32[]{:S(2)}) collective-permute-start(f32[640,128]{1,0:T(8,128)S(1)} %slice.4), channel_id=1, source_target_pairs={{0,128},{128,0},{256,384},{384,256},{1,129},{129,1},{257,385},{385... | collective-permute-start | bytes 983048 | tf_op jit(solution)/shard_map/ppermute | solution.py:355

commit v3 on v2

--- a/solution.py
+++ b/solution.py
@@ -121,9 +121,14 @@
         picked = jnp.where(row_of((24, LANES)) < own, picked, 0.0)
         board[b * 32 : b * 32 + 24, :] = board_ref[b * 32 : b * 32 + 24, :] + picked
         board[b * 32 + 24 : b * 32 + 32, :] = board_ref[b * 32 + 24 : b * 32 + 32, :]
-    parcel = board[...].T[:slots, :]
-    for i in range(parcel_ref.shape[0]):
-        parcel_ref[i] = parcel
+    parcel_ref[...] = board[...].T[:slots, :]
+
+
+def repeat_kernel(own_ref, other_ref, out_ref):
+    slots = own_ref.shape[0]
+    for i in range(out_ref.shape[0]):
+        out_ref[i, 0:slots, :] = own_ref[...]
+        out_ref[i, slots : 2 * slots, :] = other_ref[...]
 
 
 def finish_kernel(place_ref, partial_ref, above_ref, below_ref, diffusion_ref, stay_ref, near_ref, cross_ref):
@@ -146,15 +151,16 @@
                 out_ref[base + at : base + at + rows, :] = part
 
 
-def pack_kernel(place_ref, plane_ref, other_ref, out_ref):
-    count, slots, _ = plane_ref.shape
+def pack_kernel(place_ref, plane_ref, out_ref):
+    count = plane_ref.shape[0]
+    slots = plane_ref.shape[1] // 2
     y = place_ref[3]
 
     def parcel(o):
         at = y + o
         inside = (at >= 0) & (at < count)
         at = lax.rem(at + count, count)
-        return jnp.where(inside, plane_ref[at], other_ref[at])
+        return jnp.where(inside, plane_ref[at, 0:slots], plane_ref[count - 1 - at, slots : 2 * slots])
 
     lane = lane_of((slots, LANES))
     groups = [parcel(o) for o in (-1, 0, 1)]
@@ -191,7 +197,7 @@
 
 def update_kernel(
     place_ref, parcels_ref, state0_ref, state1_ref, state2_ref, state3_ref,
-    out_ref, obs, inc_ref, ano_ref, gain_lhs, inc_lhs, near_ref, board, state_ref, updated, *, width,
+    out_ref, obs, inc_ref, ano_ref, gain_lhs, inc_lhs, near_ref, board, state_ref, updated, whole, centre_ref, sems, *, width,
 ):
     members = 80
     parity = place_ref[0]
@@ -221,23 +227,29 @@
     starts = [0, 288, 512, 672, 768]
     centres = [96, 64, 32, 0]
     total = starts[-1]
-    pick = jnp.where(lane_of((8, LANES)) == members + ROW + row_of((8, LANES)), 1.0, 0.0)
-    across = lax.dot_general(
-        pick, obs[...], (((1,), (1,)), ((), ())), precision=lax.Precision.HIGHEST, preferred_element_type=f32
+    pick = jnp.where(lane_of((8, LANES)) == members + ROW + row_of((8, LANES)), 1.0, 0.0).astype(bf16)
+    across = sum(
+        lax.dot_general(pick, half.astype(bf16), (((1,), (1,)), ((), ())), preferred_element_type=f32)
+        for half in halves(obs[...])
     )
+    everything = obs[...]
+    inside = lane_of(everything.shape) < members
+    centre = jnp.sum(jnp.where(inside, everything, 0.0), axis=1, keepdims=True) / members
+    centre_ref[...] = jnp.broadcast_to(centre, everything.shape)
+    obs[...] = jnp.where(inside, everything - centre, everything)
     for b in range(4):
         n = starts[b + 1] - starts[b]
         x = obs[starts[b] : starts[b + 1], :]
         member = lane_of((n, LANES)) < members
         fact = lambda i: x[:, members + i : members + i + 1]
-        average = jnp.sum(jnp.where(member, x, 0.0), axis=1, keepdims=True) / members
-        anomaly = jnp.where(member, x - average, 0.0)
+        shift = jnp.sum(jnp.where(member, x, 0.0), axis=1, keepdims=True) / members
+        anomaly = jnp.where(member, x - shift, 0.0)
+        average = centre_ref[starts[b] : starts[b + 1], 0:1] + shift
         spread = jnp.sum(anomaly * anomaly, axis=1, keepdims=True) / (members - 1) + epsilon
         live = fact(LIVE)
         noise = jnp.where(live > 0.5, fact(VARIANCE), 1.0)
-        posterior = 1.0 / (1.0 / spread + 1.0 / noise)
-        post_mean = posterior * (average / spread + fact(READING) / noise)
-        increment = post_mean - average + (jnp.sqrt(posterior / spread) - 1.0) * anomaly
+        share = 1.0 / (spread + noise)
+        increment = spread * share * (fact(READING) - average) + (jnp.sqrt(noise * share) - 1.0) * anomaly
         increment = jnp.where(member, increment, 0.0)
         scaled = anomaly * (live / ((members - 1) * spread))
         inc_ref[0:n, :] = increment
@@ -251,10 +263,7 @@
         if b < 3:
             y = obs[starts[b + 1] : total, :]
             m = total - starts[b + 1]
-            inside = lane_of((m, LANES)) < members
-            mean = jnp.sum(jnp.where(inside, y, 0.0), axis=1, keepdims=True) / members
-            off = jnp.where(inside, y - mean, 0.0)
-            covariance = product(off, scaled, ((1,), (1,)))
+            covariance = product(jnp.where(lane_of((m, LANES)) < members, y, 0.0), scaled, ((1,), (1,)))
             row_gap = y[:, members + ROW : members + ROW + 1] - across[0:1, starts[b] : starts[b + 1]]
             col_gap = jnp.abs(y[:, members + COLUMN : members + COLUMN + 1] - across[1:2, starts[b] : starts[b + 1]])
             col_gap = jnp.minimum(col_gap, width - col_gap)
@@ -267,34 +276,44 @@
         gap = jnp.abs(cols - near_ref[b, :, members + COLUMN : members + COLUMN + 1])
         gap = jnp.minimum(gap, width - gap)
         closeness.append(1.0 - gap * gap * scale)
-    together = 4
+    together = 2
 
     def load(first):
-        lines = [(r, t) for r in range(first, first + together) for t in range(tiles)]
+        lines = [(r, t) for t in range(first, first + together) for r in range(rows)]
         return jnp.concatenate([state_ref[pl.ds(t * rows + r, members, stride=tiles * rows), :] for r, t in lines], axis=1)
 
     def assimilate(state, b, first):
-        mean = jnp.mean(state, axis=0, keepdims=True)
-        covariance = jnp.dot(gain_lhs[b], below_each_other(state - mean), preferred_element_type=f32)
+        covariance = jnp.dot(gain_lhs[b], below_each_other(state), preferred_element_type=f32)
         tapers = []
-        for r in range(first, first + together):
-            gap = (region * rows + r).astype(f32) - near_ref[b, :, members + ROW : members + ROW + 1]
-            remain = jnp.maximum(closeness[b] - gap * gap * scale, 0.0)
-            tapers.append(remain * remain)
+        for t in range(first, first + together):
+            near = closeness[b][:, t * LANES : (t + 1) * LANES]
+            for r in range(rows):
+                gap = (region * rows + r).astype(f32) - near_ref[b, :, members + ROW : members + ROW + 1]
+                remain = jnp.maximum(near - gap * gap * scale, 0.0)
+                tapers.append(remain * remain)
         weights = jnp.concatenate(tapers, axis=1) * covariance
         return state + jnp.dot(inc_lhs[b], below_each_other(weights), preferred_element_type=f32)
 
-    for first in range(0, rows, together):
+    copies = []
+    for first in range(0, tiles, together):
         state = load(first)
+        centre = jnp.mean(state, axis=0, keepdims=True)
+        state = state - centre
         for b in range(4):
             state = assimilate(state, b, first)
-        for i in range(together * tiles):
-            at = (i % tiles) * rows + first + i // tiles
-            updated[pl.ds(at, members, stride=tiles * rows), :] = state[:, i * LANES : (i + 1) * LANES]
-    for e in range(members):
-        for t in range(tiles):
-            at = (e * tiles + t) * rows
-            out_ref[e, :, t * LANES : (t + 1) * LANES] = updated[at : at + rows, :]
+        state = state + centre
+        for i in range(together * rows):
+            t, r = first + i // rows, i % rows
+            updated[(t * rows + r) * members : (t * rows + r + 1) * members, :] = state[:, i * LANES : (i + 1) * LANES]
+        cols = slice(first * LANES, (first + together) * LANES)
+        for e in range(members):
+            for t in range(first, first + together):
+                line = updated[pl.ds(t * rows * members + e, rows, stride=members), :]
+                whole[e, :, t * LANES : (t + 1) * LANES] = line
+        copies.append(pltpu.make_async_copy(whole.at[:, :, cols], out_ref.at[:, :, cols], sems.at[first // together]))
+        copies[-1].start()
+    for copy in copies:
+        copy.wait()
 
 
 def local(tracer, diffusion, sites, readings, variances, tally):
@@ -329,16 +348,22 @@
     )(region[None].astype(jnp.int32), sites, tally, tracer, diffusion, sites, readings, variances)
     parcel = pl.pallas_call(
         parcel_kernel,
-        out_shape=jax.ShapeDtypeStruct((RING, slots, LANES), f32),
+        out_shape=jax.ShapeDtypeStruct((slots, LANES), f32),
         in_specs=[smem] + [vmem] * 4,
         out_specs=vmem,
         scratch_shapes=[pltpu.VMEM(((2 * width // LANES + 1) * 24, LANES), f32), pltpu.VMEM((LANES, LANES), f32)],
         compiler_params=limit,
         name="parcel",
     )(sites, board, above, below, diffusion)
+    parcel, partial = lax.optimization_barrier((parcel, partial))
     planes = regions // 2 // RING
-    rings = [[(z * RING + y) * 2 + p for y in range(RING)] for z in range(planes) for p in range(2)]
-    plane = lax.all_to_all(parcel, "region", 0, 0, axis_index_groups=rings)
+    swap = []
+    for z in range(planes):
+        for y in range(RING):
+            to = z + (1 if y >= RING // 2 else -1)
+            if 0 <= to < planes:
+                swap += [((z * RING + y) * 2 + p, (to * RING + RING - 1 - y) * 2 + p) for p in range(2)]
+    other = lax.ppermute(parcel, "region", swap)
     size = own * rows * quarter_width // LANES
     stay, near, cross = pl.pallas_call(
         finish_kernel,
@@ -346,29 +371,33 @@
         in_specs=[smem] + [vmem] * 4,
         out_specs=[vmem] * 3,
         compiler_params=limit,
-        cost_estimate=pl.CostEstimate(flops=2_000_000, bytes_accessed=4_000_000, transcendentals=0),
+        cost_estimate=pl.CostEstimate(flops=10_000_000_000, bytes_accessed=4_000_000, transcendentals=0),
         name="finish",
     )(place, partial, above, below, diffusion)
     crossed = lax.ppermute(cross, "member", [(m, m ^ 2) for m in range(QUARTERS)])
-    plane, _ = lax.optimization_barrier((plane, stay))
+    other, _ = lax.optimization_barrier((other, stay))
+    repeated = pl.pallas_call(
+        repeat_kernel,
+        out_shape=jax.ShapeDtypeStruct((RING, 2 * slots, LANES), f32),
+        in_specs=[vmem] * 2,
+        out_specs=vmem,
+        compiler_params=limit,
+        cost_estimate=pl.CostEstimate(flops=50_000_000_000, bytes_accessed=2_000_000, transcendentals=0),
+        name="repeat",
+    )(parcel, other)
+    rings = [[(z * RING + y) * 2 + p for y in range(RING)] for z in range(planes) for p in range(2)]
+    plane = lax.all_to_all(repeated, "region", 0, 0, axis_index_groups=rings)
     to_core = [(m, m ^ 1) for m in range(QUARTERS)]
     states = [stay, lax.ppermute(near, "member", to_core), crossed, lax.ppermute(crossed[size:], "member", to_core)]
-    swap = []
-    for z in range(planes):
-        for y in range(RING):
-            to = z + (1 if y >= RING // 2 else -1)
-            if 0 <= to < planes:
-                swap += [((z * RING + y) * 2 + p, (to * RING + RING - 1 - y) * 2 + p) for p in range(2)]
-    other = lax.ppermute(plane, "region", swap)
     packed = pl.pallas_call(
         pack_kernel,
         out_shape=jax.ShapeDtypeStruct((2 * QUARTERS, 6 * slots, LANES), f32),
-        in_specs=[smem] + [vmem] * 2,
+        in_specs=[smem, vmem],
         out_specs=vmem,
         compiler_params=limit,
+        cost_estimate=pl.CostEstimate(flops=1_000_000, bytes_accessed=2_000_000, transcendentals=0),
         name="pack",
-    )(place, plane, other)
-    packed, _ = lax.optimization_barrier((packed, crossed))
+    )(place, plane)
     lines = [[2 * QUARTERS * g + i for i in range(2 * QUARTERS)] for g in range(regions // 2)]
     parcels = lax.all_to_all(packed, ("region", "member"), 0, 0, axis_index_groups=lines)
     block = 2 * slots
@@ -377,7 +406,7 @@
         functools.partial(update_kernel, width=width),
         out_shape=jax.ShapeDtypeStruct((members, rows, quarter_width), f32),
         in_specs=[smem] + [vmem] * 5,
-        out_specs=vmem,
+        out_specs=pl.BlockSpec(memory_space=pl.ANY),
         scratch_shapes=[
             pltpu.VMEM((total, LANES), f32),
             pltpu.VMEM((9 * block, LANES), f32),
@@ -388,6 +417,9 @@
             pltpu.VMEM((LANES, LANES), f32),
             pltpu.VMEM((members * rows * quarter_width // LANES, LANES), f32),
             pltpu.VMEM((members * rows * quarter_width // LANES, LANES), f32),
+            pltpu.VMEM((members, rows, quarter_width), f32),
+            pltpu.VMEM((total, LANES), f32),
+            pltpu.SemaphoreType.DMA((2,)),
         ],
         compiler_params=limit,
         name="update",

time: 74 us -> 70.6 us (0.954)
  the two profiles are of different devices: /device:TPU:200 before, /device:TPU:1 now
where the time goes in v3:
time: 70.6 us; the launch traced here: 69.6 us
  starting transfers between devices  23.8 us (34%)
  blocking collectives  20.5 us (29%)
  Pallas kernels  15.7 us (22%)
  waiting for transfers between devices  8 us (11%)
  local copies, waits for them, and re-layouts  1.36 us (2%)
    all_to_all x1, blocking collectives, local(): plane = lax.all_to_all(repeated, 'region', 0, 0, axis_index_groups=rings)  20.5 us
    pallas_call x1, Pallas kernels, local(): pl.pallas_call(functools.partial(update_kernel, width=width), out_shape=j...  10.1 us
    all_to_all x1, starting transfers between devices, local(): lax.all_to_all(packed, ('region', 'member'), 0, 0, axis_index_groups=lines)  8.77 us
    ppermute x1, starting transfers between devices, local(): lax.ppermute(bottom, 'region', [(i, i + 1) for i in range(regions - 1)])  5.62 us
    ppermute x1, waiting for transfers between devices, local(): lax.ppermute(top, 'region', [(i + 1, i) for i in range(regions - 1)])  4.29 us
    all_to_all x1, waiting for transfers between devices, local(): lax.all_to_all(packed, ('region', 'member'), 0, 0, axis_index_groups=lines)  3.69 us
    ppermute x1, starting transfers between devices, local(): lax.ppermute(cross, 'member', [(m, m ^ 2) for m in range(QUARTERS)])  3.15 us
    ppermute x1, starting transfers between devices, local(): lax.ppermute(crossed[size:], 'member', to_core)  2.41 us
  transfers between devices with their start and end apart: 7, of which 2 were waited for; matrix products, arithmetic and copies ran while one was open for 0% of the time, Pallas kernels for 6%

profile of v3, /device:TPU:1, one launch (start us, length us, event | category | flops | bytes accessed | tf_op | source)
XLA Modules:
  0.0 69.6 jit_solution(10930197123867585329)
XLA Ops:
  0.0 0.0 copy-start
  0.0 1.3 %copy-done = f32[20,8,2048]{2,1,0:T(8,128)S(1)} copy-done((f32[20,8,2048]{2,1,0:T(8,128)S(1)}, f32[20,8,2048]{2,1,0:T(8,128)}, u32[]{:S(2)}) %copy-start) | copy-done | bytes 1310744
  1.3 0.0 copy-start.5
  1.3 0.0 copy-start.6
  1.3 0.1 edges.1
  1.4 5.6 %collective-permute-start = (f32[20,2048]{1,0:T(8,128)S(1)}, f32[20,2048]{1,0:T(8,128)S(1)}, u32[]{:S(2)}, u32[]{:S(2)}) collective-permute-start(f32[20,2048]{1,0:T(8,128)S(1)} %get-tuple-element.16), channel_id=1, source_target_pairs={{0,1},{1,2},{2,3},{3,4},{4,5},{5,6},{6,7},{7,8},{8,9},{9,10},{10,1... | collective-permute-start | bytes 491528 | tf_op jit(solution)/shard_map/ppermute | solution.py:335
  7.1 1.3 %collective-permute-start.1 = (f32[20,2048]{1,0:T(8,128)S(1)}, f32[20,2048]{1,0:T(8,128)S(1)}, u32[]{:S(2)}, u32[]{:S(2)}) collective-permute-start(f32[20,2048]{1,0:T(8,128)S(1)} %get-tuple-element.17), channel_id=1, source_target_pairs={{1,0},{2,1},{3,2},{4,3},{5,4},{6,5},{7,6},{8,7},{9,8},{10,9},{11,1... | collective-permute-start | bytes 491528 | tf_op jit(solution)/shard_map/ppermute | solution.py:336
  8.4 0.0 copy-done.1
  8.4 0.0 copy-done.2
  8.4 0.0 copy-done.3
  8.4 0.0 copy-done.4
  8.4 0.0 copy-done.5
  8.5 0.0 copy-done.6
  8.5 2.2 %step.1 = (f32[2560,128]{1,0:T(8,128)S(1)}, f32[128,128]{1,0:T(8,128)S(1)}) custom-call(s32[1]{0:T(128)} %bitcast.2.region_ref, s32[4,16]{1,0:T(4,128)S(1)} %copy-done.3, s32[4,128]{1,0:T(4,128)S(1)} %copy-done.4, f32[20,8,2048]{2,1,0:T(8,128)S(1)} %copy-done.1, f32[8,2048]{1,0:T(8,128)S(1)} %copy-done.2, s32[4,16]{1,0:T(4,128)S(1)} %copy-done.3, ...), custom_call_target="tpu_custom_call" | custom-call | flops 20000000 | bytes 10000000 | tf_op jit(solution)/shard_map/step/pallas_call | solution.py:337
  10.6 0.1 pad_add_fusion.place_ref
  10.7 0.0 collective-permute-done.above_ref
  10.7 4.3 %collective-permute-done.1.below_ref = f32[20,2048]{1,0:T(8,128)S(1)} collective-permute-done((f32[20,2048]{1,0:T(8,128)S(1)}, f32[20,2048]{1,0:T(8,128)S(1)}, u32[]{:S(2)}, u32[]{:S(2)}) %collective-permute-start.1) | collective-permute-done | bytes 163872 | tf_op jit(solution)/shard_map/ppermute | solution.py:336
  15.0 1.2 %parcel.1.own_ref = f32[16,128]{1,0:T(8,128)S(1)} custom-call(s32[4,16]{1,0:T(4,128)S(1)} %copy-done.3, f32[128,128]{1,0:T(8,128)S(1)} %get-tuple-element.15.board_ref, f32[20,2048]{1,0:T(8,128)S(1)} %collective-permute-done.above_ref, f32[20,2048]{1,0:T(8,128)S(1)} %collective-permute-done.1.below_ref, f32[8,2048]{1,0:T(8,128)S(1)} %copy-done.2), custom_call_target="tpu_custom_call" | custom-call | tf_op jit(solution)/shard_map/parcel/pallas_call | solution.py:349
  16.2 0.7 collective-permute-start.2
  16.9 0.8 %finish.1 = (f32[640,128]{1,0:T(8,128)S(1)}, f32[640,128]{1,0:T(8,128)S(1)}, f32[1280,128]{1,0:T(8,128)S(1)}) custom-call(s32[4]{0:T(128)S(1)} %pad_add_fusion.place_ref, f32[2560,128]{1,0:T(8,128)S(1)} %get-tuple-element.20.partial_ref, f32[20,2048]{1,0:T(8,128)S(1)} %collective-permute-done.above_ref, f32[20,2048]{1,0:T(8,128)S(1)} %collective-permute-done.1.below_ref, ...), custom_call_target="tpu_custom_call" | custom-call | flops 10000000000 | bytes 4000000 | tf_op jit(solution)/shard_map/finish/pallas_call | solution.py:368
  17.6 3.2 %collective-permute-start.4 = (f32[1280,128]{1,0:T(8,128)S(1)}, f32[1280,128]{1,0:T(8,128)S(1)}, u32[]{:S(2)}, u32[]{:S(2)}) collective-permute-start(f32[1280,128]{1,0:T(8,128)S(1)} %get-tuple-element.24), channel_id=1, source_target_pairs={{0,256},{128,384},{256,0},{384,128},{1,257},{129,385},{257,1},{385... | collective-permute-start | bytes 1966088 | tf_op jit(solution)/shard_map/ppermute | solution.py:377
  20.8 0.0 collective-permute-done.2.other_ref
  20.8 20.5 %all_to_all.10.plane_ref = f32[8,32,128]{2,1,0:T(8,128)S(1)} all-to-all(f32[8,32,128]{2,1,0:T(8,128)S(1)} %repeat.1), channel_id=1, replica_groups={{0,2,4,6,8,10,12,14},{1,3,5,7,9,11,13,15},{16,18,20,22,24,26,28,30},{17..., dimensions={0} | all-to-all | bytes 262144 | tf_op jit(solution)/shard_map/all_to_all | solution.py:389
  41.3 1.4 %pack.1 = f32[8,96,128]{2,1,0:T(8,128)} custom-call(s32[4]{0:T(128)S(1)} %pad_add_fusion.place_ref, f32[8,32,128]{2,1,0:T(8,128)S(1)} %all_to_all.10.plane_ref), custom_call_target="tpu_custom_call" | custom-call | flops 1000000 | bytes 2000000 | tf_op jit(solution)/shard_map/pack/pallas_call | solution.py:392
  42.7 8.8 %all-to-all-start.1 = ((f32[8,96,128]{2,1,0:T(8,128)}), f32[8,96,128]{2,1,0:T(8,128)S(1)}, u32[]{:S(2)}, u32[]{:S(2)}) async-start(f32[8,96,128]{2,1,0:T(8,128)} %pack.1), calls=%async_computation.1 | async-start | bytes 786432 | tf_op jit(solution)/shard_map/all_to_all | solution.py:402
  51.4 1.9 %collective-permute-start.3 = (f32[640,128]{1,0:T(8,128)S(1)}, f32[640,128]{1,0:T(8,128)S(1)}, u32[]{:S(2)}, u32[]{:S(2)}) collective-permute-start(f32[640,128]{1,0:T(8,128)S(1)} %get-tuple-element.23), channel_id=1, source_target_pairs={{0,128},{128,0},{256,384},{384,256},{1,129},{129,1},{257,385},{385... | collective-permute-start | bytes 983048 | tf_op jit(solution)/shard_map/ppermute | solution.py:391
  53.4 0.0 collective-permute-done.4.state2_ref
  53.4 2.4 %collective-permute-start.5 = (f32[640,128]{1,0:T(8,128)S(1)}, f32[640,128]{1,0:T(8,128)S(1)}, u32[]{:S(2)}, u32[]{:S(2)}) collective-permute-start(f32[640,128]{1,0:T(8,128)S(1)} %slice.4), channel_id=1, source_target_pairs={{0,128},{128,0},{256,384},{384,256},{1,129},{129,1},{257,385},{385... | collective-permute-start | bytes 983048 | tf_op jit(solution)/shard_map/ppermute | solution.py:391
  55.8 0.0 collective-permute-done.3.state1_ref
  55.8 3.7 %all-to-all-done.1.parcels_ref = f32[8,96,128]{2,1,0:T(8,128)S(1)} async-done(((f32[8,96,128]{2,1,0:T(8,128)}), f32[8,96,128]{2,1,0:T(8,128)S(1)}, u32[]{:S(2)}, u32[]{:S(2)}) %all-to-all-start.1) | async-done | bytes 393248 | tf_op jit(solution)/shard_map/all_to_all | solution.py:402
  59.5 0.0 collective-permute-done.5.state3_ref
  59.5 10.1 %update.1 = f32[80,8,512]{2,1,0:T(8,128)} custom-call(s32[4]{0:T(128)S(1)} %pad_add_fusion.place_ref, f32[8,96,128]{2,1,0:T(8,128)S(1)} %all-to-all-done.1.parcels_ref, f32[640,128]{1,0:T(8,128)S(1)} %get-tuple-element.21.state0_ref, f32[640,128]{1,0:T(8,128)S(1)} %collective-permute-done.3.state1_ref, f32[1280,128]{1,0:T(8,128)S(1)} %collective-permute-done.4.state2_ref, ...), custom_call_target="tpu_custom_call" | custom-call | tf_op jit(solution)/shard_map/update/pallas_call | solution.py:405
  (6 shorter events, 0.0 us)
Async XLA Ops:
  0.0 1.3 %copy-start = (f32[20,8,2048]{2,1,0:T(8,128)S(1)}, f32[20,8,2048]{2,1,0:T(8,128)}, u32[]{:S(2)}) copy-start(f32[20,8,2048]{2,1,0:T(8,128)} %tracer_ref.3) | copy-start | bytes 3932164
  1.3 7.1 %copy-start.1 = (f32[20,8,2048]{2,1,0:T(8,128)S(1)}, f32[20,8,2048]{2,1,0:T(8,128)}, u32[]{:S(2)}) copy-start(f32[20,8,2048]{2,1,0:T(8,128)} %tracer_ref.3) | copy-start | bytes 3932164
  1.3 7.1 %copy-start.2 = (f32[8,2048]{1,0:T(8,128)S(1)}, f32[8,2048]{1,0:T(8,128)}, u32[]{:S(2)}) copy-start(f32[8,2048]{1,0:T(8,128)} %diffusion_ref.5) | copy-start | bytes 196612
  1.3 7.1 %copy-start.3 = (s32[4,16]{1,0:T(4,128)S(1)}, s32[4,16]{1,0:T(4,128)}, u32[]{:S(2)}) copy-start(s32[4,16]{1,0:T(4,128)} %site_ref.3) | copy-start | bytes 772
  1.3 7.1 %copy-start.4 = (s32[4,128]{1,0:T(4,128)S(1)}, s32[4,128]{1,0:T(4,128)}, u32[]{:S(2)}) copy-start(s32[4,128]{1,0:T(4,128)} %tally_ref.1) | copy-start | bytes 6148
  1.3 7.1 %copy-start.5 = (f32[4,16]{1,0:T(4,128)S(1)}, f32[4,16]{1,0:T(4,128)}, u32[]{:S(2)}) copy-start(f32[4,16]{1,0:T(4,128)} %reading_ref.1) | copy-start | bytes 772
  1.3 7.1 %copy-start.6 = (f32[4,16]{1,0:T(4,128)S(1)}, f32[4,16]{1,0:T(4,128)}, u32[]{:S(2)}) copy-start(f32[4,16]{1,0:T(4,128)} %variance_ref.1) | copy-start | bytes 772
  1.4 9.3 %collective-permute-start = (f32[20,2048]{1,0:T(8,128)S(1)}, f32[20,2048]{1,0:T(8,128)S(1)}, u32[]{:S(2)}, u32[]{:S(2)}) collective-permute-start(f32[20,2048]{1,0:T(8,128)S(1)} %get-tuple-element.16), channel_id=1, source_target_pairs={{0,1},{1,2},{2,3},{3,4},{4,5},{5,6},{6,7},{7,8},{8,9},{9,10},{10,1... | collective-permute-start | bytes 491528 | tf_op jit(solution)/shard_map/ppermute | solution.py:335
  7.1 7.9 %collective-permute-start.1 = (f32[20,2048]{1,0:T(8,128)S(1)}, f32[20,2048]{1,0:T(8,128)S(1)}, u32[]{:S(2)}, u32[]{:S(2)}) collective-permute-start(f32[20,2048]{1,0:T(8,128)S(1)} %get-tuple-element.17), channel_id=1, source_target_pairs={{1,0},{2,1},{3,2},{4,3},{5,4},{6,5},{7,6},{8,7},{9,8},{10,9},{11,1... | collective-permute-start | bytes 491528 | tf_op jit(solution)/shard_map/ppermute | solution.py:336
  16.2 4.6 %collective-permute-start.2 = (f32[16,128]{1,0:T(8,128)S(1)}, f32[16,128]{1,0:T(8,128)S(1)}, u32[]{:S(2)}, u32[]{:S(2)}) collective-permute-start(f32[16,128]{1,0:T(8,128)S(1)} %parcel.1.own_ref), channel_id=1, source_target_pairs={{8,22},{9,23},{10,20},{11,21},{12,18},{13,19},{14,16},{15,17},{16,... | collective-permute-start | bytes 24584 | tf_op jit(solution)/shard_map/ppermute | solution.py:366
  17.6 35.7 %collective-permute-start.4 = (f32[1280,128]{1,0:T(8,128)S(1)}, f32[1280,128]{1,0:T(8,128)S(1)}, u32[]{:S(2)}, u32[]{:S(2)}) collective-permute-start(f32[1280,128]{1,0:T(8,128)S(1)} %get-tuple-element.24), channel_id=1, source_target_pairs={{0,256},{128,384},{256,0},{384,128},{1,257},{129,385},{257,1},{385... | collective-permute-start | bytes 1966088 | tf_op jit(solution)/shard_map/ppermute | solution.py:377
  42.7 16.9 %all-to-all-start.1 = ((f32[8,96,128]{2,1,0:T(8,128)}), f32[8,96,128]{2,1,0:T(8,128)S(1)}, u32[]{:S(2)}, u32[]{:S(2)}) async-start(f32[8,96,128]{2,1,0:T(8,128)} %pack.1), calls=%async_computation.1 | async-start | bytes 786432 | tf_op jit(solution)/shard_map/all_to_all | solution.py:402
  51.4 4.4 %collective-permute-start.3 = (f32[640,128]{1,0:T(8,128)S(1)}, f32[640,128]{1,0:T(8,128)S(1)}, u32[]{:S(2)}, u32[]{:S(2)}) collective-permute-start(f32[640,128]{1,0:T(8,128)S(1)} %get-tuple-element.23), channel_id=1, source_target_pairs={{0,128},{128,0},{256,384},{384,256},{1,129},{129,1},{257,385},{385... | collective-permute-start | bytes 983048 | tf_op jit(solution)/shard_map/ppermute | solution.py:391
  53.4 6.1 %collective-permute-start.5 = (f32[640,128]{1,0:T(8,128)S(1)}, f32[640,128]{1,0:T(8,128)S(1)}, u32[]{:S(2)}, u32[]{:S(2)}) collective-permute-start(f32[640,128]{1,0:T(8,128)S(1)} %slice.4), channel_id=1, source_target_pairs={{0,128},{128,0},{256,384},{384,256},{1,129},{129,1},{257,385},{385... | collective-permute-start | bytes 983048 | tf_op jit(solution)/shard_map/ppermute | solution.py:391

commit v4 on v3

--- a/solution.py
+++ b/solution.py
@@ -237,6 +237,30 @@
     centre = jnp.sum(jnp.where(inside, everything, 0.0), axis=1, keepdims=True) / members
     centre_ref[...] = jnp.broadcast_to(centre, everything.shape)
     obs[...] = jnp.where(inside, everything - centre, everything)
+    cols = (lane_of((80, quarter_width)) + quarter * quarter_width).astype(f32)
+    closeness = {}
+    together = 4
+
+    def load(first):
+        lines = [(r, t) for t in range(first, first + together) for r in range(rows)]
+        return jnp.concatenate([state_ref[pl.ds(t * rows + r, members, stride=tiles * rows), :] for r, t in lines], axis=1)
+
+    def assimilate(state, b, first):
+        covariance = jnp.dot(gain_lhs[b], below_each_other(state), preferred_element_type=f32)
+        tapers = []
+        for t in range(first, first + together):
+            near = closeness[b][:, t * LANES : (t + 1) * LANES]
+            for r in range(rows):
+                gap = (region * rows + r).astype(f32) - near_ref[b, :, members + ROW : members + ROW + 1]
+                remain = jnp.maximum(near - gap * gap * scale, 0.0)
+                tapers.append(remain * remain)
+        weights = jnp.concatenate(tapers, axis=1) * covariance
+        return state + jnp.dot(inc_lhs[b], below_each_other(weights), preferred_element_type=f32)
+
+    firsts = range(0, tiles, together)
+    fields = [load(first) for first in firsts]
+    centres_of = [jnp.mean(field, axis=0, keepdims=True) for field in fields]
+    fields = [field - centre for field, centre in zip(fields, centres_of)]
     for b in range(4):
         n = starts[b + 1] - starts[b]
         x = obs[starts[b] : starts[b + 1], :]
@@ -260,6 +284,9 @@
         board[...] = jnp.zeros_like(board)
         board[0:80, :] = inc_ref[pl.ds(at, 80), :]
         inc_lhs[b] = beside(*halves(board[...].T[0:80, :]))
+        gap = jnp.abs(cols - near_ref[b, :, members + COLUMN : members + COLUMN + 1])
+        gap = jnp.minimum(gap, width - gap)
+        closeness[b] = 1.0 - gap * gap * scale
         if b < 3:
             y = obs[starts[b + 1] : total, :]
             m = total - starts[b + 1]
@@ -270,38 +297,11 @@
             remain = jnp.maximum(1.0 - (row_gap * row_gap + col_gap * col_gap) * scale, 0.0)
             weights = remain * remain * covariance
             obs[starts[b + 1] : total, :] = y + product(weights, increment, ((1,), (0,)))
-    cols = (lane_of((80, quarter_width)) + quarter * quarter_width).astype(f32)
-    closeness = []
-    for b in range(4):
-        gap = jnp.abs(cols - near_ref[b, :, members + COLUMN : members + COLUMN + 1])
-        gap = jnp.minimum(gap, width - gap)
-        closeness.append(1.0 - gap * gap * scale)
-    together = 2
-
-    def load(first):
-        lines = [(r, t) for t in range(first, first + together) for r in range(rows)]
-        return jnp.concatenate([state_ref[pl.ds(t * rows + r, members, stride=tiles * rows), :] for r, t in lines], axis=1)
-
-    def assimilate(state, b, first):
-        covariance = jnp.dot(gain_lhs[b], below_each_other(state), preferred_element_type=f32)
-        tapers = []
-        for t in range(first, first + together):
-            near = closeness[b][:, t * LANES : (t + 1) * LANES]
-            for r in range(rows):
-                gap = (region * rows + r).astype(f32) - near_ref[b, :, members + ROW : members + ROW + 1]
-                remain = jnp.maximum(near - gap * gap * scale, 0.0)
-                tapers.append(remain * remain)
-        weights = jnp.concatenate(tapers, axis=1) * covariance
-        return state + jnp.dot(inc_lhs[b], below_each_other(weights), preferred_element_type=f32)
-
+        if b < 3:
+            fields = [assimilate(field, b, first) for field, first in zip(fields, firsts)]
     copies = []
-    for first in range(0, tiles, together):
-        state = load(first)
-        centre = jnp.mean(state, axis=0, keepdims=True)
-        state = state - centre
-        for b in range(4):
-            state = assimilate(state, b, first)
-        state = state + centre
+    for first, field, centre in zip(firsts, fields, centres_of):
+        state = assimilate(field, 3, first) + centre
         for i in range(together * rows):
             t, r = first + i // rows, i % rows
             updated[(t * rows + r) * members : (t * rows + r + 1) * members, :] = state[:, i * LANES : (i + 1) * LANES]

time: 70.6 us -> 70 us (level)
  no operation moved by 1% of the time
where the time goes in v4:
time: 70 us; the launch traced here: 69.1 us
  starting transfers between devices  23.8 us (34%)
  blocking collectives  20.5 us (29%)
  Pallas kernels  15.1 us (22%)
  waiting for transfers between devices  8 us (11%)
  local copies, waits for them, and re-layouts  1.36 us (2%)
    all_to_all x1, blocking collectives, local(): plane = lax.all_to_all(repeated, 'region', 0, 0, axis_index_groups=rings)  20.5 us
    pallas_call x1, Pallas kernels, local(): pl.pallas_call(functools.partial(update_kernel, width=width), out_shape=j...  9.54 us
    all_to_all x1, starting transfers between devices, local(): lax.all_to_all(packed, ('region', 'member'), 0, 0, axis_index_groups=lines)  8.77 us
    ppermute x1, starting transfers between devices, local(): lax.ppermute(bottom, 'region', [(i, i + 1) for i in range(regions - 1)])  5.62 us
    ppermute x1, waiting for transfers between devices, local(): lax.ppermute(top, 'region', [(i + 1, i) for i in range(regions - 1)])  4.29 us
    all_to_all x1, waiting for transfers between devices, local(): lax.all_to_all(packed, ('region', 'member'), 0, 0, axis_index_groups=lines)  3.69 us
    ppermute x1, starting transfers between devices, local(): lax.ppermute(cross, 'member', [(m, m ^ 2) for m in range(QUARTERS)])  3.15 us
    ppermute x1, starting transfers between devices, local(): lax.ppermute(crossed[size:], 'member', to_core)  2.41 us
  transfers between devices with their start and end apart: 7, of which 2 were waited for; matrix products, arithmetic and copies ran while one was open for 0% of the time, Pallas kernels for 6%

profile of v4, /device:TPU:1, one launch (start us, length us, event | category | flops | bytes accessed | tf_op | source)
XLA Modules:
  0.0 69.1 jit_solution(9270494616790450206)
XLA Ops:
  0.0 0.0 copy-start
  0.0 1.3 %copy-done = f32[20,8,2048]{2,1,0:T(8,128)S(1)} copy-done((f32[20,8,2048]{2,1,0:T(8,128)S(1)}, f32[20,8,2048]{2,1,0:T(8,128)}, u32[]{:S(2)}) %copy-start) | copy-done | bytes 1310744
  1.3 0.0 copy-start.5
  1.3 0.0 copy-start.6
  1.3 0.1 edges.1
  1.4 5.6 %collective-permute-start = (f32[20,2048]{1,0:T(8,128)S(1)}, f32[20,2048]{1,0:T(8,128)S(1)}, u32[]{:S(2)}, u32[]{:S(2)}) collective-permute-start(f32[20,2048]{1,0:T(8,128)S(1)} %get-tuple-element.16), channel_id=1, source_target_pairs={{0,1},{1,2},{2,3},{3,4},{4,5},{5,6},{6,7},{7,8},{8,9},{9,10},{10,1... | collective-permute-start | bytes 491528 | tf_op jit(solution)/shard_map/ppermute | solution.py:335
  7.1 1.3 %collective-permute-start.1 = (f32[20,2048]{1,0:T(8,128)S(1)}, f32[20,2048]{1,0:T(8,128)S(1)}, u32[]{:S(2)}, u32[]{:S(2)}) collective-permute-start(f32[20,2048]{1,0:T(8,128)S(1)} %get-tuple-element.17), channel_id=1, source_target_pairs={{1,0},{2,1},{3,2},{4,3},{5,4},{6,5},{7,6},{8,7},{9,8},{10,9},{11,1... | collective-permute-start | bytes 491528 | tf_op jit(solution)/shard_map/ppermute | solution.py:336
  8.4 0.0 copy-done.1
  8.4 0.0 copy-done.2
  8.4 0.0 copy-done.3
  8.4 0.0 copy-done.4
  8.4 0.0 copy-done.5
  8.5 0.0 copy-done.6
  8.5 2.2 %step.1 = (f32[2560,128]{1,0:T(8,128)S(1)}, f32[128,128]{1,0:T(8,128)S(1)}) custom-call(s32[1]{0:T(128)} %bitcast.2.region_ref, s32[4,16]{1,0:T(4,128)S(1)} %copy-done.3, s32[4,128]{1,0:T(4,128)S(1)} %copy-done.4, f32[20,8,2048]{2,1,0:T(8,128)S(1)} %copy-done.1, f32[8,2048]{1,0:T(8,128)S(1)} %copy-done.2, s32[4,16]{1,0:T(4,128)S(1)} %copy-done.3, ...), custom_call_target="tpu_custom_call" | custom-call | flops 20000000 | bytes 10000000 | tf_op jit(solution)/shard_map/step/pallas_call | solution.py:337
  10.6 0.1 pad_add_fusion.place_ref
  10.7 0.0 collective-permute-done.above_ref
  10.7 4.3 %collective-permute-done.1.below_ref = f32[20,2048]{1,0:T(8,128)S(1)} collective-permute-done((f32[20,2048]{1,0:T(8,128)S(1)}, f32[20,2048]{1,0:T(8,128)S(1)}, u32[]{:S(2)}, u32[]{:S(2)}) %collective-permute-start.1) | collective-permute-done | bytes 163872 | tf_op jit(solution)/shard_map/ppermute | solution.py:336
  15.0 1.2 %parcel.1.own_ref = f32[16,128]{1,0:T(8,128)S(1)} custom-call(s32[4,16]{1,0:T(4,128)S(1)} %copy-done.3, f32[128,128]{1,0:T(8,128)S(1)} %get-tuple-element.15.board_ref, f32[20,2048]{1,0:T(8,128)S(1)} %collective-permute-done.above_ref, f32[20,2048]{1,0:T(8,128)S(1)} %collective-permute-done.1.below_ref, f32[8,2048]{1,0:T(8,128)S(1)} %copy-done.2), custom_call_target="tpu_custom_call" | custom-call | tf_op jit(solution)/shard_map/parcel/pallas_call | solution.py:349
  16.2 0.7 collective-permute-start.2
  16.9 0.8 %finish.1 = (f32[640,128]{1,0:T(8,128)S(1)}, f32[640,128]{1,0:T(8,128)S(1)}, f32[1280,128]{1,0:T(8,128)S(1)}) custom-call(s32[4]{0:T(128)S(1)} %pad_add_fusion.place_ref, f32[2560,128]{1,0:T(8,128)S(1)} %get-tuple-element.20.partial_ref, f32[20,2048]{1,0:T(8,128)S(1)} %collective-permute-done.above_ref, f32[20,2048]{1,0:T(8,128)S(1)} %collective-permute-done.1.below_ref, ...), custom_call_target="tpu_custom_call" | custom-call | flops 10000000000 | bytes 4000000 | tf_op jit(solution)/shard_map/finish/pallas_call | solution.py:368
  17.6 3.2 %collective-permute-start.4 = (f32[1280,128]{1,0:T(8,128)S(1)}, f32[1280,128]{1,0:T(8,128)S(1)}, u32[]{:S(2)}, u32[]{:S(2)}) collective-permute-start(f32[1280,128]{1,0:T(8,128)S(1)} %get-tuple-element.24), channel_id=1, source_target_pairs={{0,256},{128,384},{256,0},{384,128},{1,257},{129,385},{257,1},{385... | collective-permute-start | bytes 1966088 | tf_op jit(solution)/shard_map/ppermute | solution.py:377
  20.8 0.0 collective-permute-done.2.other_ref
  20.8 20.5 %all_to_all.10.plane_ref = f32[8,32,128]{2,1,0:T(8,128)S(1)} all-to-all(f32[8,32,128]{2,1,0:T(8,128)S(1)} %repeat.1), channel_id=1, replica_groups={{0,2,4,6,8,10,12,14},{1,3,5,7,9,11,13,15},{16,18,20,22,24,26,28,30},{17..., dimensions={0} | all-to-all | bytes 262144 | tf_op jit(solution)/shard_map/all_to_all | solution.py:389
  41.3 1.4 %pack.1 = f32[8,96,128]{2,1,0:T(8,128)} custom-call(s32[4]{0:T(128)S(1)} %pad_add_fusion.place_ref, f32[8,32,128]{2,1,0:T(8,128)S(1)} %all_to_all.10.plane_ref), custom_call_target="tpu_custom_call" | custom-call | flops 1000000 | bytes 2000000 | tf_op jit(solution)/shard_map/pack/pallas_call | solution.py:392
  42.7 8.8 %all-to-all-start.1 = ((f32[8,96,128]{2,1,0:T(8,128)}), f32[8,96,128]{2,1,0:T(8,128)S(1)}, u32[]{:S(2)}, u32[]{:S(2)}) async-start(f32[8,96,128]{2,1,0:T(8,128)} %pack.1), calls=%async_computation.1 | async-start | bytes 786432 | tf_op jit(solution)/shard_map/all_to_all | solution.py:402
  51.4 1.9 %collective-permute-start.3 = (f32[640,128]{1,0:T(8,128)S(1)}, f32[640,128]{1,0:T(8,128)S(1)}, u32[]{:S(2)}, u32[]{:S(2)}) collective-permute-start(f32[640,128]{1,0:T(8,128)S(1)} %get-tuple-element.23), channel_id=1, source_target_pairs={{0,128},{128,0},{256,384},{384,256},{1,129},{129,1},{257,385},{385... | collective-permute-start | bytes 983048 | tf_op jit(solution)/shard_map/ppermute | solution.py:391
  53.4 0.0 collective-permute-done.4.state2_ref
  53.4 2.4 %collective-permute-start.5 = (f32[640,128]{1,0:T(8,128)S(1)}, f32[640,128]{1,0:T(8,128)S(1)}, u32[]{:S(2)}, u32[]{:S(2)}) collective-permute-start(f32[640,128]{1,0:T(8,128)S(1)} %slice.4), channel_id=1, source_target_pairs={{0,128},{128,0},{256,384},{384,256},{1,129},{129,1},{257,385},{385... | collective-permute-start | bytes 983048 | tf_op jit(solution)/shard_map/ppermute | solution.py:391
  55.8 0.0 collective-permute-done.3.state1_ref
  55.8 3.7 %all-to-all-done.1.parcels_ref = f32[8,96,128]{2,1,0:T(8,128)S(1)} async-done(((f32[8,96,128]{2,1,0:T(8,128)}), f32[8,96,128]{2,1,0:T(8,128)S(1)}, u32[]{:S(2)}, u32[]{:S(2)}) %all-to-all-start.1) | async-done | bytes 393248 | tf_op jit(solution)/shard_map/all_to_all | solution.py:402
  59.5 0.0 collective-permute-done.5.state3_ref
  59.5 9.5 %update.1 = f32[80,8,512]{2,1,0:T(8,128)} custom-call(s32[4]{0:T(128)S(1)} %pad_add_fusion.place_ref, f32[8,96,128]{2,1,0:T(8,128)S(1)} %all-to-all-done.1.parcels_ref, f32[640,128]{1,0:T(8,128)S(1)} %get-tuple-element.21.state0_ref, f32[640,128]{1,0:T(8,128)S(1)} %collective-permute-done.3.state1_ref, f32[1280,128]{1,0:T(8,128)S(1)} %collective-permute-done.4.state2_ref, ...), custom_call_target="tpu_custom_call" | custom-call | tf_op jit(solution)/shard_map/update/pallas_call | solution.py:405
  (6 shorter events, 0.0 us)
Async XLA Ops:
  0.0 1.3 %copy-start = (f32[20,8,2048]{2,1,0:T(8,128)S(1)}, f32[20,8,2048]{2,1,0:T(8,128)}, u32[]{:S(2)}) copy-start(f32[20,8,2048]{2,1,0:T(8,128)} %tracer_ref.3) | copy-start | bytes 3932164
  1.3 7.1 %copy-start.1 = (f32[20,8,2048]{2,1,0:T(8,128)S(1)}, f32[20,8,2048]{2,1,0:T(8,128)}, u32[]{:S(2)}) copy-start(f32[20,8,2048]{2,1,0:T(8,128)} %tracer_ref.3) | copy-start | bytes 3932164
  1.3 7.1 %copy-start.2 = (f32[8,2048]{1,0:T(8,128)S(1)}, f32[8,2048]{1,0:T(8,128)}, u32[]{:S(2)}) copy-start(f32[8,2048]{1,0:T(8,128)} %diffusion_ref.5) | copy-start | bytes 196612
  1.3 7.1 %copy-start.3 = (s32[4,16]{1,0:T(4,128)S(1)}, s32[4,16]{1,0:T(4,128)}, u32[]{:S(2)}) copy-start(s32[4,16]{1,0:T(4,128)} %site_ref.3) | copy-start | bytes 772
  1.3 7.1 %copy-start.4 = (s32[4,128]{1,0:T(4,128)S(1)}, s32[4,128]{1,0:T(4,128)}, u32[]{:S(2)}) copy-start(s32[4,128]{1,0:T(4,128)} %tally_ref.1) | copy-start | bytes 6148
  1.3 7.1 %copy-start.5 = (f32[4,16]{1,0:T(4,128)S(1)}, f32[4,16]{1,0:T(4,128)}, u32[]{:S(2)}) copy-start(f32[4,16]{1,0:T(4,128)} %reading_ref.1) | copy-start | bytes 772
  1.3 7.1 %copy-start.6 = (f32[4,16]{1,0:T(4,128)S(1)}, f32[4,16]{1,0:T(4,128)}, u32[]{:S(2)}) copy-start(f32[4,16]{1,0:T(4,128)} %variance_ref.1) | copy-start | bytes 772
  1.4 9.3 %collective-permute-start = (f32[20,2048]{1,0:T(8,128)S(1)}, f32[20,2048]{1,0:T(8,128)S(1)}, u32[]{:S(2)}, u32[]{:S(2)}) collective-permute-start(f32[20,2048]{1,0:T(8,128)S(1)} %get-tuple-element.16), channel_id=1, source_target_pairs={{0,1},{1,2},{2,3},{3,4},{4,5},{5,6},{6,7},{7,8},{8,9},{9,10},{10,1... | collective-permute-start | bytes 491528 | tf_op jit(solution)/shard_map/ppermute | solution.py:335
  7.1 7.9 %collective-permute-start.1 = (f32[20,2048]{1,0:T(8,128)S(1)}, f32[20,2048]{1,0:T(8,128)S(1)}, u32[]{:S(2)}, u32[]{:S(2)}) collective-permute-start(f32[20,2048]{1,0:T(8,128)S(1)} %get-tuple-element.17), channel_id=1, source_target_pairs={{1,0},{2,1},{3,2},{4,3},{5,4},{6,5},{7,6},{8,7},{9,8},{10,9},{11,1... | collective-permute-start | bytes 491528 | tf_op jit(solution)/shard_map/ppermute | solution.py:336
  16.2 4.6 %collective-permute-start.2 = (f32[16,128]{1,0:T(8,128)S(1)}, f32[16,128]{1,0:T(8,128)S(1)}, u32[]{:S(2)}, u32[]{:S(2)}) collective-permute-start(f32[16,128]{1,0:T(8,128)S(1)} %parcel.1.own_ref), channel_id=1, source_target_pairs={{8,22},{9,23},{10,20},{11,21},{12,18},{13,19},{14,16},{15,17},{16,... | collective-permute-start | bytes 24584 | tf_op jit(solution)/shard_map/ppermute | solution.py:366
  17.6 35.7 %collective-permute-start.4 = (f32[1280,128]{1,0:T(8,128)S(1)}, f32[1280,128]{1,0:T(8,128)S(1)}, u32[]{:S(2)}, u32[]{:S(2)}) collective-permute-start(f32[1280,128]{1,0:T(8,128)S(1)} %get-tuple-element.24), channel_id=1, source_target_pairs={{0,256},{128,384},{256,0},{384,128},{1,257},{129,385},{257,1},{385... | collective-permute-start | bytes 1966088 | tf_op jit(solution)/shard_map/ppermute | solution.py:377
  42.7 16.9 %all-to-all-start.1 = ((f32[8,96,128]{2,1,0:T(8,128)}), f32[8,96,128]{2,1,0:T(8,128)S(1)}, u32[]{:S(2)}, u32[]{:S(2)}) async-start(f32[8,96,128]{2,1,0:T(8,128)} %pack.1), calls=%async_computation.1 | async-start | bytes 786432 | tf_op jit(solution)/shard_map/all_to_all | solution.py:402
  51.4 4.4 %collective-permute-start.3 = (f32[640,128]{1,0:T(8,128)S(1)}, f32[640,128]{1,0:T(8,128)S(1)}, u32[]{:S(2)}, u32[]{:S(2)}) collective-permute-start(f32[640,128]{1,0:T(8,128)S(1)} %get-tuple-element.23), channel_id=1, source_target_pairs={{0,128},{128,0},{256,384},{384,256},{1,129},{129,1},{257,385},{385... | collective-permute-start | bytes 983048 | tf_op jit(solution)/shard_map/ppermute | solution.py:391
  53.4 6.1 %collective-permute-start.5 = (f32[640,128]{1,0:T(8,128)S(1)}, f32[640,128]{1,0:T(8,128)S(1)}, u32[]{:S(2)}, u32[]{:S(2)}) collective-permute-start(f32[640,128]{1,0:T(8,128)S(1)} %slice.4), channel_id=1, source_target_pairs={{0,128},{128,0},{256,384},{384,256},{1,129},{129,1},{257,385},{385... | collective-permute-start | bytes 983048 | tf_op jit(solution)/shard_map/ppermute | solution.py:391

commit v5 on v4

--- a/solution.py
+++ b/solution.py
@@ -49,7 +49,7 @@
 
 def step_kernel(
     region_ref, site_ref, tally_ref, tracer_ref, diffusion_ref, site_vec_ref, reading_ref, variance_ref,
-    partial_ref, board_ref,
+    partial_ref, board_ref, spot_ref,
 ):
     own, rows, width = tracer_ref.shape
     batches, slots = site_ref.shape
@@ -81,6 +81,10 @@
             line = partial_ref[pl.ds(start, own, stride=tiles * rows), :]
             shift = lax.rem(k - lax.rem(col, LANES) + LANES, LANES)
             picked = jnp.where(lane == k, pltpu.roll(line, shift, 1), picked)
+            row = lax.div(cell, width)
+            block = jnp.where(row == 0, tile, jnp.where(row == rows - 1, QUARTERS * tiles + tile, 2 * QUARTERS * tiles))
+            spot_ref[b, k] = block * 24
+            spot_ref[batches + b, k] = shift
         at = b * 32
         board_ref[at : at + own, :] = picked
         cells = site_vec_ref[b : b + 1, :]
@@ -96,9 +100,9 @@
             board_ref[at + own + i : at + own + i + 1, 0:slots] = fact
 
 
-def parcel_kernel(site_ref, board_ref, above_ref, below_ref, diffusion_ref, parcel_ref, halo, board):
+def parcel_kernel(spot_ref, board_ref, above_ref, below_ref, diffusion_ref, parcel_ref, halo, board):
     own, width = above_ref.shape
-    batches, slots = site_ref.shape
+    batches, slots = spot_ref.shape[0] // 2, spot_ref.shape[1]
     rows = diffusion_ref.shape[0]
     tiles = width // LANES
     for t in range(tiles):
@@ -110,13 +114,8 @@
     for b in range(batches):
         picked = jnp.zeros((24, LANES), f32)
         for k in range(slots):
-            cell = site_ref[b, k]
-            col = lax.rem(cell, width)
-            row = lax.div(cell, width)
-            tile = lax.div(col, LANES)
-            block = jnp.where(row == 0, tile, jnp.where(row == rows - 1, tiles + tile, 2 * tiles))
-            line = halo[pl.ds(pl.multiple_of(block * 24, 8), 24), :]
-            shift = lax.rem(k - lax.rem(col, LANES) + LANES, LANES)
+            line = halo[pl.ds(pl.multiple_of(spot_ref[b, k], 8), 24), :]
+            shift = spot_ref[batches + b, k]
             picked = jnp.where(lane == k, pltpu.roll(line, shift, 1), picked)
         picked = jnp.where(row_of((24, LANES)) < own, picked, 0.0)
         board[b * 32 : b * 32 + 24, :] = board_ref[b * 32 : b * 32 + 24, :] + picked
@@ -299,18 +298,18 @@
             obs[starts[b + 1] : total, :] = y + product(weights, increment, ((1,), (0,)))
         if b < 3:
             fields = [assimilate(field, b, first) for field, first in zip(fields, firsts)]
+    state = assimilate(fields[0], 3, 0) + centres_of[0]
     copies = []
-    for first, field, centre in zip(firsts, fields, centres_of):
-        state = assimilate(field, 3, first) + centre
-        for i in range(together * rows):
-            t, r = first + i // rows, i % rows
-            updated[(t * rows + r) * members : (t * rows + r + 1) * members, :] = state[:, i * LANES : (i + 1) * LANES]
-        cols = slice(first * LANES, (first + together) * LANES)
-        for e in range(members):
-            for t in range(first, first + together):
+    for half in range(2):
+        for t in range(half * tiles // 2, (half + 1) * tiles // 2):
+            for r in range(rows):
+                i = t * rows + r
+                updated[i * members : (i + 1) * members, :] = state[:, i * LANES : (i + 1) * LANES]
+            for e in range(members):
                 line = updated[pl.ds(t * rows * members + e, rows, stride=members), :]
                 whole[e, :, t * LANES : (t + 1) * LANES] = line
-        copies.append(pltpu.make_async_copy(whole.at[:, :, cols], out_ref.at[:, :, cols], sems.at[first // together]))
+        cols = pl.ds(half * quarter_width // 2, quarter_width // 2)
+        copies.append(pltpu.make_async_copy(whole.at[:, :, cols], out_ref.at[:, :, cols], sems.at[half]))
         copies[-1].start()
     for copy in copies:
         copy.wait()
@@ -334,14 +333,15 @@
     )(tracer)
     above = lax.ppermute(bottom, "region", [(i, i + 1) for i in range(regions - 1)])
     below = lax.ppermute(top, "region", [(i + 1, i) for i in range(regions - 1)])
-    partial, board = pl.pallas_call(
+    partial, board, spots = pl.pallas_call(
         step_kernel,
         out_shape=(
             jax.ShapeDtypeStruct((own * rows * width // LANES, LANES), f32),
             jax.ShapeDtypeStruct((LANES, LANES), f32),
+            jax.ShapeDtypeStruct((2 * batches, slots), jnp.int32),
         ),
         in_specs=[smem] * 3 + [vmem] * 5,
-        out_specs=(vmem, vmem),
+        out_specs=(vmem, vmem, smem),
         compiler_params=limit,
         cost_estimate=pl.CostEstimate(flops=20_000_000, bytes_accessed=10_000_000, transcendentals=0),
         name="step",
@@ -354,7 +354,7 @@
         scratch_shapes=[pltpu.VMEM(((2 * width // LANES + 1) * 24, LANES), f32), pltpu.VMEM((LANES, LANES), f32)],
         compiler_params=limit,
         name="parcel",
-    )(sites, board, above, below, diffusion)
+    )(spots, board, above, below, diffusion)
     parcel, partial = lax.optimization_barrier((parcel, partial))
     planes = regions // 2 // RING
     swap = []

time: 70 us -> 69.6 us (level)
  transfers between devices with their start and end apart: 7 -> 7, of which waited for: 2 -> 2; matrix products, arithmetic and copies ran while one was open for 0% -> 0% of each run, Pallas kernels for 6% -> 7%
where the time goes in v5:
time: 69.6 us; the launch traced here: 68.6 us
  starting transfers between devices  23.8 us (34%)
  blocking collectives  20.5 us (29%)
  Pallas kernels  15.3 us (22%)
  waiting for transfers between devices  7.34 us (11%)
  local copies, waits for them, and re-layouts  1.36 us (2%)
    all_to_all x1, blocking collectives, local(): plane = lax.all_to_all(repeated, 'region', 0, 0, axis_index_groups=rings)  20.5 us
    pallas_call x1, Pallas kernels, local(): pl.pallas_call(functools.partial(update_kernel, width=width), out_shape=j...  9.32 us
    all_to_all x1, starting transfers between devices, local(): lax.all_to_all(packed, ('region', 'member'), 0, 0, axis_index_groups=lines)  8.77 us
    ppermute x1, starting transfers between devices, local(): lax.ppermute(bottom, 'region', [(i, i + 1) for i in range(regions - 1)])  5.62 us
    all_to_all x1, waiting for transfers between devices, local(): lax.all_to_all(packed, ('region', 'member'), 0, 0, axis_index_groups=lines)  3.69 us
    ppermute x1, waiting for transfers between devices, local(): lax.ppermute(top, 'region', [(i + 1, i) for i in range(regions - 1)])  3.63 us
    ppermute x1, starting transfers between devices, local(): lax.ppermute(cross, 'member', [(m, m ^ 2) for m in range(QUARTERS)])  3.15 us
    pallas_call x1, Pallas kernels, local(): pl.pallas_call(step_kernel, out_shape=(jax.ShapeDtypeStruct((own * rows *...  2.8 us
  transfers between devices with their start and end apart: 7, of which 2 were waited for; matrix products, arithmetic and copies ran while one was open for 0% of the time, Pallas kernels for 7%

profile of v5, /device:TPU:1, one launch (start us, length us, event | category | flops | bytes accessed | tf_op | source)
XLA Modules:
  0.0 68.6 jit_solution(11410614094883735487)
XLA Ops:
  0.0 0.0 copy-start
  0.0 1.3 %copy-done = f32[20,8,2048]{2,1,0:T(8,128)S(1)} copy-done((f32[20,8,2048]{2,1,0:T(8,128)S(1)}, f32[20,8,2048]{2,1,0:T(8,128)}, u32[]{:S(2)}) %copy-start) | copy-done | bytes 1310744
  1.3 0.0 copy-start.5
  1.3 0.0 copy-start.6
  1.3 0.1 edges.1
  1.4 5.6 %collective-permute-start = (f32[20,2048]{1,0:T(8,128)S(1)}, f32[20,2048]{1,0:T(8,128)S(1)}, u32[]{:S(2)}, u32[]{:S(2)}) collective-permute-start(f32[20,2048]{1,0:T(8,128)S(1)} %get-tuple-element.18), channel_id=1, source_target_pairs={{0,1},{1,2},{2,3},{3,4},{4,5},{5,6},{6,7},{7,8},{8,9},{9,10},{10,1... | collective-permute-start | bytes 491528 | tf_op jit(solution)/shard_map/ppermute | solution.py:334
  7.1 1.3 %collective-permute-start.1 = (f32[20,2048]{1,0:T(8,128)S(1)}, f32[20,2048]{1,0:T(8,128)S(1)}, u32[]{:S(2)}, u32[]{:S(2)}) collective-permute-start(f32[20,2048]{1,0:T(8,128)S(1)} %get-tuple-element.19), channel_id=1, source_target_pairs={{1,0},{2,1},{3,2},{4,3},{5,4},{6,5},{7,6},{8,7},{9,8},{10,9},{11,1... | collective-permute-start | bytes 491528 | tf_op jit(solution)/shard_map/ppermute | solution.py:335
  8.4 0.0 copy-done.1
  8.4 0.0 copy-done.2
  8.4 0.0 copy-done.3
  8.4 0.0 copy-done.4
  8.4 0.0 copy-done.5
  8.5 0.0 copy-done.6
  8.5 2.8 %step.1 = (f32[2560,128]{1,0:T(8,128)S(1)}, f32[128,128]{1,0:T(8,128)S(1)}, s32[8,16]{1,0:T(8,128)S(1)}) custom-call(s32[1]{0:T(128)} %bitcast.2.region_ref, s32[4,16]{1,0:T(4,128)S(1)} %copy-done.3, s32[4,128]{1,0:T(4,128)S(1)} %copy-done.4, f32[20,8,2048]{2,1,0:T(8,128)S(1)} %copy-done.1, f32[8,2048]{1,0:T(8,128)S(1)} %copy-done.2, s32[4,16]{1,0:T(4,128)S(1)} %copy-done.3, ...), custom_call_target="tpu_custom_call" | custom-call | flops 20000000 | bytes 10000000 | tf_op jit(solution)/shard_map/step/pallas_call | solution.py:336
  11.3 0.1 pad_add_fusion.place_ref
  11.4 0.0 collective-permute-done.above_ref
  11.4 3.6 %collective-permute-done.1.below_ref = f32[20,2048]{1,0:T(8,128)S(1)} collective-permute-done((f32[20,2048]{1,0:T(8,128)S(1)}, f32[20,2048]{1,0:T(8,128)S(1)}, u32[]{:S(2)}, u32[]{:S(2)}) %collective-permute-start.1) | collective-permute-done | bytes 163872 | tf_op jit(solution)/shard_map/ppermute | solution.py:335
  15.0 0.9 %parcel.1.own_ref = f32[16,128]{1,0:T(8,128)S(1)} custom-call(s32[8,16]{1,0:T(8,128)S(1)} %get-tuple-element.16.spot_ref, f32[128,128]{1,0:T(8,128)S(1)} %get-tuple-element.17.board_ref, f32[20,2048]{1,0:T(8,128)S(1)} %collective-permute-done.above_ref, f32[20,2048]{1,0:T(8,128)S(1)} %collective-permute-done.1.below_ref, f32[8,2048]{1,0:T(8,128)S(1)} %copy-done.2), custom_call_target="tpu_custom_call" | custom-call | tf_op jit(solution)/shard_map/parcel/pallas_call | solution.py:349
  15.9 0.7 collective-permute-start.2
  16.6 0.8 %finish.1 = (f32[640,128]{1,0:T(8,128)S(1)}, f32[640,128]{1,0:T(8,128)S(1)}, f32[1280,128]{1,0:T(8,128)S(1)}) custom-call(s32[4]{0:T(128)S(1)} %pad_add_fusion.place_ref, f32[2560,128]{1,0:T(8,128)S(1)} %get-tuple-element.22.partial_ref, f32[20,2048]{1,0:T(8,128)S(1)} %collective-permute-done.above_ref, f32[20,2048]{1,0:T(8,128)S(1)} %collective-permute-done.1.below_ref, ...), custom_call_target="tpu_custom_call" | custom-call | flops 10000000000 | bytes 4000000 | tf_op jit(solution)/shard_map/finish/pallas_call | solution.py:368
  17.4 3.2 %collective-permute-start.4 = (f32[1280,128]{1,0:T(8,128)S(1)}, f32[1280,128]{1,0:T(8,128)S(1)}, u32[]{:S(2)}, u32[]{:S(2)}) collective-permute-start(f32[1280,128]{1,0:T(8,128)S(1)} %get-tuple-element.26), channel_id=1, source_target_pairs={{0,256},{128,384},{256,0},{384,128},{1,257},{129,385},{257,1},{385... | collective-permute-start | bytes 1966088 | tf_op jit(solution)/shard_map/ppermute | solution.py:377
  20.5 0.0 collective-permute-done.2.other_ref
  20.6 20.5 %all_to_all.10.plane_ref = f32[8,32,128]{2,1,0:T(8,128)S(1)} all-to-all(f32[8,32,128]{2,1,0:T(8,128)S(1)} %repeat.1), channel_id=1, replica_groups={{0,2,4,6,8,10,12,14},{1,3,5,7,9,11,13,15},{16,18,20,22,24,26,28,30},{17..., dimensions={0} | all-to-all | bytes 262144 | tf_op jit(solution)/shard_map/all_to_all | solution.py:389
  41.0 1.4 %pack.1 = f32[8,96,128]{2,1,0:T(8,128)} custom-call(s32[4]{0:T(128)S(1)} %pad_add_fusion.place_ref, f32[8,32,128]{2,1,0:T(8,128)S(1)} %all_to_all.10.plane_ref), custom_call_target="tpu_custom_call" | custom-call | flops 1000000 | bytes 2000000 | tf_op jit(solution)/shard_map/pack/pallas_call | solution.py:392
  42.4 8.8 %all-to-all-start.1 = ((f32[8,96,128]{2,1,0:T(8,128)}), f32[8,96,128]{2,1,0:T(8,128)S(1)}, u32[]{:S(2)}, u32[]{:S(2)}) async-start(f32[8,96,128]{2,1,0:T(8,128)} %pack.1), calls=%async_computation.1 | async-start | bytes 786432 | tf_op jit(solution)/shard_map/all_to_all | solution.py:402
  51.2 1.9 %collective-permute-start.3 = (f32[640,128]{1,0:T(8,128)S(1)}, f32[640,128]{1,0:T(8,128)S(1)}, u32[]{:S(2)}, u32[]{:S(2)}) collective-permute-start(f32[640,128]{1,0:T(8,128)S(1)} %get-tuple-element.25), channel_id=1, source_target_pairs={{0,128},{128,0},{256,384},{384,256},{1,129},{129,1},{257,385},{385... | collective-permute-start | bytes 983048 | tf_op jit(solution)/shard_map/ppermute | solution.py:391
  53.1 0.0 collective-permute-done.4.state2_ref
  53.1 2.4 %collective-permute-start.5 = (f32[640,128]{1,0:T(8,128)S(1)}, f32[640,128]{1,0:T(8,128)S(1)}, u32[]{:S(2)}, u32[]{:S(2)}) collective-permute-start(f32[640,128]{1,0:T(8,128)S(1)} %slice.4), channel_id=1, source_target_pairs={{0,128},{128,0},{256,384},{384,256},{1,129},{129,1},{257,385},{385... | collective-permute-start | bytes 983048 | tf_op jit(solution)/shard_map/ppermute | solution.py:391
  55.6 0.0 collective-permute-done.3.state1_ref
  55.6 3.7 %all-to-all-done.1.parcels_ref = f32[8,96,128]{2,1,0:T(8,128)S(1)} async-done(((f32[8,96,128]{2,1,0:T(8,128)}), f32[8,96,128]{2,1,0:T(8,128)S(1)}, u32[]{:S(2)}, u32[]{:S(2)}) %all-to-all-start.1) | async-done | bytes 393248 | tf_op jit(solution)/shard_map/all_to_all | solution.py:402
  59.3 0.0 collective-permute-done.5.state3_ref
  59.3 9.3 %update.1 = f32[80,8,512]{2,1,0:T(8,128)} custom-call(s32[4]{0:T(128)S(1)} %pad_add_fusion.place_ref, f32[8,96,128]{2,1,0:T(8,128)S(1)} %all-to-all-done.1.parcels_ref, f32[640,128]{1,0:T(8,128)S(1)} %get-tuple-element.23.state0_ref, f32[640,128]{1,0:T(8,128)S(1)} %collective-permute-done.3.state1_ref, f32[1280,128]{1,0:T(8,128)S(1)} %collective-permute-done.4.state2_ref, ...), custom_call_target="tpu_custom_call" | custom-call | tf_op jit(solution)/shard_map/update/pallas_call | solution.py:405
  (6 shorter events, 0.0 us)
Async XLA Ops:
  0.0 1.3 %copy-start = (f32[20,8,2048]{2,1,0:T(8,128)S(1)}, f32[20,8,2048]{2,1,0:T(8,128)}, u32[]{:S(2)}) copy-start(f32[20,8,2048]{2,1,0:T(8,128)} %tracer_ref.3) | copy-start | bytes 3932164
  1.3 7.1 %copy-start.1 = (f32[20,8,2048]{2,1,0:T(8,128)S(1)}, f32[20,8,2048]{2,1,0:T(8,128)}, u32[]{:S(2)}) copy-start(f32[20,8,2048]{2,1,0:T(8,128)} %tracer_ref.3) | copy-start | bytes 3932164
  1.3 7.1 %copy-start.2 = (f32[8,2048]{1,0:T(8,128)S(1)}, f32[8,2048]{1,0:T(8,128)}, u32[]{:S(2)}) copy-start(f32[8,2048]{1,0:T(8,128)} %diffusion_ref.5) | copy-start | bytes 196612
  1.3 7.1 %copy-start.3 = (s32[4,16]{1,0:T(4,128)S(1)}, s32[4,16]{1,0:T(4,128)}, u32[]{:S(2)}) copy-start(s32[4,16]{1,0:T(4,128)} %site_vec_ref.1) | copy-start | bytes 772
  1.3 7.1 %copy-start.4 = (s32[4,128]{1,0:T(4,128)S(1)}, s32[4,128]{1,0:T(4,128)}, u32[]{:S(2)}) copy-start(s32[4,128]{1,0:T(4,128)} %tally_ref.1) | copy-start | bytes 6148
  1.3 7.1 %copy-start.5 = (f32[4,16]{1,0:T(4,128)S(1)}, f32[4,16]{1,0:T(4,128)}, u32[]{:S(2)}) copy-start(f32[4,16]{1,0:T(4,128)} %reading_ref.1) | copy-start | bytes 772
  1.3 7.1 %copy-start.6 = (f32[4,16]{1,0:T(4,128)S(1)}, f32[4,16]{1,0:T(4,128)}, u32[]{:S(2)}) copy-start(f32[4,16]{1,0:T(4,128)} %variance_ref.1) | copy-start | bytes 772
  1.4 9.9 %collective-permute-start = (f32[20,2048]{1,0:T(8,128)S(1)}, f32[20,2048]{1,0:T(8,128)S(1)}, u32[]{:S(2)}, u32[]{:S(2)}) collective-permute-start(f32[20,2048]{1,0:T(8,128)S(1)} %get-tuple-element.18), channel_id=1, source_target_pairs={{0,1},{1,2},{2,3},{3,4},{4,5},{5,6},{6,7},{7,8},{8,9},{9,10},{10,1... | collective-permute-start | bytes 491528 | tf_op jit(solution)/shard_map/ppermute | solution.py:334
  7.1 7.9 %collective-permute-start.1 = (f32[20,2048]{1,0:T(8,128)S(1)}, f32[20,2048]{1,0:T(8,128)S(1)}, u32[]{:S(2)}, u32[]{:S(2)}) collective-permute-start(f32[20,2048]{1,0:T(8,128)S(1)} %get-tuple-element.19), channel_id=1, source_target_pairs={{1,0},{2,1},{3,2},{4,3},{5,4},{6,5},{7,6},{8,7},{9,8},{10,9},{11,1... | collective-permute-start | bytes 491528 | tf_op jit(solution)/shard_map/ppermute | solution.py:335
  15.9 4.6 %collective-permute-start.2 = (f32[16,128]{1,0:T(8,128)S(1)}, f32[16,128]{1,0:T(8,128)S(1)}, u32[]{:S(2)}, u32[]{:S(2)}) collective-permute-start(f32[16,128]{1,0:T(8,128)S(1)} %parcel.1.own_ref), channel_id=1, source_target_pairs={{8,22},{9,23},{10,20},{11,21},{12,18},{13,19},{14,16},{15,17},{16,... | collective-permute-start | bytes 24584 | tf_op jit(solution)/shard_map/ppermute | solution.py:366
  17.4 35.7 %collective-permute-start.4 = (f32[1280,128]{1,0:T(8,128)S(1)}, f32[1280,128]{1,0:T(8,128)S(1)}, u32[]{:S(2)}, u32[]{:S(2)}) collective-permute-start(f32[1280,128]{1,0:T(8,128)S(1)} %get-tuple-element.26), channel_id=1, source_target_pairs={{0,256},{128,384},{256,0},{384,128},{1,257},{129,385},{257,1},{385... | collective-permute-start | bytes 1966088 | tf_op jit(solution)/shard_map/ppermute | solution.py:377
  42.4 16.9 %all-to-all-start.1 = ((f32[8,96,128]{2,1,0:T(8,128)}), f32[8,96,128]{2,1,0:T(8,128)S(1)}, u32[]{:S(2)}, u32[]{:S(2)}) async-start(f32[8,96,128]{2,1,0:T(8,128)} %pack.1), calls=%async_computation.1 | async-start | bytes 786432 | tf_op jit(solution)/shard_map/all_to_all | solution.py:402
  51.2 4.4 %collective-permute-start.3 = (f32[640,128]{1,0:T(8,128)S(1)}, f32[640,128]{1,0:T(8,128)S(1)}, u32[]{:S(2)}, u32[]{:S(2)}) collective-permute-start(f32[640,128]{1,0:T(8,128)S(1)} %get-tuple-element.25), channel_id=1, source_target_pairs={{0,128},{128,0},{256,384},{384,256},{1,129},{129,1},{257,385},{385... | collective-permute-start | bytes 983048 | tf_op jit(solution)/shard_map/ppermute | solution.py:391
  53.1 6.1 %collective-permute-start.5 = (f32[640,128]{1,0:T(8,128)S(1)}, f32[640,128]{1,0:T(8,128)S(1)}, u32[]{:S(2)}, u32[]{:S(2)}) collective-permute-start(f32[640,128]{1,0:T(8,128)S(1)} %slice.4), channel_id=1, source_target_pairs={{0,128},{128,0},{256,384},{384,256},{1,129},{129,1},{257,385},{385... | collective-permute-start | bytes 983048 | tf_op jit(solution)/shard_map/ppermute | solution.py:391

commit v6 on v5

--- a/solution.py
+++ b/solution.py
@@ -150,7 +150,7 @@
                 out_ref[base + at : base + at + rows, :] = part
 
 
-def pack_kernel(place_ref, plane_ref, out_ref):
+def pack_kernel(place_ref, plane_ref, out_ref, packed, sems):
     count = plane_ref.shape[0]
     slots = plane_ref.shape[1] // 2
     y = place_ref[3]
@@ -166,9 +166,13 @@
     groups.append(jnp.where(lane < 96, parcel(-2), pltpu.roll(parcel(-4), 96, 1)))
     groups.append(jnp.where(lane < 96, parcel(2), pltpu.roll(parcel(4), 96, 1)))
     groups.append(jnp.where(lane < 64, parcel(-3), pltpu.roll(parcel(3), 64, 1)))
-    for i in range(out_ref.shape[0]):
-        for g, group in enumerate(groups):
-            out_ref[i, g * slots : (g + 1) * slots, :] = group
+    for g, group in enumerate(groups):
+        packed[g * slots : (g + 1) * slots, :] = group
+    copies = [pltpu.make_async_copy(packed, out_ref.at[i], sems.at[i]) for i in range(out_ref.shape[0])]
+    for copy in copies:
+        copy.start()
+    for copy in copies:
+        copy.wait()
 
 
 def packed_at(offset, batch):
@@ -393,7 +397,8 @@
         pack_kernel,
         out_shape=jax.ShapeDtypeStruct((2 * QUARTERS, 6 * slots, LANES), f32),
         in_specs=[smem, vmem],
-        out_specs=vmem,
+        out_specs=pl.BlockSpec(memory_space=pl.ANY),
+        scratch_shapes=[pltpu.VMEM((6 * slots, LANES), f32), pltpu.SemaphoreType.DMA((2 * QUARTERS,))],
         compiler_params=limit,
         cost_estimate=pl.CostEstimate(flops=1_000_000, bytes_accessed=2_000_000, transcendentals=0),
         name="pack",

time: 69.6 us -> 69.6 us (level)
  no operation moved by 1% of the time
where the time goes in v6:
time: 69.6 us; the launch traced here: 68.6 us
  starting transfers between devices  23.8 us (34%)
  blocking collectives  20.5 us (29%)
  Pallas kernels  15.3 us (22%)
  waiting for transfers between devices  7.34 us (11%)
  local copies, waits for them, and re-layouts  1.36 us (2%)
    all_to_all x1, blocking collectives, local(): plane = lax.all_to_all(repeated, 'region', 0, 0, axis_index_groups=rings)  20.5 us
    pallas_call x1, Pallas kernels, local(): pl.pallas_call(functools.partial(update_kernel, width=width), out_shape=j...  9.32 us
    all_to_all x1, starting transfers between devices, local(): lax.all_to_all(packed, ('region', 'member'), 0, 0, axis_index_groups=lines)  8.79 us
    ppermute x1, starting transfers between devices, local(): lax.ppermute(bottom, 'region', [(i, i + 1) for i in range(regions - 1)])  5.62 us
    all_to_all x1, waiting for transfers between devices, local(): lax.all_to_all(packed, ('region', 'member'), 0, 0, axis_index_groups=lines)  3.69 us
    ppermute x1, waiting for transfers between devices, local(): lax.ppermute(top, 'region', [(i + 1, i) for i in range(regions - 1)])  3.63 us
    ppermute x1, starting transfers between devices, local(): lax.ppermute(cross, 'member', [(m, m ^ 2) for m in range(QUARTERS)])  3.15 us
    pallas_call x1, Pallas kernels, local(): pl.pallas_call(step_kernel, out_shape=(jax.ShapeDtypeStruct((own * rows *...  2.8 us
  transfers between devices with their start and end apart: 7, of which 2 were waited for; matrix products, arithmetic and copies ran while one was open for 0% of the time, Pallas kernels for 7%

profile of v6, /device:TPU:1, one launch (start us, length us, event | category | flops | bytes accessed | tf_op | source)
XLA Modules:
  0.0 68.6 jit_solution(3264161101554457194)
XLA Ops:
  0.0 0.0 copy-start
  0.0 1.3 %copy-done = f32[20,8,2048]{2,1,0:T(8,128)S(1)} copy-done((f32[20,8,2048]{2,1,0:T(8,128)S(1)}, f32[20,8,2048]{2,1,0:T(8,128)}, u32[]{:S(2)}) %copy-start) | copy-done | bytes 1310744
  1.3 0.0 copy-start.5
  1.3 0.0 copy-start.6
  1.3 0.1 edges.1
  1.4 5.6 %collective-permute-start = (f32[20,2048]{1,0:T(8,128)S(1)}, f32[20,2048]{1,0:T(8,128)S(1)}, u32[]{:S(2)}, u32[]{:S(2)}) collective-permute-start(f32[20,2048]{1,0:T(8,128)S(1)} %get-tuple-element.18), channel_id=1, source_target_pairs={{0,1},{1,2},{2,3},{3,4},{4,5},{5,6},{6,7},{7,8},{8,9},{9,10},{10,1... | collective-permute-start | bytes 491528 | tf_op jit(solution)/shard_map/ppermute | solution.py:338
  7.1 1.3 %collective-permute-start.1 = (f32[20,2048]{1,0:T(8,128)S(1)}, f32[20,2048]{1,0:T(8,128)S(1)}, u32[]{:S(2)}, u32[]{:S(2)}) collective-permute-start(f32[20,2048]{1,0:T(8,128)S(1)} %get-tuple-element.19), channel_id=1, source_target_pairs={{1,0},{2,1},{3,2},{4,3},{5,4},{6,5},{7,6},{8,7},{9,8},{10,9},{11,1... | collective-permute-start | bytes 491528 | tf_op jit(solution)/shard_map/ppermute | solution.py:339
  8.4 0.0 copy-done.1
  8.4 0.0 copy-done.2
  8.4 0.0 copy-done.3
  8.4 0.0 copy-done.4
  8.4 0.0 copy-done.5
  8.5 0.0 copy-done.6
  8.5 2.8 %step.1 = (f32[2560,128]{1,0:T(8,128)S(1)}, f32[128,128]{1,0:T(8,128)S(1)}, s32[8,16]{1,0:T(8,128)S(1)}) custom-call(s32[1]{0:T(128)} %bitcast.2.region_ref, s32[4,16]{1,0:T(4,128)S(1)} %copy-done.3, s32[4,128]{1,0:T(4,128)S(1)} %copy-done.4, f32[20,8,2048]{2,1,0:T(8,128)S(1)} %copy-done.1, f32[8,2048]{1,0:T(8,128)S(1)} %copy-done.2, s32[4,16]{1,0:T(4,128)S(1)} %copy-done.3, ...), custom_call_target="tpu_custom_call" | custom-call | flops 20000000 | bytes 10000000 | tf_op jit(solution)/shard_map/step/pallas_call | solution.py:340
  11.3 0.1 pad_add_fusion.place_ref
  11.4 0.0 collective-permute-done.above_ref
  11.4 3.6 %collective-permute-done.1.below_ref = f32[20,2048]{1,0:T(8,128)S(1)} collective-permute-done((f32[20,2048]{1,0:T(8,128)S(1)}, f32[20,2048]{1,0:T(8,128)S(1)}, u32[]{:S(2)}, u32[]{:S(2)}) %collective-permute-start.1) | collective-permute-done | bytes 163872 | tf_op jit(solution)/shard_map/ppermute | solution.py:339
  15.0 0.9 %parcel.1.own_ref = f32[16,128]{1,0:T(8,128)S(1)} custom-call(s32[8,16]{1,0:T(8,128)S(1)} %get-tuple-element.16.spot_ref, f32[128,128]{1,0:T(8,128)S(1)} %get-tuple-element.17.board_ref, f32[20,2048]{1,0:T(8,128)S(1)} %collective-permute-done.above_ref, f32[20,2048]{1,0:T(8,128)S(1)} %collective-permute-done.1.below_ref, f32[8,2048]{1,0:T(8,128)S(1)} %copy-done.2), custom_call_target="tpu_custom_call" | custom-call | tf_op jit(solution)/shard_map/parcel/pallas_call | solution.py:353
  15.9 0.7 collective-permute-start.2
  16.6 0.8 %finish.1 = (f32[640,128]{1,0:T(8,128)S(1)}, f32[640,128]{1,0:T(8,128)S(1)}, f32[1280,128]{1,0:T(8,128)S(1)}) custom-call(s32[4]{0:T(128)S(1)} %pad_add_fusion.place_ref, f32[2560,128]{1,0:T(8,128)S(1)} %get-tuple-element.22.partial_ref, f32[20,2048]{1,0:T(8,128)S(1)} %collective-permute-done.above_ref, f32[20,2048]{1,0:T(8,128)S(1)} %collective-permute-done.1.below_ref, ...), custom_call_target="tpu_custom_call" | custom-call | flops 10000000000 | bytes 4000000 | tf_op jit(solution)/shard_map/finish/pallas_call | solution.py:372
  17.4 3.2 %collective-permute-start.4 = (f32[1280,128]{1,0:T(8,128)S(1)}, f32[1280,128]{1,0:T(8,128)S(1)}, u32[]{:S(2)}, u32[]{:S(2)}) collective-permute-start(f32[1280,128]{1,0:T(8,128)S(1)} %get-tuple-element.26), channel_id=1, source_target_pairs={{0,256},{128,384},{256,0},{384,128},{1,257},{129,385},{257,1},{385... | collective-permute-start | bytes 1966088 | tf_op jit(solution)/shard_map/ppermute | solution.py:381
  20.5 0.0 collective-permute-done.2.other_ref
  20.6 20.5 %all_to_all.10.plane_ref = f32[8,32,128]{2,1,0:T(8,128)S(1)} all-to-all(f32[8,32,128]{2,1,0:T(8,128)S(1)} %repeat.1), channel_id=1, replica_groups={{0,2,4,6,8,10,12,14},{1,3,5,7,9,11,13,15},{16,18,20,22,24,26,28,30},{17..., dimensions={0} | all-to-all | bytes 262144 | tf_op jit(solution)/shard_map/all_to_all | solution.py:393
  41.0 1.4 %pack.1 = f32[8,96,128]{2,1,0:T(8,128)} custom-call(s32[4]{0:T(128)S(1)} %pad_add_fusion.place_ref, f32[8,32,128]{2,1,0:T(8,128)S(1)} %all_to_all.10.plane_ref), custom_call_target="tpu_custom_call" | custom-call | flops 1000000 | bytes 2000000 | tf_op jit(solution)/shard_map/pack/pallas_call | solution.py:396
  42.4 8.8 %all-to-all-start.1 = ((f32[8,96,128]{2,1,0:T(8,128)}), f32[8,96,128]{2,1,0:T(8,128)S(1)}, u32[]{:S(2)}, u32[]{:S(2)}) async-start(f32[8,96,128]{2,1,0:T(8,128)} %pack.1), calls=%async_computation.1 | async-start | bytes 786432 | tf_op jit(solution)/shard_map/all_to_all | solution.py:407
  51.2 1.9 %collective-permute-start.3 = (f32[640,128]{1,0:T(8,128)S(1)}, f32[640,128]{1,0:T(8,128)S(1)}, u32[]{:S(2)}, u32[]{:S(2)}) collective-permute-start(f32[640,128]{1,0:T(8,128)S(1)} %get-tuple-element.25), channel_id=1, source_target_pairs={{0,128},{128,0},{256,384},{384,256},{1,129},{129,1},{257,385},{385... | collective-permute-start | bytes 983048 | tf_op jit(solution)/shard_map/ppermute | solution.py:395
  53.2 0.0 collective-permute-done.4.state2_ref
  53.2 2.4 %collective-permute-start.5 = (f32[640,128]{1,0:T(8,128)S(1)}, f32[640,128]{1,0:T(8,128)S(1)}, u32[]{:S(2)}, u32[]{:S(2)}) collective-permute-start(f32[640,128]{1,0:T(8,128)S(1)} %slice.4), channel_id=1, source_target_pairs={{0,128},{128,0},{256,384},{384,256},{1,129},{129,1},{257,385},{385... | collective-permute-start | bytes 983048 | tf_op jit(solution)/shard_map/ppermute | solution.py:395
  55.6 0.0 collective-permute-done.3.state1_ref
  55.6 3.7 %all-to-all-done.1.parcels_ref = f32[8,96,128]{2,1,0:T(8,128)S(1)} async-done(((f32[8,96,128]{2,1,0:T(8,128)}), f32[8,96,128]{2,1,0:T(8,128)S(1)}, u32[]{:S(2)}, u32[]{:S(2)}) %all-to-all-start.1) | async-done | bytes 393248 | tf_op jit(solution)/shard_map/all_to_all | solution.py:407
  59.3 0.0 collective-permute-done.5.state3_ref
  59.3 9.3 %update.1 = f32[80,8,512]{2,1,0:T(8,128)} custom-call(s32[4]{0:T(128)S(1)} %pad_add_fusion.place_ref, f32[8,96,128]{2,1,0:T(8,128)S(1)} %all-to-all-done.1.parcels_ref, f32[640,128]{1,0:T(8,128)S(1)} %get-tuple-element.23.state0_ref, f32[640,128]{1,0:T(8,128)S(1)} %collective-permute-done.3.state1_ref, f32[1280,128]{1,0:T(8,128)S(1)} %collective-permute-done.4.state2_ref, ...), custom_call_target="tpu_custom_call" | custom-call | tf_op jit(solution)/shard_map/update/pallas_call | solution.py:410
  (6 shorter events, 0.0 us)
Async XLA Ops:
  0.0 1.3 %copy-start = (f32[20,8,2048]{2,1,0:T(8,128)S(1)}, f32[20,8,2048]{2,1,0:T(8,128)}, u32[]{:S(2)}) copy-start(f32[20,8,2048]{2,1,0:T(8,128)} %tracer_ref.3) | copy-start | bytes 3932164
  1.3 7.1 %copy-start.1 = (f32[20,8,2048]{2,1,0:T(8,128)S(1)}, f32[20,8,2048]{2,1,0:T(8,128)}, u32[]{:S(2)}) copy-start(f32[20,8,2048]{2,1,0:T(8,128)} %tracer_ref.3) | copy-start | bytes 3932164
  1.3 7.1 %copy-start.2 = (f32[8,2048]{1,0:T(8,128)S(1)}, f32[8,2048]{1,0:T(8,128)}, u32[]{:S(2)}) copy-start(f32[8,2048]{1,0:T(8,128)} %diffusion_ref.5) | copy-start | bytes 196612
  1.3 7.1 %copy-start.3 = (s32[4,16]{1,0:T(4,128)S(1)}, s32[4,16]{1,0:T(4,128)}, u32[]{:S(2)}) copy-start(s32[4,16]{1,0:T(4,128)} %site_vec_ref.1) | copy-start | bytes 772
  1.3 7.1 %copy-start.4 = (s32[4,128]{1,0:T(4,128)S(1)}, s32[4,128]{1,0:T(4,128)}, u32[]{:S(2)}) copy-start(s32[4,128]{1,0:T(4,128)} %tally_ref.1) | copy-start | bytes 6148
  1.3 7.1 %copy-start.5 = (f32[4,16]{1,0:T(4,128)S(1)}, f32[4,16]{1,0:T(4,128)}, u32[]{:S(2)}) copy-start(f32[4,16]{1,0:T(4,128)} %reading_ref.1) | copy-start | bytes 772
  1.3 7.1 %copy-start.6 = (f32[4,16]{1,0:T(4,128)S(1)}, f32[4,16]{1,0:T(4,128)}, u32[]{:S(2)}) copy-start(f32[4,16]{1,0:T(4,128)} %variance_ref.1) | copy-start | bytes 772
  1.4 9.9 %collective-permute-start = (f32[20,2048]{1,0:T(8,128)S(1)}, f32[20,2048]{1,0:T(8,128)S(1)}, u32[]{:S(2)}, u32[]{:S(2)}) collective-permute-start(f32[20,2048]{1,0:T(8,128)S(1)} %get-tuple-element.18), channel_id=1, source_target_pairs={{0,1},{1,2},{2,3},{3,4},{4,5},{5,6},{6,7},{7,8},{8,9},{9,10},{10,1... | collective-permute-start | bytes 491528 | tf_op jit(solution)/shard_map/ppermute | solution.py:338
  7.1 7.9 %collective-permute-start.1 = (f32[20,2048]{1,0:T(8,128)S(1)}, f32[20,2048]{1,0:T(8,128)S(1)}, u32[]{:S(2)}, u32[]{:S(2)}) collective-permute-start(f32[20,2048]{1,0:T(8,128)S(1)} %get-tuple-element.19), channel_id=1, source_target_pairs={{1,0},{2,1},{3,2},{4,3},{5,4},{6,5},{7,6},{8,7},{9,8},{10,9},{11,1... | collective-permute-start | bytes 491528 | tf_op jit(solution)/shard_map/ppermute | solution.py:339
  15.9 4.6 %collective-permute-start.2 = (f32[16,128]{1,0:T(8,128)S(1)}, f32[16,128]{1,0:T(8,128)S(1)}, u32[]{:S(2)}, u32[]{:S(2)}) collective-permute-start(f32[16,128]{1,0:T(8,128)S(1)} %parcel.1.own_ref), channel_id=1, source_target_pairs={{8,22},{9,23},{10,20},{11,21},{12,18},{13,19},{14,16},{15,17},{16,... | collective-permute-start | bytes 24584 | tf_op jit(solution)/shard_map/ppermute | solution.py:370
  17.4 35.8 %collective-permute-start.4 = (f32[1280,128]{1,0:T(8,128)S(1)}, f32[1280,128]{1,0:T(8,128)S(1)}, u32[]{:S(2)}, u32[]{:S(2)}) collective-permute-start(f32[1280,128]{1,0:T(8,128)S(1)} %get-tuple-element.26), channel_id=1, source_target_pairs={{0,256},{128,384},{256,0},{384,128},{1,257},{129,385},{257,1},{385... | collective-permute-start | bytes 1966088 | tf_op jit(solution)/shard_map/ppermute | solution.py:381
  42.4 16.9 %all-to-all-start.1 = ((f32[8,96,128]{2,1,0:T(8,128)}), f32[8,96,128]{2,1,0:T(8,128)S(1)}, u32[]{:S(2)}, u32[]{:S(2)}) async-start(f32[8,96,128]{2,1,0:T(8,128)} %pack.1), calls=%async_computation.1 | async-start | bytes 786432 | tf_op jit(solution)/shard_map/all_to_all | solution.py:407
  51.2 4.4 %collective-permute-start.3 = (f32[640,128]{1,0:T(8,128)S(1)}, f32[640,128]{1,0:T(8,128)S(1)}, u32[]{:S(2)}, u32[]{:S(2)}) collective-permute-start(f32[640,128]{1,0:T(8,128)S(1)} %get-tuple-element.25), channel_id=1, source_target_pairs={{0,128},{128,0},{256,384},{384,256},{1,129},{129,1},{257,385},{385... | collective-permute-start | bytes 983048 | tf_op jit(solution)/shard_map/ppermute | solution.py:395
  53.2 6.1 %collective-permute-start.5 = (f32[640,128]{1,0:T(8,128)S(1)}, f32[640,128]{1,0:T(8,128)S(1)}, u32[]{:S(2)}, u32[]{:S(2)}) collective-permute-start(f32[640,128]{1,0:T(8,128)S(1)} %slice.4), channel_id=1, source_target_pairs={{0,128},{128,0},{256,384},{384,256},{1,129},{129,1},{257,385},{385... | collective-permute-start | bytes 983048 | tf_op jit(solution)/shard_map/ppermute | solution.py:395
